TPU v7x, 128 devices: a whole 4x4x4 slice. The times are simulated.
128 devices in a mesh: dp: 32 (over y, z_hi, x), mp: 4 (over z_lo, core).
Axes of the slice: x: 4, y: 4, z: 4 (z_hi: 2, z_lo: 2; z = z_hi * 2 + z_lo), core: 2. Of those that a mesh axis runs over, the one named last changes fastest.
Arguments:
- tokens: bfloat16 [32768, 1024], P('dp'), may hold values from -6 to 6
- lengths: int32 [32, 8], P('dp'), may hold values from 1 to 768, 1024 in all within a row
- norm_gain_one: float32 [1024], replicated, may hold values from 0.5 to 1.5
- w_query: bfloat16 [1024, 512], P(None, 'mp'), may hold values from -0.1875 to 0.1875
- w_key: bfloat16 [1024, 512], P(None, 'mp'), may hold values from -0.1875 to 0.1875
- w_value: bfloat16 [1024, 1024], P(None, 'mp'), may hold values from -0.1875 to 0.1875
- w_gate_down: bfloat16 [1024, 16], replicated, may hold values from -0.1875 to 0.1875
- w_gate_up: bfloat16 [16, 512], P(None, 'mp'), may hold values from -1.5 to 1.5
- gate_bias: float32 [512], P('mp'), may hold values from -4.5 to 4.5
- w_out: bfloat16 [1024, 1024], P('mp'), may hold values from -0.09375 to 0.09375
- norm_gain_two: float32 [1024], replicated, may hold values from 0.5 to 1.5
- w_mlp_gate: bfloat16 [1024, 2816], P(None, 'mp'), may hold values from -0.1875 to 0.1875
- w_mlp_up: bfloat16 [1024, 2816], P(None, 'mp'), may hold values from -0.1875 to 0.1875
- w_mlp_down: bfloat16 [2816, 1024], P('mp'), may hold values from -0.109375 to 0.109375
- cotangent: bfloat16 [32768, 1024], P('dp'), may hold values from -6 to 6
Outputs:
- result: bfloat16 [32768, 1024], P('dp')
- grad_tokens: float32 [32768, 1024], P('dp')
- grad_gain_one: float32 [1024], replicated
- grad_query: float32 [1024, 512], P('dp', 'mp')
- grad_key: float32 [1024, 512], P('dp', 'mp')
- grad_value: float32 [1024, 1024], P('dp', 'mp')
- grad_gate_down: float32 [1024, 16], replicated
- grad_gate_up: float32 [16, 512], P(None, 'mp')
- grad_gate_bias: float32 [512], P('mp')
- grad_out: float32 [1024, 1024], P('mp', 'dp')
- grad_gain_two: float32 [1024], replicated
- grad_mlp_gate: float32 [1024, 2816], P('dp', 'mp')
- grad_mlp_up: float32 [1024, 2816], P('dp', 'mp')
- grad_mlp_down: float32 [2816, 1024], P('mp', 'dp')
Inputs may be any that keep to these rules, and one draw needn't show every extreme that they name: `lengths`: each row sums to 1024, and its largest length is exactly 768.
All inputs are finite; a program needn't handle non-finite values.
Results may differ from a plain program's by a relative error of at most 0.02.
Values sent between devices are 32-bit elements; how exact they have to be, the bound alone decides.
No kernel may reach another device: no remote copies, remote signals or barrier semaphores. Data moves between devices by JAX's collectives and lax.ppermute only.
A program may use at most 128 MiB of HBM per device.

v0:
```python
import jax
import jax.numpy as jnp
from jax import lax
from jax.sharding import PartitionSpec as P

DK = 128
DV = 256
BLK = 64


gate_normalizer = 16.0
norm_epsilon = 1e-06


def side_by_side(arrays, axis, dim, along):
    widths = [a.shape[along] for a in arrays]
    both = jnp.concatenate(arrays, axis=along)
    out = lax.psum_scatter(both, axis, scatter_dimension=dim, tiled=True)
    return tuple(jnp.split(out, [sum(widths[:k]) for k in range(1, len(widths))], axis=along))


def over_pieces(x, axis):
    return lax.all_gather(x, axis).sum(0)


def exact_dot(left_side, right_side):
    return jnp.dot(left_side, right_side, precision=lax.Precision.HIGHEST)


def fast_dot(left_side, right_side):
    return jnp.dot(left_side, right_side, preferred_element_type=jnp.float32)


def rounded_low(values):
    return lax.optimization_barrier(values.astype(jnp.bfloat16))


def norm_apply(values, gains):
    inverse_rms = lax.rsqrt(jnp.mean(values * values, axis=-1, keepdims=True) + norm_epsilon)
    return values * inverse_rms * gains


def span_step(carry_state, pieces):
    query_rows, key_rows, value_rows, decay_rows, item_ids, before = pieces
    query_wide = query_rows.astype(jnp.float32)
    key_wide = key_rows.astype(jnp.float32)
    cumulative = jnp.cumsum(decay_rows, axis=0)
    block_end = cumulative[-1]
    q_scaled = rounded_low(query_wide * query_rows.shape[-1] ** (-0.5) * jnp.exp(cumulative))
    k_scaled = rounded_low(key_wide * jnp.exp(-cumulative))
    k_final = rounded_low(key_wide * jnp.exp(block_end - cumulative))
    places = jnp.arange(item_ids.shape[0])
    visible = (item_ids[:, None] == item_ids[None, :]) & (places[:, None] >= places[None, :])
    scores = rounded_low(jnp.where(visible, fast_dot(q_scaled, k_scaled.T), 0.0))
    carried = (item_ids == before)[:, None]
    outputs = fast_dot(scores, value_rows) + jnp.where(
        carried, fast_dot(q_scaled, rounded_low(carry_state)), 0.0
    )
    keep_state = jnp.where(item_ids[-1] == before, 1.0, 0.0)
    tail_keys = jnp.where((item_ids == item_ids[-1])[:, None], k_final, jnp.zeros_like(k_final))
    new_state = keep_state * jnp.exp(block_end)[:, None] * carry_state + fast_dot(
        tail_keys.T, value_rows
    )
    return (new_state, outputs)


def gla_head(queries, keysets, valueset, decays, item_ids):
    blocks = item_ids.shape[0] // BLK
    before = jnp.concatenate([jnp.full((1,), -1, dtype=jnp.int32), item_ids[BLK - 1 :: BLK][:-1]])
    start_state = jnp.zeros((keysets.shape[1], valueset.shape[1]), jnp.float32)
    pieces = (
        queries.reshape(blocks, BLK, -1),
        keysets.reshape(blocks, BLK, -1),
        valueset.reshape(blocks, BLK, -1),
        decays.reshape(blocks, BLK, -1),
        item_ids.reshape(blocks, BLK),
        before,
    )
    unused, outputs = lax.scan(jax.checkpoint(span_step), start_state, pieces)
    return outputs.reshape(-1, valueset.shape[1])


def gla_heads(queries, keysets, valueset, decays, item_ids):
    row_count = queries.shape[0]
    heads = queries.shape[1] // DK
    mapped = jax.vmap(gla_head, in_axes=(1, 1, 1, 1, None), out_axes=1)
    mixed_heads = mapped(
        queries.reshape(row_count, heads, DK),
        keysets.reshape(row_count, heads, DK),
        valueset.reshape(row_count, heads, DV),
        decays.reshape(row_count, heads, DK),
        item_ids,
    )
    return mixed_heads.reshape(row_count, heads * DV)


def local(
    tokens,
    lengths,
    norm_gain_one,
    w_query,
    w_key,
    w_value,
    w_gate_down,
    w_gate_up,
    gate_bias,
    w_out,
    norm_gain_two,
    w_mlp_gate,
    w_mlp_up,
    w_mlp_down,
    cotangent,
):
    row_count = tokens.shape[0]
    places = jnp.arange(row_count, dtype=jnp.int32)
    sizes_here = lengths[0]
    starts = jnp.cumsum(sizes_here) - sizes_here
    item_ids = jnp.sum((places[:, None] >= starts[None, :]).astype(jnp.int32), axis=1) - 1
    inputs = tokens.astype(jnp.float32)
    normed_one, norm_one_back = jax.vjp(norm_apply, inputs, norm_gain_one)
    low_one = normed_one.astype(jnp.bfloat16)
    queries = fast_dot(low_one, w_query).astype(jnp.bfloat16)
    keysets = fast_dot(low_one, w_key).astype(jnp.bfloat16)
    valueset = fast_dot(low_one, w_value).astype(jnp.bfloat16)
    low_rank = fast_dot(low_one, w_gate_down).astype(jnp.bfloat16)
    gate_up_wide = w_gate_up.astype(jnp.float32)
    logits = exact_dot(low_rank.astype(jnp.float32), gate_up_wide) + gate_bias
    decays = jax.nn.log_sigmoid(logits) / gate_normalizer

    def local_mixer(query_part, key_part, value_part, decay_part):
        return gla_heads(query_part, key_part, value_part, decay_part, item_ids)

    mixed_heads, mixer_back = jax.vjp(local_mixer, queries, keysets, valueset, decays)
    mixed_low = mixed_heads.astype(jnp.bfloat16)
    attention = lax.psum(fast_dot(mixed_low, w_out), "mp")
    middle = inputs + attention
    normed_two, norm_two_back = jax.vjp(norm_apply, middle, norm_gain_two)
    low_two = normed_two.astype(jnp.bfloat16)
    gate_pre = fast_dot(low_two, w_mlp_gate)
    up_pre = fast_dot(low_two, w_mlp_up)
    sigmoid_gate = jax.nn.sigmoid(gate_pre)
    activated = gate_pre * sigmoid_gate
    hidden_low = (activated * up_pre).astype(jnp.bfloat16)
    feed_sum = lax.psum(fast_dot(hidden_low, w_mlp_down), "mp")
    result = (middle + feed_sum).astype(jnp.bfloat16)
    grad_mlp_down = fast_dot(hidden_low.T, cotangent)
    grad_hidden = fast_dot(cotangent, w_mlp_down.T)
    grad_gate_low = (
        grad_hidden * up_pre * sigmoid_gate * (1.0 + gate_pre * (1.0 - sigmoid_gate))
    ).astype(jnp.bfloat16)
    grad_up_low = (grad_hidden * activated).astype(jnp.bfloat16)
    grad_mlp_gate = fast_dot(low_two.T, grad_gate_low)
    grad_mlp_up = fast_dot(low_two.T, grad_up_low)
    mlp_shards = (
        *side_by_side((grad_mlp_gate, grad_mlp_up), "dp", 0, 1),
        lax.psum_scatter(grad_mlp_down, "dp", scatter_dimension=1, tiled=True),
    )
    partial_two = fast_dot(grad_gate_low, w_mlp_gate.T) + fast_dot(grad_up_low, w_mlp_up.T)
    grad_normed_two = lax.psum(partial_two, "mp")
    grad_middle_norm, grad_gain_two_part = norm_two_back(grad_normed_two)
    grad_middle = cotangent.astype(jnp.float32) + grad_middle_norm
    grad_attention = grad_middle.astype(jnp.bfloat16)
    grad_out = fast_dot(mixed_low.T, grad_attention)
    grad_mixed = fast_dot(grad_attention, w_out.T).astype(jnp.bfloat16)
    grad_q_low, grad_k_low, grad_v_low, grad_decays = mixer_back(grad_mixed.astype(jnp.float32))
    grad_logits = grad_decays * jax.nn.sigmoid(-logits) / gate_normalizer
    grad_bias_part = jnp.sum(grad_logits, axis=0)
    grad_gate_up_part = exact_dot(low_rank.astype(jnp.float32).T, grad_logits)
    grad_low_rank = exact_dot(grad_logits, gate_up_wide.T)
    grad_query = fast_dot(low_one.T, grad_q_low)
    grad_key = fast_dot(low_one.T, grad_k_low)
    grad_value = fast_dot(low_one.T, grad_v_low)
    partial_one = (
        fast_dot(grad_q_low, w_query.T)
        + fast_dot(grad_k_low, w_key.T)
        + fast_dot(grad_v_low, w_value.T)
        + exact_dot(grad_low_rank, w_gate_down.astype(jnp.float32).T)
    )
    gate_down_part = exact_dot(low_one.astype(jnp.float32).T, grad_low_rank)
    grad_normed_one, grad_gate_down_group = (
        over_pieces(partial_one, "mp"),
        over_pieces(gate_down_part, "mp"),
    )
    grad_inputs_norm, grad_gain_one_part = norm_one_back(grad_normed_one)
    grad_tokens = grad_middle + grad_inputs_norm
    grad_gain_one, grad_gain_two, grad_gate_down, grad_gate_up, grad_gate_bias = (
        over_pieces(grad_gain_one_part, "dp"),
        over_pieces(grad_gain_two_part, "dp"),
        over_pieces(grad_gate_down_group, "dp"),
        over_pieces(grad_gate_up_part, "dp"),
        over_pieces(grad_bias_part, "dp"),
    )
    attention_shards = (
        *side_by_side((grad_query, grad_key, grad_value), "dp", 0, 1),
        lax.psum_scatter(grad_out, "dp", scatter_dimension=1, tiled=True),
    )
    query_rows, key_rows, value_rows, out_rows = attention_shards
    gate_rows, up_rows, down_rows = mlp_shards
    return (
        result,
        grad_tokens,
        grad_gain_one,
        query_rows,
        key_rows,
        value_rows,
        grad_gate_down,
        grad_gate_up,
        grad_gate_bias,
        out_rows,
        grad_gain_two,
        gate_rows,
        up_rows,
        down_rows,
    )


def solution(mesh):
    placed = (
        P("dp", None),
        P("dp", None),
        P(),
        P(None, "mp"),
        P(None, "mp"),
        P(None, "mp"),
        P(),
        P(None, "mp"),
        P("mp"),
        P("mp", None),
        P(),
        P(None, "mp"),
        P(None, "mp"),
        P("mp", None),
        P("dp", None),
    )
    return jax.shard_map(
        local,
        mesh=mesh,
        in_specs=placed,
        out_specs=(
            P("dp", None),
            P("dp", None),
            P(),
            P("dp", "mp"),
            P("dp", "mp"),
            P("dp", "mp"),
            P(),
            P(None, "mp"),
            P("mp"),
            P("mp", "dp"),
            P(),
            P("dp", "mp"),
            P("dp", "mp"),
            P("mp", "dp"),
        ),
        check_vma=False,
    )
```

profile of v0, /device:TPU:0, one launch (start us, length us, event | category | flops | bytes accessed | tf_op | source)
XLA Modules:
  0.0 1680.0 jit_solution(12077775155636623572)
XLA Ops:
  20.4 280.2 %while.39 = (s32[]{:T(128)}, f32[1,128,256]{2,1,0:T(8,128)}, bf16[16,1,64,256]{3,2,1,0:T(8,128)(2,1)}, f32[16,1,128,256]{3,2,1,0:T(8,128)}, s32[16,64]{1,0:T(8,1...) while((s32[]{:T(128)}, f32[1,128,256]{2,1,0:T(8,128)}, ...), condition=%wide.region_5.6_spmd.clone, body=%wide.region_3.5_spmd.clone.sunk | while | flops 12366085 | bytes 1381899 | solution.py:79
  300.5 3.9 fusion.131
  305.1 93.6 %all-reduce.5.cloned.1.call-done = f32[1024,1024]{1,0:T(8,128)} async-done(((f32[1024,1024]{1,0:T(8,128)}), f32[1024,1024]{1,0:T(8,128)}) %all-reduce.5.cloned.1.call-update) | async-done | bytes 4194320 | tf_op jit(solution)/shard_map/psum | solution.py:135
  413.5 3.9 fusion.134
  417.4 4.0 convolution_add_fusion
  421.7 3.8 fusion.147
  430.7 6.6 copy.76
  437.3 144.5 %all-reduce.7.cloned.1.call-done = (f32[1024,1024]{1,0:T(8,128)}, f32[1024,1024]{1,0:T(8,128)}) async-done(((f32[1024,1024]{1,0:T(8,128)}, f32[1024,1024]{1,0:T(8,128)}), (f32[1024,1024]{1,0:T(8,128)}, f32[1024,1024]{1,0:T(8,128)})) %all-reduce.7.cloned.1.call-update) | async-done | bytes 8388624 | tf_op jit(solution)/shard_map/psum | solution.py:144
  581.9 5.2 multiply_reduce_fusion.1
  587.8 4.6 fusion.108
  596.3 237.0 %while.40 = (s32[]{:T(128)}, f32[1,128,256]{1,2,0:T(8,128)S(1)}, bf16[16,1,64,128]{3,2,1,0:T(8,128)(2,1)}, bf16[16,1,64,128]{3,2,1,0:T(8,128)(2,1)S(1)}, bf16[16...) while((s32[]{:T(128)}, f32[1,128,256]{1,2,0:T(8,128)S(1)}, ...), condition=%wide.region_16.17_spmd.clone, body=%wide.region_11.16_spmd.clone.sunk | while | flops 25956740 | bytes 3083401 | solution.py:79
  837.8 6.3 all-gather.2
  854.6 4.2 add_add_fusion.2
  860.9 3.6 fusion.145
  865.1 95.4 %all-gather.6 = f32[32768]{0:T(1024)S(1)} all-gather(f32[1024]{0:T(1024)S(1)} %copy-done.36), channel_id=8, replica_groups=mesh['dp'=32,'mp'=4] {'dp'}, dimensions={0}, use_global_device_ids=true | all-gather | bytes 135168 | tf_op jit(solution)/shard_map/all_gather | solution.py:23
  961.2 86.9 %all-gather.7 = f32[32,1,128]{2,1,0:T(1,128)S(1)} all-gather(f32[1,1,128]{2,1,0:T(1,128)S(1)} %bitcast.419), channel_id=7, replica_groups=mesh['dp'=32,'mp'=4] {'dp'}, dimensions={0}, use_global_device_ids=true | all-gather | bytes 16896 | tf_op jit(solution)/shard_map/all_gather | solution.py:23
  1049.0 4.1 fusion.113
  1053.1 91.4 %all-gather.4 = f32[512,128]{1,0:T(8,128)S(1)} all-gather(f32[16,128]{1,0:T(8,128)S(1)} %fusion.144), channel_id=6, replica_groups=mesh['dp'=32,'mp'=4] {'dp'}, dimensions={0}, use_global_device_ids=true | all-gather | bytes 270336 | tf_op jit(solution)/shard_map/all_gather | solution.py:23
  1153.2 100.5 %all-gather.11.cloned.1.call-done = f32[4096,1024]{1,0:T(8,128)} async-done(((f32[1024,1024]{1,0:T(8,128)}), f32[4096,1024]{1,0:T(8,128)}) %all-gather.11.cloned.1.call-update) | async-done | bytes 16777232 | tf_op jit(solution)/shard_map/all_gather | solution.py:23
  1253.7 10.4 reduce_sum.159
  1267.7 95.6 %all-gather.1 = f32[32768]{0:T(1024)S(1)} all-gather(f32[1024]{0:T(1024)S(1)} %get-tuple-element.615), channel_id=3, replica_groups=mesh['dp'=32,'mp'=4] {'dp'}, dimensions={0}, use_global_device_ids=true | all-gather | bytes 135168 | tf_op jit(solution)/shard_map/all_gather | solution.py:23
  1363.9 5.5 fusion.109
  1369.4 118.4 %reduce-scatter.11.cloned.1.call-done = f32[704,32]{0,1:T(8,128)} async-done(((f32[704,1024]{0,1:T(8,128)}), f32[704,32]{0,1:T(8,128)}) %reduce-scatter.11.cloned.1.call-update) | async-done | bytes 90128 | tf_op jit(solution)/shard_map/reduce_scatter | solution.py:156
  1487.8 185.2 %reduce-scatter.9.cloned.1.call-done = f32[256,32]{0,1:T(8,128)} async-done(((f32[256,1024]{0,1:T(8,128)}), f32[256,32]{0,1:T(8,128)}) %reduce-scatter.9.cloned.1.call-update) | async-done | bytes 32784 | tf_op jit(solution)/shard_map/reduce_scatter | solution.py:195
  (940 shorter events, 544.5 us)
Async XLA Ops:
  7.2 401.3 %copy-start = (bf16[704,1024]{1,0:T(8,128)(2,1)S(1)}, bf16[704,1024]{1,0:T(8,128)(2,1)}, u32[]{:S(2)}) copy-start(bf16[704,1024]{1,0:T(8,128)(2,1)} %param.32) | copy-start | bytes 4325380
  7.2 391.5 %all-reduce.5.cloned.1.call-start = ((), (), s32[]{:S(2)}) async-start(), calls=%async_computation.4 | async-start | bytes 8388608 | tf_op jit(solution)/shard_map/psum | solution.py:135
  304.5 277.4 %all-reduce.7.cloned.1.call-start = ((), (), s32[]{:S(2)}) async-start(), calls=%async_computation.11 | async-start | bytes 16777216 | tf_op jit(solution)/shard_map/psum | solution.py:144
  411.6 5.8 copy-start.43
  421.4 723.7 %reduce-scatter.15.cloned.1.call-start = ((), (), s32[]{:S(2)}) async-start(), calls=%async_computation.10 | async-start | bytes 5947392
  437.3 144.6 %copy-start.34 = (f32[1024]{0:T(1024)S(1)}, f32[1024]{0:T(1024)}, u32[]{:S(2)}) copy-start(f32[1024]{0:T(1024)} %param.29) | copy-start | bytes 12292
  437.3 709.5 %all-gather.13.cloned.1.call-start = ((), (), s32[]{:S(2)}) async-start(), calls=%async_computation.8 | async-start | bytes 2162688 | tf_op jit(solution)/shard_map/all_gather | solution.py:23
  581.9 5.9 copy-start.7
  627.9 5.2 copy-start.37
  746.4 5.2 copy-start.37
  833.4 14.8 copy-start.13
  833.4 15.3 copy-start.8
  833.4 14.3 copy-start.15
  836.9 11.3 copy-start.26
  847.7 302.8 %reduce-scatter.13.cloned.1.call-start = ((), (), s32[]{:S(2)}) async-start(), calls=%async_computation.9 | async-start | bytes 2162688
  851.6 402.1 %all-gather.11.cloned.1.call-start = ((), (), s32[]{:S(2)}) async-start(), calls=%async_computation.7 | async-start | bytes 20971520 | tf_op jit(solution)/shard_map/all_gather | solution.py:23
  858.9 628.9 %reduce-scatter.11.cloned.1.call-start = ((), (), s32[]{:S(2)}) async-start(), calls=%async_computation.6 | async-start | bytes 3244032 | tf_op jit(solution)/shard_map/reduce_scatter | solution.py:156
  864.5 184.2 %copy-start.11 = (f32[1024,128]{1,0:T(8,128)S(1)}, f32[1024,128]{1,0:T(8,128)}, u32[]{:S(2)}) copy-start(f32[1024,128]{1,0:T(8,128)} %copy-done.10) | copy-start | bytes 1572868
  864.5 184.2 %copy-start.33 = (bf16[1024,16]{0,1:T(8,128)(2,1)S(1)}, bf16[1024,16]{0,1:T(8,128)(2,1)}, u32[]{:S(2)}) copy-start(bf16[1024,16]{0,1:T(8,128)(2,1)} %copy-done.32) | copy-start | bytes 98308
  864.5 184.5 %copy-start.12 = (bf16[16,1,64,256]{3,2,1,0:T(8,128)(2,1)S(1)}, bf16[16,1,64,256]{3,2,1,0:T(8,128)(2,1)}, u32[]{:S(2)}) copy-start(bf16[16,1,64,256]{3,2,1,0:T(8,128)(2,1)} %get-tuple-element.404) | copy-start | bytes 1572868
  864.5 808.4 %reduce-scatter.9.cloned.1.call-start = ((), (), s32[]{:S(2)}) async-start(), calls=%async_computation.5 | async-start | bytes 1081344 | tf_op jit(solution)/shard_map/reduce_scatter | solution.py:195
  1253.7 10.4 copy-start.6
  1253.7 10.4 copy-start.35
  1363.9 309.0 %copy-start.1 = (bf16[704,1024]{1,0:T(8,128)(2,1)S(1)}, bf16[704,1024]{1,0:T(8,128)(2,1)}, u32[]{:S(2)}) copy-start(bf16[704,1024]{1,0:T(8,128)(2,1)} %param.32) | copy-start | bytes 4325380
  (62 other events, 174.7 us)
Sparse Core Ops, SparseCore 0:
  304.6 94.0 all-reduce.4
  421.5 160.3 all-reduce.6
  584.4 197.7 reduce-scatter.14
  847.8 73.4 all-gather.12
  923.7 184.0 reduce-scatter.12
  1109.2 144.3 all-gather.10
  1259.2 228.5 reduce-scatter.10
  1490.8 182.0 reduce-scatter.8
where the time goes:
time: 1700 us; the launch traced here: 1680 us
  waiting for transfers between devices  642 us (38%)
  blocking collectives  375 us (22%)
  other arithmetic  228 us (13%)
  local copies, waits for them, and re-layouts  191 us (11%)
  matrix products  183 us (11%)
  loops' own time  43 us (3%)
    all_gather x5, blocking collectives, over_pieces(): return lax.all_gather(x, axis).sum(0)  375 us
    reduce_scatter x1, waiting for transfers between devices, local(): lax.psum_scatter(grad_out, 'dp', scatter_dimension=1, tiled=True)  185 us
    dot_general x230, matrix products, fast_dot(): return jnp.dot(left_side, right_side, preferred_element_type=jnp.float32)  176 us
    psum x1, waiting for transfers between devices, local(): feed_sum = lax.psum(fast_dot(hidden_low, w_mlp_down), 'mp')  145 us
    reduce_scatter x1, waiting for transfers between devices, local(): lax.psum_scatter(grad_mlp_down, 'dp', scatter_dimension=1, tiled=True)  118 us
    all_gather x2, waiting for transfers between devices, over_pieces(): return lax.all_gather(x, axis).sum(0)  101 us
    psum x1, waiting for transfers between devices, local(): attention = lax.psum(fast_dot(mixed_low, w_out), 'mp')  93.6 us
    squeeze x80, local copies, waits for them, and re-layouts, gla_head(): unused, outputs = lax.scan(jax.checkpoint(span_step), start_state, pieces)  69.5 us
  transfers between devices with their start and end apart: 8, of which 5 were waited for; matrix products, arithmetic and copies ran while one was open for 18% of the time, Pallas kernels for 0%

commit v1 on v0

v1 whole, which is shorter than its diff:
```python
import jax
import jax.numpy as jnp
from jax import lax
from jax.experimental import pallas as pl
from jax.experimental.pallas import tpu as pltpu
from jax.sharding import PartitionSpec as P

BLK = 64
CH = 256
EPS = 1e-6
SCALE = 128 ** -0.5
F32 = jnp.float32
BF16 = jnp.bfloat16
VMEM_BYTES = 56 * 1024 * 1024


def nn(a, b, **kw):
    return lax.dot_general(a, b, (((1,), (0,)), ((), ())), preferred_element_type=F32, **kw)


def nt(a, b, **kw):
    return lax.dot_general(a, b, (((1,), (1,)), ((), ())), preferred_element_type=F32, **kw)


def tn(a, b, **kw):
    return lax.dot_general(a, b, (((0,), (0,)), ((), ())), preferred_element_type=F32, **kw)


HIGH = dict(precision=lax.Precision.HIGHEST)


CORE = [(0, 1), (1, 0), (2, 3), (3, 2)]
ZLO = [(0, 2), (2, 0), (1, 3), (3, 1)]


def dp_perm(dy, dz, dx):
    out = []
    for y in range(4):
        for z in range(2):
            for x in range(4):
                out.append(((y * 2 + z) * 4 + x, (((y + dy) % 4) * 2 + (z + dz) % 2) * 4 + (x + dx) % 4))
    return out


XS = {1: dp_perm(0, 0, 1), 3: dp_perm(0, 0, -1), 2: dp_perm(0, 0, 2)}
YS = {1: dp_perm(1, 0, 0), 3: dp_perm(-1, 0, 0), 2: dp_perm(2, 0, 0)}
ZH = dp_perm(0, 1, 0)


def core_swap(v):
    return lax.ppermute(v, "mp", CORE)


def z_swap(v):
    return lax.ppermute(v, "mp", ZLO)


def rows_of(v, start, size):
    return lax.dynamic_slice_in_dim(v, start, size, 0)


def item_starts(len_ref):
    starts, total = [], jnp.int32(0)
    for j in range(8):
        starts.append(total)
        total = total + len_ref[0, j]
    return starts


def start_at(starts, place):
    best = jnp.int32(0)
    for s in starts[1:]:
        best = jnp.where(s <= place, jnp.maximum(best, s), best)
    return best


def chunk_masks(starts, base):
    row = lax.broadcasted_iota(jnp.int32, (CH, CH), 0)
    col = lax.broadcasted_iota(jnp.int32, (CH, CH), 1)
    blk = jnp.bitwise_and(row, -BLK)
    row1 = lax.broadcasted_iota(jnp.int32, (CH, 128), 0)
    place = row1 + base
    low = jnp.zeros_like(place)
    for s in starts[1:]:
        low = jnp.where(place >= s, jnp.maximum(low, s), low)
    low = low - base
    blk1 = jnp.bitwise_and(row1, -BLK)
    carried = low < blk1
    low_wide = jnp.concatenate([low, low], axis=1)
    causal = (col <= row) & (col >= blk)
    visible = causal & (col >= low_wide)
    return causal, visible, carried


def block_scalars(starts, base, b):
    first = base + b * BLK
    origin = start_at(starts, first + BLK - 1)
    keep = jnp.where(origin < first, 1.0, 0.0).astype(F32)
    place = lax.broadcasted_iota(jnp.int32, (BLK, 128), 0) + first
    return keep, place >= origin


def scaled_parts(q, k, cum):
    last = jnp.broadcast_to(cum.reshape(CH // BLK, BLK, 128)[:, BLK - 1 :, :], (CH // BLK, BLK, 128))
    last = last.reshape(CH, 128)
    e, en, ef = jnp.exp(cum), jnp.exp(-cum), jnp.exp(last - cum)
    qf = q.astype(F32) * SCALE * e
    ks = k.astype(F32) * en
    kf = k.astype(F32) * ef
    return last, e, en, ef, qf, ks, kf


def mixer_forward(
    len_ref, tok_ref, g1_ref, wq_ref, wk_ref, wv_ref, wgd_ref, wgu_ref, bias_ref,
    n_ref, q_ref, k_ref, v_ref, low_ref, logit_ref, cum_ref, mixed_ref, st_ref, state,
):
    step = pl.program_id(0)
    base = step * CH
    starts = item_starts(len_ref)

    @pl.when(step == 0)
    def _():
        state[...] = jnp.zeros_like(state)

    x = tok_ref[...].astype(F32)
    r = lax.rsqrt(jnp.mean(x * x, axis=-1, keepdims=True) + EPS)
    n = (x * r * g1_ref[...]).astype(BF16)
    n_ref[...] = n
    q = nn(n, wq_ref[...]).astype(BF16)
    k = nn(n, wk_ref[...]).astype(BF16)
    v = nn(n, wv_ref[...]).astype(BF16)
    low = nn(n, wgd_ref[...]).astype(BF16)
    q_ref[...] = q
    k_ref[...] = k
    v_ref[...] = v
    low_ref[...] = low
    logits = nn(low, wgu_ref[...]) + bias_ref[...]
    logit_ref[...] = logits
    decays = (jnp.minimum(logits, 0.0) - jnp.log1p(jnp.exp(-jnp.abs(logits)))) * (1.0 / 16.0)
    causal, visible, carried = chunk_masks(starts, base)
    cum = nn(jnp.where(causal, 1.0, 0.0).astype(F32), decays, **HIGH)
    cum_ref[...] = cum
    last, e, en, ef, qf, ks, kf = scaled_parts(q, k, cum)
    qs, ks, kf = qf.astype(BF16), ks.astype(BF16), kf.astype(BF16)
    scores = jnp.where(visible, nt(qs, ks), 0.0).astype(BF16)
    out = nn(scores, v)
    q_carried = jnp.where(carried, qf, 0.0).astype(BF16)
    for b in range(CH // BLK):
        sl = slice(b * BLK, (b + 1) * BLK)
        keep, tail = block_scalars(starts, base, b)
        s = state[...]
        st_ref[b] = s
        inter = nt(q_carried[sl], s.astype(BF16))
        mixed_ref[sl, :] = (out[sl] + inter).astype(BF16).astype(F32)
        k_tail = jnp.where(tail, kf[sl].astype(F32), 0.0).astype(BF16)
        state[...] = keep * jnp.exp(last[b * BLK : b * BLK + 1]) * s + tn(v[sl], k_tail)


def run_mixer_forward(lengths, tokens, g1, wq, wk, wv, wgd, wgu, bias):
    t = tokens.shape[0]
    whole = lambda a: pl.BlockSpec(a.shape, lambda i: (0,) * a.ndim)
    rows = lambda c: pl.BlockSpec((CH, c), lambda i: (i, 0))
    nb = CH // BLK
    outs = [
        ((t, 1024), BF16), ((t, 128), BF16), ((t, 128), BF16), ((t, 256), BF16), ((t, 16), BF16),
        ((t, 128), F32), ((t, 128), F32), ((t, 256), F32),
    ]
    return pl.pallas_call(
        mixer_forward,
        grid=(t // CH,),
        in_specs=[pl.BlockSpec(memory_space=pltpu.SMEM), rows(1024), whole(g1), whole(wq), whole(wk), whole(wv),
                  whole(wgd), whole(wgu), whole(bias)],
        out_specs=[rows(s[1]) for s, _ in outs] + [pl.BlockSpec((nb, 256, 128), lambda i: (i, 0, 0))],
        out_shape=[jax.ShapeDtypeStruct(s, d) for s, d in outs] + [jax.ShapeDtypeStruct((t // BLK, 256, 128), F32)],
        scratch_shapes=[pltpu.VMEM((256, 128), F32)],
        compiler_params=pltpu.CompilerParams(vmem_limit_bytes=VMEM_BYTES),
        cost_estimate=pl.CostEstimate(flops=2 * t * 1024 * 600, bytes_accessed=12 << 20, transcendentals=t * 700),
        name="mixer_forward",
    )(lengths, tokens, g1, wq, wk, wv, wgd, wgu, bias)


def feed_kernel(
    tok_ref, cot_ref, m0_ref, m1_ref, m2_ref, m3_ref, w0_ref, w1_ref, w2_ref, w3_ref, g2_ref, wg_ref, wu_ref, wd_ref,
    mid_ref, n_ref, hid_ref, gg_ref, feed_ref, part_ref, wo,
):
    @pl.when(pl.program_id(0) == 0)
    def _():
        wo[0:256] = w0_ref[...]
        wo[256:512] = w1_ref[...].astype(BF16)
        wo[512:768] = w2_ref[...].astype(BF16)
        wo[768:1024] = w3_ref[...].astype(BF16)

    mixed = jnp.concatenate([m0_ref[...], m1_ref[...], m2_ref[...], m3_ref[...]], axis=1).astype(BF16)
    mid = tok_ref[...].astype(F32) + nn(mixed, wo[...])
    mid_ref[...] = mid
    r = lax.rsqrt(jnp.mean(mid * mid, axis=-1, keepdims=True) + EPS)
    n = (mid * r * g2_ref[...]).astype(BF16)
    n_ref[...] = n
    pre = nn(n, wg_ref[...])
    up = nn(n, wu_ref[...])
    sg = jax.nn.sigmoid(pre)
    act = pre * sg
    hid = (act * up).astype(BF16)
    hid_ref[...] = hid
    feed_ref[...] = nn(hid, wd_ref[...])
    gh = nt(cot_ref[...], wd_ref[...])
    gg = (gh * up * sg * (1.0 + pre * (1.0 - sg))).astype(BF16)
    gu = (gh * act).astype(BF16)
    gg_ref[:, 0:704] = gg
    gg_ref[:, 704:1408] = gu
    part_ref[...] = nt(gg, wg_ref[...]) + nt(gu, wu_ref[...])


def run_feed(start, count, tokens, cot, mixed, wo, g2, wg, wu, wd):
    first = start // CH
    whole = lambda a: pl.BlockSpec(a.shape, lambda i: (0,) * a.ndim)
    rows = lambda c: pl.BlockSpec((CH, c), lambda i: (first + i, 0))
    outr = lambda c: pl.BlockSpec((CH, c), lambda i: (i, 0))
    outs = [((count, 1024), F32), ((count, 1024), BF16), ((count, 704), BF16), ((count, 1408), BF16),
            ((count, 1024), F32), ((count, 1024), F32)]
    return pl.pallas_call(
        feed_kernel,
        grid=(count // CH,),
        in_specs=[rows(1024), rows(1024)] + [rows(256)] * 4 + [whole(w) for w in wo] + [whole(g2), whole(wg), whole(wu), whole(wd)],
        out_specs=[outr(s[1]) for s, _ in outs],
        out_shape=[jax.ShapeDtypeStruct(s, d) for s, d in outs],
        scratch_shapes=[pltpu.VMEM((1024, 1024), BF16)],
        compiler_params=pltpu.CompilerParams(vmem_limit_bytes=VMEM_BYTES),
        cost_estimate=pl.CostEstimate(flops=2 * count * 1024 * 5300, bytes_accessed=count * 22000, transcendentals=count * 704),
        name="feed_both_ways",
    )(tokens, cot, *mixed, *wo, g2, wg, wu, wd)


def mixer_backward(
    len_ref, gm_ref, tok_ref, n_ref, q_ref, k_ref, v_ref, low_ref, logit_ref, cum_ref, st_ref,
    wo_ref, wq_ref, wk_ref, wv_ref, wgd_ref, wgu_ref,
    dqkv_ref, part_ref, ga_ref, small_ref, gup_ref, bias_ref, dstate, dq_s, dv_s, dk_s, dl_s,
):
    step = pl.program_id(0)
    steps = pl.num_programs(0)
    base = (steps - 1 - step) * CH
    starts = item_starts(len_ref)

    @pl.when(step == 0)
    def _():
        dstate[...] = jnp.zeros_like(dstate)
        small_ref[...] = jnp.zeros_like(small_ref)
        gup_ref[...] = jnp.zeros_like(gup_ref)
        bias_ref[...] = jnp.zeros_like(bias_ref)

    ga = gm_ref[...].astype(BF16)
    ga_ref[...] = ga
    g = nt(ga, wo_ref[...]).astype(BF16)
    q, k, v, cum = q_ref[...], k_ref[...], v_ref[...], cum_ref[...]
    causal, visible, carried = chunk_masks(starts, base)
    last, e, en, ef, qf, ksf, kff = scaled_parts(q, k, cum)
    qs, ks, kf = qf.astype(BF16), ksf.astype(BF16), kff.astype(BF16)
    scores = jnp.where(visible, nt(qs, ks), 0.0).astype(BF16)
    dscores = jnp.where(visible, nt(g, v), 0.0).astype(BF16)
    dv = tn(scores, g)
    dqs = nn(dscores, ks)
    dks = tn(dscores, qs)
    q_carried = jnp.where(carried, qf, 0.0).astype(BF16)
    for b in reversed(range(CH // BLK)):
        sl = slice(b * BLK, (b + 1) * BLK)
        keep, tail = block_scalars(starts, base, b)
        ds = dstate[...]
        dsb = ds.astype(BF16)
        s = st_ref[b]
        k_tail = jnp.where(tail, kff[sl], 0.0).astype(BF16)
        dv_s[sl, :] = dv[sl] + nt(k_tail, dsb)
        dkf = jnp.where(tail, nn(v[sl], dsb), 0.0)
        dk_s[sl, :] = dkf
        dq_s[sl, :] = dqs[sl] + jnp.where(carried[sl], nn(g[sl], s.astype(BF16)), 0.0)
        grow = keep * jnp.exp(last[b * BLK : b * BLK + 1])
        dlast = grow * jnp.sum(s * ds, axis=0, keepdims=True) + jnp.sum(dkf * kff[sl], axis=0, keepdims=True)
        dl_s[sl, :] = jnp.broadcast_to(dlast, (BLK, 128))
        dstate[...] = grow * ds + tn(g[sl], q_carried[sl])
    dqs = dq_s[...]
    dkf = dk_s[...]
    dq = (dqs * (SCALE * e)).astype(BF16)
    dk = (dks * en + dkf * ef).astype(BF16)
    dv = dv_s[...].astype(BF16)
    dqkv_ref[:, 0:128] = dq
    dqkv_ref[:, 128:256] = dk
    dqkv_ref[:, 256:512] = dv
    dcum = dqs * qf - dks * ksf - dkf * kff
    ddec = tn(jnp.where(causal, 1.0, 0.0).astype(F32), dcum, **HIGH) + dl_s[...]
    glog = ddec * jax.nn.sigmoid(-logit_ref[...]) * (1.0 / 16.0)
    bias_ref[0:1, :] += jnp.sum(glog, axis=0, keepdims=True)
    gup_ref[...] += tn(low_ref[...].astype(F32), glog, **HIGH)
    glr = nt(glog, wgu_ref[...].astype(F32), **HIGH).astype(BF16)
    part = nt(dq, wq_ref[...]) + nt(dk, wk_ref[...]) + nt(dv, wv_ref[...]) + nt(glr, wgd_ref[...])
    part_ref[...] = part
    small_ref[0:16, :] += tn(glr, n_ref[...])
    x = tok_ref[...].astype(F32)
    r = lax.rsqrt(jnp.mean(x * x, axis=-1, keepdims=True) + EPS)
    small_ref[16:17, :] += jnp.sum(part * x * r, axis=0, keepdims=True)


def run_mixer_backward(lengths, gm, tokens, n, q, k, v, low, logits, cum, st, wo, wq, wk, wv, wgd, wgu):
    t = tokens.shape[0]
    steps = t // CH
    whole = lambda a: pl.BlockSpec(a.shape, lambda i: (0,) * a.ndim)
    rows = lambda c: pl.BlockSpec((CH, c), lambda i: (steps - 1 - i, 0))
    nb = CH // BLK
    fixed = lambda s: pl.BlockSpec(s, lambda i: (0, 0))
    return pl.pallas_call(
        mixer_backward,
        grid=(steps,),
        in_specs=[pl.BlockSpec(memory_space=pltpu.SMEM), rows(1024), rows(1024), rows(1024), rows(128), rows(128), rows(256),
                  rows(16), rows(128), rows(128), pl.BlockSpec((nb, 256, 128), lambda i: (steps - 1 - i, 0, 0)),
                  whole(wo), whole(wq), whole(wk), whole(wv), whole(wgd), whole(wgu)],
        out_specs=[rows(512), rows(1024), rows(1024), fixed((24, 1024)), fixed((16, 128)), fixed((8, 128))],
        out_shape=[jax.ShapeDtypeStruct((t, 512), BF16), jax.ShapeDtypeStruct((t, 1024), F32),
                   jax.ShapeDtypeStruct((t, 1024), BF16), jax.ShapeDtypeStruct((24, 1024), F32),
                   jax.ShapeDtypeStruct((16, 128), F32), jax.ShapeDtypeStruct((8, 128), F32)],
        scratch_shapes=[pltpu.VMEM((256, 128), F32), pltpu.VMEM((CH, 128), F32), pltpu.VMEM((CH, 256), F32),
                        pltpu.VMEM((CH, 128), F32), pltpu.VMEM((CH, 128), F32)],
        compiler_params=pltpu.CompilerParams(vmem_limit_bytes=VMEM_BYTES),
        cost_estimate=pl.CostEstimate(flops=2 * t * 1024 * 1200, bytes_accessed=20 << 20, transcendentals=t * 600),
        name="mixer_backward",
    )(lengths, gm, tokens, n, q, k, v, low, logits, cum, st, wo, wq, wk, wv, wgd, wgu)


def mp_scatter(part, core, z):
    half, quarter = part.shape[0] // 2, part.shape[0] // 4
    acc = rows_of(part, core * half, half) + core_swap(rows_of(part, (1 - core) * half, half))
    return rows_of(acc, z * quarter, quarter) + z_swap(rows_of(acc, (1 - z) * quarter, quarter))


def paired(own, other, bit):
    first = jnp.where(bit == 0, own, other)
    second = jnp.where(bit == 0, other, own)
    return jnp.concatenate([first, second], axis=0)


def mp_join(own, core, z):
    half = paired(own, z_swap(own), z)
    return paired(half, core_swap(half), core)


def norm_back(y, gain, dn):
    r = lax.rsqrt(jnp.mean(y * y, axis=-1, keepdims=True) + EPS)
    gd = dn * gain
    dy = r * gd - r * r * r * y * jnp.mean(gd * y, axis=-1, keepdims=True)
    return dy, jnp.sum(dn * y * r, axis=0)


def direct_scatter(chunk, at, shifts):
    total = chunk(at)
    for d in (2, 1, 3):
        total = total + lax.ppermute(chunk((at + d) % 4), "dp", shifts[d])
    return total


def dp_scatter(grads, y, zh, x):
    cut = [g.reshape(4, 2, 4, 2, 16, g.shape[1]) for g in grads]

    def take_x(i, h):
        return jnp.concatenate([lax.dynamic_index_in_dim(g, i, 2, False)[:, :, h] for g in cut], axis=-1)

    def take_y(i, h):
        return jnp.concatenate([lax.dynamic_index_in_dim(g, i, 0, False)[:, :, h] for g in cut], axis=-1)

    a = direct_scatter(lambda i: take_x(i, 0), x, XS)
    b = direct_scatter(lambda i: take_y(i, 1), y, YS)
    a = direct_scatter(lambda i: lax.dynamic_index_in_dim(a, i, 0, False), y, YS)
    b = direct_scatter(lambda i: lax.dynamic_index_in_dim(b, i, 1, False), x, XS)
    ab = jnp.concatenate([a, b], axis=1)
    mine = lax.dynamic_index_in_dim(ab, zh, 0, False)
    return mine + lax.ppermute(lax.dynamic_index_in_dim(ab, 1 - zh, 0, False), "dp", ZH)


def dp_total(v):
    for perm in (XS[1], XS[2], YS[1], YS[2], ZH):
        pass
    v = v + lax.ppermute(v, "dp", XS[2])
    v = v + lax.ppermute(v, "dp", XS[1])
    v = v + lax.ppermute(v, "dp", YS[2])
    v = v + lax.ppermute(v, "dp", YS[1])
    return v + lax.ppermute(v, "dp", ZH)


FEED_CHUNKS = 2


def local(tokens, lengths, g1, wq, wk, wv, wgd, wgu, bias, wout, g2, wg, wu, wd, cot):
    mp, dp = lax.axis_index("mp"), lax.axis_index("dp")
    core, z = mp % 2, mp // 2
    x, zh, y = dp % 4, (dp // 4) % 2, dp // 8
    t = tokens.shape[0]
    g1r, g2r, biasr = g1.reshape(1, -1), g2.reshape(1, -1), bias.reshape(1, -1)

    wide = wout.astype(F32)
    wout_z = z_swap(wide)
    wout_c = core_swap(wide)
    wout_cz = core_swap(wout_z)
    wo = (wout, wout_z, wout_c, wout_cz)

    n1, q, k, v, low, logits, cum, mixed, st = run_mixer_forward(lengths, tokens, g1r, wq, wk, wv, wgd, wgu, biasr)
    mixed_z = z_swap(mixed)
    mixed_c = core_swap(mixed)
    mixed_cz = core_swap(mixed_z)
    mixed_all = (mixed, mixed_z, mixed_c, mixed_cz)

    size = t // FEED_CHUNKS
    quarter = size // 4
    parts = {}
    for c in reversed(range(FEED_CHUNKS)):
        parts[c] = run_feed(c * size, size, tokens, cot, mixed_all, wo, g2r, wg, wu, wd)
    joined = [jnp.concatenate([parts[c][j] for c in range(FEED_CHUNKS)], axis=0) for j in range(4)]
    middle, n2, hid, gg = joined

    own_at = [c * size + core * (size // 2) + z * quarter for c in range(FEED_CHUNKS)]
    gm_own, gm_full = [None] * FEED_CHUNKS, [None] * FEED_CHUNKS
    gain2 = 0.0
    dns = {c: mp_scatter(parts[c][5], core, z) for c in reversed(range(FEED_CHUNKS))}
    for c in reversed(range(FEED_CHUNKS)):
        dmid, gain = norm_back(rows_of(middle, own_at[c], quarter), g2, dns[c])
        gain2 = gain2 + gain
        gm_own[c] = rows_of(cot, own_at[c], quarter).astype(F32) + dmid
        gm_full[c] = mp_join(gm_own[c], core, z)
    grad_middle = jnp.concatenate(gm_full, axis=0)

    grad_gate_up_t = tn(n2, gg)
    grad_down_t = tn(cot, hid)
    mlp_rows = dp_scatter([grad_gate_up_t, grad_down_t], y, zh, x)

    dqkv, part1, ga, small, gup, gbias = run_mixer_backward(
        lengths, grad_middle, tokens, n1, q, k, v, low, logits, cum, st, wout, wq, wk, wv, wgd, wgu)

    feed = jnp.concatenate([mp_join(mp_scatter(parts[c][4], core, z), core, z) for c in range(FEED_CHUNKS)], axis=0)
    result = (middle + feed).astype(BF16)

    own1 = core * (t // 2) + z * (t // 4)
    dn1 = mp_scatter(part1, core, z)
    dx, _ = norm_back(rows_of(tokens, own1, t // 4).astype(F32), g1, dn1)
    grad_tokens = mp_join(dx, core, z) + grad_middle

    grad_qkv = tn(n1, dqkv)
    grad_out_t = tn(ga, mixed.astype(BF16))
    att_rows = dp_scatter([grad_qkv, grad_out_t], y, zh, x)

    shared = jnp.concatenate([small[0:17], gain2.reshape(1, 1024), jnp.zeros((6, 1024), F32)], axis=0)
    shared = shared + core_swap(shared)
    shared = shared + z_swap(shared)
    rest = jnp.concatenate([gup.reshape(2, 1024), jnp.pad(gbias[0:1], ((0, 5), (0, 896)))], axis=0)
    total = dp_total(jnp.concatenate([shared, rest], axis=0))

    return (
        result,
        grad_tokens,
        total[16],
        att_rows[:, 0:128],
        att_rows[:, 128:256],
        att_rows[:, 256:512],
        total[0:16].T,
        total[24:26].reshape(16, 128),
        total[26, 0:128],
        att_rows[:, 512:768].T,
        total[17],
        mlp_rows[:, 0:704],
        mlp_rows[:, 704:1408],
        mlp_rows[:, 1408:2112].T,
    )


def solution(mesh):
    placed = (
        P("dp", None), P("dp", None), P(), P(None, "mp"), P(None, "mp"), P(None, "mp"), P(), P(None, "mp"),
        P("mp"), P("mp", None), P(), P(None, "mp"), P(None, "mp"), P("mp", None), P("dp", None),
    )
    outs = (
        P("dp", None), P("dp", None), P(), P("dp", "mp"), P("dp", "mp"), P("dp", "mp"), P(), P(None, "mp"),
        P("mp"), P("mp", "dp"), P(), P("dp", "mp"), P("dp", "mp"), P("mp", "dp"),
    )
    return jax.shard_map(local, mesh=mesh, in_specs=placed, out_specs=outs, check_vma=False)
```

time: 1700 us -> 402 us (0.24)
  waiting for transfers between devices: 642 us -> 166 us
  blocking collectives: 375 us -> 0 us
  other arithmetic: 228 us -> 33.7 us
  matrix products: 183 us -> 14 us
  local copies, waits for them, and re-layouts: 191 us -> 32.9 us
  starting transfers between devices: 1.24 us -> 91.6 us
  Pallas kernels: 0 us -> 57.2 us
  loops' own time: 43 us -> 0 us
    all_gather x5 -> x0, blocking collectives: 375 us -> none  [over_pieces(): return lax.all_gather(x, axis).sum(0)]
    reduce_scatter x2 -> x0, waiting for transfers between devices: 304 us -> none  [the longest x1 185 us: local(): lax.psum_scatter(grad_out, 'dp', scatter_dimension=1, tiled=True)]
    psum x2 -> x0, waiting for transfers between devices: 238 us -> none  [the longest x1 145 us: local(): feed_sum = lax.psum(fast_dot(hidden_low, w_mlp_down), 'mp')]
    dot_general x235 -> x4, matrix products: 183 us -> 14 us  [tn(): lax.dot_general(a, b, (((0,), (0,)), ((), ())), preferred_element_type=F3...]
    ppermute x0 -> x59, waiting for transfers between devices: none -> 166 us  [the longest x13 98.7 us: z_swap(): return lax.ppermute(v, 'mp', ZLO)]
    all_gather x2 -> x0, waiting for transfers between devices: 101 us -> none  [over_pieces(): return lax.all_gather(x, axis).sum(0)]
    ppermute x0 -> x59, starting transfers between devices: none -> 91.6 us  [the longest x24 53.5 us: direct_scatter(): total = total + lax.ppermute(chunk((at + d) % 4), 'dp', shifts[d])]
    eq x48 -> x0, other arithmetic: 73.6 us -> none  [the longest x32 52.1 us: span_step(): item_ids == item_ids[-1]]
  transfers between devices with their start and end apart: 8 -> 59, of which waited for: 5 -> 22; matrix products, arithmetic and copies ran while one was open for 18% -> 13% of each run, Pallas kernels for 0% -> 7%
where the time goes in v1:
time: 402 us; the launch traced here: 398 us
  waiting for transfers between devices  166 us (41%)
  starting transfers between devices  91.6 us (23%)
  Pallas kernels  57.2 us (14%)
  other arithmetic  33.7 us (8%)
  local copies, waits for them, and re-layouts  32.9 us (8%)
  matrix products  14 us (3%)
    ppermute x13, waiting for transfers between devices, z_swap(): return lax.ppermute(v, 'mp', ZLO)  98.7 us
    ppermute x24, starting transfers between devices, direct_scatter(): total = total + lax.ppermute(chunk((at + d) % 4), 'dp', shifts[d])  53.5 us
    ppermute x24, waiting for transfers between devices, direct_scatter(): total = total + lax.ppermute(chunk((at + d) % 4), 'dp', shifts[d])  52.7 us
    pallas_call x2, Pallas kernels, run_feed(): pl.pallas_call(feed_kernel, grid=(count // CH,), in_specs=[rows(1024), ro...  28 us
    pallas_call x1, Pallas kernels, run_mixer_backward(): pl.pallas_call(mixer_backward, grid=(steps,), in_specs=[pl.BlockSpec(memo...  16.6 us
    ppermute x13, starting transfers between devices, z_swap(): return lax.ppermute(v, 'mp', ZLO)  15.2 us
    dot_general x4, matrix products, tn(): lax.dot_general(a, b, (((0,), (0,)), ((), ())), preferred_element_type=F3...  14 us
    unnamed x80, local copies, waits for them, and re-layouts  12.7 us
  transfers between devices with their start and end apart: 59, of which 22 were waited for; matrix products, arithmetic and copies ran while one was open for 13% of the time, Pallas kernels for 7%

profile of v1, /device:TPU:0, one launch (start us, length us, event | category | flops | bytes accessed | tf_op | source)
XLA Modules:
  0.0 398.2 jit_solution(12020433401058301860)
XLA Ops:
  6.4 12.6 %mixer_forward.1 = (bf16[1024,1024]{1,0:T(8,128)(2,1)}, bf16[1024,128]{1,0:T(8,128)(2,1)}, bf16[1024,128]{1,0:T(8,128)(2,1)}, bf16[1024,256]{1,0:T(8,128)(2,1)},...) custom-call(s32[1,8]{1,0:T(1,128)} %len_ref.3, ...), custom_call_target="tpu_custom_call" | custom-call | flops 1258291200 | bytes 12582912 | tf_op jit(solution)/shard_map/mixer_forward/pallas_call | solution.py:168
  19.7 9.5 %collective-permute-done.3.w1_ref = f32[256,1024]{1,0:T(8,128)} collective-permute-done((f32[256,1024]{1,0:T(8,128)}, f32[256,1024]{1,0:T(8,128)}, u32[]{:S(2)}, u32[]{:S(2)}) %collective-permute-start.3) | collective-permute-done | bytes 1048608 | tf_op jit(solution)/shard_map/ppermute | solution.py:55
  29.1 21.6 %collective-permute-done.m1_ref = f32[1024,256]{1,0:T(8,128)} collective-permute-done((f32[1024,256]{1,0:T(8,128)}, f32[1024,256]{1,0:T(8,128)}, u32[]{:S(2)}, u32[]{:S(2)}) %collective-permute-start) | collective-permute-done | bytes 1048608 | tf_op jit(solution)/shard_map/ppermute | solution.py:55
  54.4 14.0 %feed_both_ways.3 = (f32[512,1024]{1,0:T(8,128)}, bf16[512,1024]{1,0:T(8,128)(2,1)}, bf16[512,704]{1,0:T(8,128)(2,1)}, bf16[512,1408]{1,0:T(8,128)(2,1)}, f32[512,1024]{1,0:T(8,128)}, /*index=5*/f32[512,1024]{1,0:T(8,128)}) custom-call(bf16[1024,1024]{1,0:T(8,128)(2,1)} %tok_ref.7, bf16[1024,1024]{1,0:T(8,128)(2,1)} %cot_ref.3, ...), custom_call_target="tpu_custom_call" | custom-call | flops 5557452800 | bytes 11264000 | tf_op jit(solution)/shard_map/feed_both_ways/pallas_call | solution.py:221
  68.4 14.1 %feed_both_ways.2 = (f32[512,1024]{1,0:T(8,128)}, bf16[512,1024]{1,0:T(8,128)(2,1)}, bf16[512,704]{1,0:T(8,128)(2,1)}, bf16[512,1408]{1,0:T(8,128)(2,1)}, f32[512,1024]{1,0:T(8,128)}, /*index=5*/f32[512,1024]{1,0:T(8,128)}) custom-call(bf16[1024,1024]{1,0:T(8,128)(2,1)} %tok_ref.7, bf16[1024,1024]{1,0:T(8,128)(2,1)} %cot_ref.3, ...), custom_call_target="tpu_custom_call" | custom-call | flops 5557452800 | bytes 11264000 | tf_op jit(solution)/shard_map/feed_both_ways/pallas_call | solution.py:221
  82.5 4.4 %convolution_bitcast_fusion = f32[1024,704]{0,1:T(8,128)} fusion(bf16[1024,1024]{1,0:T(8,128)(2,1)S(1)} %copy-done.14, bf16[512,704]{1,0:T(8,128)(2,1)S(1)} %copy-done.27, bf16[512,704]{1,0:T(8,128)(2,1)} %get-tuple-element.66), kind=kOutput, calls=%fused_computation.13 | convolution fusion | flops 1479278592 | bytes 6422528 | tf_op jit(solution)/shard_map/dot_general | solution.py:26
  89.6 6.0 %fusion.1 = f32[1024,1408]{1,0:T(8,128)S(1)} fusion(bf16[512,1408]{1,0:T(8,128)(2,1)} %get-tuple-element.65, bf16[512,1408]{1,0:T(8,128)(2,1)} %get-tuple-element.64, bf16[512,1024]{1,0:T(8,128)(2,1)} %get-tuple-element.63, bf16[512,1024]{1,0:T(8,128)(2,1)} %get-tuple-element.62), kind=kOutput, calls=%fused_computation.4 | convolution fusion | flops 2962751488 | bytes 10747904 | tf_op jit(solution)/shard_map/dot_general | solution.py:26
  117.2 13.8 %collective-permute-done.47 = f32[4,2,16,2112]{3,2,1,0:T(8,128)S(1)} collective-permute-done((f32[4,2,16,2112]{3,2,1,0:T(8,128)S(1)}, f32[4,2,16,2112]{3,2,1,0:T(8,128)S(1)}, u32[]{:S(2)}, u32[]{:S(2)}) %collective-permute-start.47) | collective-permute-done | bytes 1081376 | tf_op jit(solution)/shard_map/ppermute | solution.py:353
  134.0 21.9 %collective-permute-done.46 = f32[4,2,16,2112]{3,2,1,0:T(8,128)S(1)} collective-permute-done((f32[4,2,16,2112]{3,2,1,0:T(8,128)S(1)}, f32[4,2,16,2112]{3,2,1,0:T(8,128)S(1)}, u32[]{:S(2)}, u32[]{:S(2)}) %collective-permute-start.46) | collective-permute-done | bytes 1081376 | tf_op jit(solution)/shard_map/ppermute | solution.py:353
  160.3 4.8 %collective-permute-start.49 = (f32[2,16,2112]{2,1,0:T(8,128)S(1)}, f32[2,16,2112]{2,1,0:T(8,128)S(1)}, u32[]{:S(2)}, u32[]{:S(2)}) collective-permute-start(f32[2,16,2112]{2,1,0:T(8,128)S(1)} %get-tuple-element.121), channel_id=1, source_target_pairs={{0,64},{4,68},{8,72},{12,76},{16,80},{20,84},{24,88},{28,92},{32,9... | collective-permute-start | bytes 811016 | tf_op jit(solution)/shard_map/ppermute | solution.py:353
  180.3 5.1 %collective-permute-done.57 = f32[2,16,2112]{2,1,0:T(8,128)S(1)} collective-permute-done((f32[2,16,2112]{2,1,0:T(8,128)S(1)}, f32[2,16,2112]{2,1,0:T(8,128)S(1)}, u32[]{:S(2)}, u32[]{:S(2)}) %collective-permute-start.57) | collective-permute-done | bytes 270368 | tf_op jit(solution)/shard_map/ppermute | solution.py:353
  187.7 3.7 collective-permute-start.58
  191.5 14.1 %collective-permute-done.7 = f32[128,1024]{1,0:T(8,128)S(1)} collective-permute-done((f32[128,1024]{1,0:T(8,128)S(1)}, f32[128,1024]{1,0:T(8,128)S(1)}, u32[]{:S(2)}, u32[]{:S(2)}) %collective-permute-start.7) | collective-permute-done | bytes 524320 | tf_op jit(solution)/shard_map/ppermute | solution.py:55
  210.5 3.4 collective-permute-done.58
  214.7 30.6 %collective-permute-done.16 = f32[128,1024]{1,0:T(8,128)S(1)} collective-permute-done((f32[128,1024]{1,0:T(8,128)S(1)}, f32[128,1024]{1,0:T(8,128)S(1)}, u32[]{:S(2)}, u32[]{:S(2)}) %collective-permute-start.16) | collective-permute-done | bytes 524320 | tf_op jit(solution)/shard_map/ppermute | solution.py:55
  245.6 8.4 %collective-permute-done.20 = f32[128,1024]{1,0:T(8,128)S(1)} collective-permute-done((f32[128,1024]{1,0:T(8,128)S(1)}, f32[128,1024]{1,0:T(8,128)S(1)}, u32[]{:S(2)}, u32[]{:S(2)}) %collective-permute-start.20) | collective-permute-done | bytes 524320 | tf_op jit(solution)/shard_map/ppermute | solution.py:55
  260.2 16.6 %mixer_backward.1 = (bf16[1024,512]{1,0:T(8,128)(2,1)}, f32[1024,1024]{1,0:T(8,128)}, bf16[1024,1024]{1,0:T(8,128)(2,1)}, f32[24,1024]{1,0:T(8,128)}, f32[16,128]{1,0:T(8,128)}, /*index=5*/f32[8,128]{1,0:T(8,128)}) custom-call(s32[1,8]{1,0:T(1,128)} %len_ref.3, f32[1024,1024]{1,0:T(8,128)} %pad_maximum_fusion.gm_ref, bf16[1024,1024]{1,0:T(8,128)(2,1)} %tok_ref.7, ...), custom_call_target="tpu_custom_call" | custom-call | flops 2516582400 | bytes 20971520 | tf_op jit(solution)/shard_map/mixer_backward/pallas_call | solution.py:308
  310.8 14.5 %collective-permute-done.27 = f32[24,1024]{1,0:T(8,128)S(1)} collective-permute-done((f32[24,1024]{1,0:T(8,128)S(1)}, f32[24,1024]{1,0:T(8,128)S(1)}, u32[]{:S(2)}, u32[]{:S(2)}) %collective-permute-start.27) | collective-permute-done | bytes 98336 | tf_op jit(solution)/shard_map/ppermute | solution.py:55
  339.6 5.7 %collective-permute-start.29 = (f32[32,1024]{1,0:T(8,128)S(1)}, f32[32,1024]{1,0:T(8,128)S(1)}, u32[]{:S(2)}, u32[]{:S(2)}) collective-permute-start(f32[32,1024]{1,0:T(8,128)S(1)} %fusion.45), channel_id=1, source_target_pairs={{0,4},{4,8},{8,12},{12,0},{16,20},{20,24},{24,28},{28,16},{32,36},... | collective-permute-start | bytes 393224 | tf_op jit(solution)/shard_map/ppermute | solution.py:379
  350.9 3.7 collective-permute-done.41
  357.6 8.6 %collective-permute-start.44 = (f32[2,16,768]{2,1,0:T(8,128)S(1)}, f32[2,16,768]{2,1,0:T(8,128)S(1)}, u32[]{:S(2)}, u32[]{:S(2)}) collective-permute-start(f32[2,16,768]{2,1,0:T(8,128)S(1)} %get-tuple-element.141), channel_id=1, source_target_pairs={{0,12},{4,0},{8,4},{12,8},{16,28},{20,16},{24,20},{28,24},{32,44},... | collective-permute-start | bytes 294920 | tf_op jit(solution)/shard_map/ppermute | solution.py:353
  372.1 3.7 collective-permute-start.45
  380.1 4.0 collective-permute-done.31
  385.5 5.2 %collective-permute-done.32 = f32[32,1024]{1,0:T(8,128)S(1)} collective-permute-done((f32[32,1024]{1,0:T(8,128)S(1)}, f32[32,1024]{1,0:T(8,128)S(1)}, u32[]{:S(2)}, u32[]{:S(2)}) %collective-permute-start.32) | collective-permute-done | bytes 131104 | tf_op jit(solution)/shard_map/ppermute | solution.py:382
  (324 shorter events, 146.1 us)
Async XLA Ops:
  2.8 26.3 %collective-permute-start.3 = (f32[256,1024]{1,0:T(8,128)}, f32[256,1024]{1,0:T(8,128)}, u32[]{:S(2)}, u32[]{:S(2)}) collective-permute-start(f32[256,1024]{1,0:T(8,128)} %convert_element_type.20), channel_id=1, source_target_pairs={{0,2},{2,0},{1,3},{3,1},{4,6},{6,4},{5,7},{7,5},{8,10},{10,8},{9,1... | collective-permute-start | bytes 3145736 | tf_op jit(solution)/shard_map/ppermute | solution.py:55
  19.0 31.8 %collective-permute-start = (f32[1024,256]{1,0:T(8,128)}, f32[1024,256]{1,0:T(8,128)}, u32[]{:S(2)}, u32[]{:S(2)}) collective-permute-start(f32[1024,256]{1,0:T(8,128)} %get-tuple-element.41.m0_ref), channel_id=1, source_target_pairs={{0,2},{2,0},{1,3},{3,1},{4,6},{6,4},{5,7},{7,5},{8,10},{10,8},{9,1... | collective-permute-start | bytes 3145736 | tf_op jit(solution)/shard_map/ppermute | solution.py:55
  19.1 35.3 %collective-permute-start.4 = (f32[256,1024]{1,0:T(8,128)}, f32[256,1024]{1,0:T(8,128)}, u32[]{:S(2)}, u32[]{:S(2)}) collective-permute-start(f32[256,1024]{1,0:T(8,128)} %convert_element_type.20), channel_id=1, source_target_pairs={{0,1},{1,0},{2,3},{3,2},{4,5},{5,4},{6,7},{7,6},{8,9},{9,8},{10,11... | collective-permute-start | bytes 3145736 | tf_op jit(solution)/shard_map/ppermute | solution.py:51
  19.2 35.2 %collective-permute-start.1 = (f32[1024,256]{1,0:T(8,128)}, f32[1024,256]{1,0:T(8,128)}, u32[]{:S(2)}, u32[]{:S(2)}) collective-permute-start(f32[1024,256]{1,0:T(8,128)} %get-tuple-element.41.m0_ref), channel_id=1, source_target_pairs={{0,1},{1,0},{2,3},{3,2},{4,5},{5,4},{6,7},{7,6},{8,9},{9,8},{10,11... | collective-permute-start | bytes 3145736 | tf_op jit(solution)/shard_map/ppermute | solution.py:51
  103.0 28.0 %collective-permute-start.47 = (f32[4,2,16,2112]{3,2,1,0:T(8,128)S(1)}, f32[4,2,16,2112]{3,2,1,0:T(8,128)S(1)}, u32[]{:S(2)}, u32[]{:S(2)}) collective-permute-start(f32[4,2,16,2112]{3,2,1,0:T(8,128)S(1)} %pad_maximum_fusion.3), channel_id=1, source_target_pairs={{0,4},{4,8},{8,12},{12,0},{16,20},{20,24},{24,28},{28,16},{32,36},... | collective-permute-start | bytes 3244040 | tf_op jit(solution)/shard_map/ppermute | solution.py:353
  107.2 48.6 %collective-permute-start.46 = (f32[4,2,16,2112]{3,2,1,0:T(8,128)S(1)}, f32[4,2,16,2112]{3,2,1,0:T(8,128)S(1)}, u32[]{:S(2)}, u32[]{:S(2)}) collective-permute-start(f32[4,2,16,2112]{3,2,1,0:T(8,128)S(1)} %pad_maximum_fusion.2), channel_id=1, source_target_pairs={{0,8},{4,12},{8,0},{12,4},{16,24},{20,28},{24,16},{28,20},{32,40},... | collective-permute-start | bytes 3244040 | tf_op jit(solution)/shard_map/ppermute | solution.py:353
  110.2 48.0 %collective-permute-start.48 = (f32[4,2,16,2112]{3,2,1,0:T(8,128)S(1)}, f32[4,2,16,2112]{3,2,1,0:T(8,128)S(1)}, u32[]{:S(2)}, u32[]{:S(2)}) collective-permute-start(f32[4,2,16,2112]{3,2,1,0:T(8,128)S(1)} %pad_maximum_fusion.4), channel_id=1, source_target_pairs={{0,12},{4,0},{8,4},{12,8},{16,28},{20,16},{24,20},{28,24},{32,44},... | collective-permute-start | bytes 3244040 | tf_op jit(solution)/shard_map/ppermute | solution.py:353
  112.1 48.2 %collective-permute-start.53 = (f32[2,4,16,2112]{3,2,1,0:T(8,128)S(1)}, f32[2,4,16,2112]{3,2,1,0:T(8,128)S(1)}, u32[]{:S(2)}, u32[]{:S(2)}) collective-permute-start(f32[2,4,16,2112]{3,2,1,0:T(8,128)S(1)} %pad_maximum_fusion.6), channel_id=1, source_target_pairs={{0,32},{4,36},{8,40},{12,44},{16,48},{20,52},{24,56},{28,60},{32,6... | collective-permute-start | bytes 3244040 | tf_op jit(solution)/shard_map/ppermute | solution.py:353
  114.0 51.4 %collective-permute-start.52 = (f32[2,4,16,2112]{3,2,1,0:T(8,128)S(1)}, f32[2,4,16,2112]{3,2,1,0:T(8,128)S(1)}, u32[]{:S(2)}, u32[]{:S(2)}) collective-permute-start(f32[2,4,16,2112]{3,2,1,0:T(8,128)S(1)} %pad_maximum_fusion.5), channel_id=1, source_target_pairs={{0,64},{4,68},{8,72},{12,76},{16,80},{20,84},{24,88},{28,92},{32,9... | collective-permute-start | bytes 3244040 | tf_op jit(solution)/shard_map/ppermute | solution.py:353
  130.9 34.5 %collective-permute-start.54 = (f32[2,4,16,2112]{3,2,1,0:T(8,128)S(1)}, f32[2,4,16,2112]{3,2,1,0:T(8,128)S(1)}, u32[]{:S(2)}, u32[]{:S(2)}) collective-permute-start(f32[2,4,16,2112]{3,2,1,0:T(8,128)S(1)} %pad_maximum_fusion.7), channel_id=1, source_target_pairs={{0,96},{4,100},{8,104},{12,108},{16,112},{20,116},{24,120},{28,124... | collective-permute-start | bytes 3244040 | tf_op jit(solution)/shard_map/ppermute | solution.py:353
  155.8 50.7 %collective-permute-start.19 = (f32[128,1024]{1,0:T(8,128)S(1)}, f32[128,1024]{1,0:T(8,128)S(1)}, u32[]{:S(2)}, u32[]{:S(2)}) collective-permute-start(f32[128,1024]{1,0:T(8,128)S(1)} %constant_dynamic-slice_fusion.6), channel_id=1, source_target_pairs={{0,2},{2,0},{1,3},{3,1},{4,6},{6,4},{5,7},{7,5},{8,10},{10,8},{9,1... | collective-permute-start | bytes 1572872 | tf_op jit(solution)/shard_map/ppermute | solution.py:55
  158.2 33.1 %collective-permute-start.11 = (f32[128,1024]{1,0:T(8,128)S(1)}, f32[128,1024]{1,0:T(8,128)S(1)}, u32[]{:S(2)}, u32[]{:S(2)}) collective-permute-start(f32[128,1024]{1,0:T(8,128)S(1)} %constant_dynamic-slice_fusion.10), channel_id=1, source_target_pairs={{0,2},{2,0},{1,3},{3,1},{4,6},{6,4},{5,7},{7,5},{8,10},{10,8},{9,1... | collective-permute-start | bytes 1572872 | tf_op jit(solution)/shard_map/ppermute | solution.py:55
  179.5 27.0 %collective-permute-start.15 = (f32[128,1024]{1,0:T(8,128)S(1)}, f32[128,1024]{1,0:T(8,128)S(1)}, u32[]{:S(2)}, u32[]{:S(2)}) collective-permute-start(f32[128,1024]{1,0:T(8,128)S(1)} %constant_dynamic-slice_fusion.8), channel_id=1, source_target_pairs={{0,2},{2,0},{1,3},{3,1},{4,6},{6,4},{5,7},{7,5},{8,10},{10,8},{9,1... | collective-permute-start | bytes 1572872 | tf_op jit(solution)/shard_map/ppermute | solution.py:55
  191.4 62.8 %collective-permute-start.12 = (f32[128,1024]{1,0:T(8,128)S(1)}, f32[128,1024]{1,0:T(8,128)S(1)}, u32[]{:S(2)}, u32[]{:S(2)}) collective-permute-start(f32[128,1024]{1,0:T(8,128)S(1)} %dynamic-slice_add_fusion.7), channel_id=1, source_target_pairs={{0,2},{2,0},{1,3},{3,1},{4,6},{6,4},{5,7},{7,5},{8,10},{10,8},{9,1... | collective-permute-start | bytes 1572872 | tf_op jit(solution)/shard_map/ppermute | solution.py:55
  205.7 49.3 %collective-permute-start.8 = (f32[128,1024]{1,0:T(8,128)S(1)}, f32[128,1024]{1,0:T(8,128)S(1)}, u32[]{:S(2)}, u32[]{:S(2)}) collective-permute-start(f32[128,1024]{1,0:T(8,128)S(1)} %dynamic-slice_add_fusion.8), channel_id=1, source_target_pairs={{0,2},{2,0},{1,3},{3,1},{4,6},{6,4},{5,7},{7,5},{8,10},{10,8},{9,1... | collective-permute-start | bytes 1572872 | tf_op jit(solution)/shard_map/ppermute | solution.py:55
  208.3 36.9 %collective-permute-start.16 = (f32[128,1024]{1,0:T(8,128)S(1)}, f32[128,1024]{1,0:T(8,128)S(1)}, u32[]{:S(2)}, u32[]{:S(2)}) collective-permute-start(f32[128,1024]{1,0:T(8,128)S(1)} %get-tuple-element.80), channel_id=1, source_target_pairs={{0,2},{2,0},{1,3},{3,1},{4,6},{6,4},{5,7},{7,5},{8,10},{10,8},{9,1... | collective-permute-start | bytes 1572872 | tf_op jit(solution)/shard_map/ppermute | solution.py:55
  209.7 44.3 %collective-permute-start.20 = (f32[128,1024]{1,0:T(8,128)S(1)}, f32[128,1024]{1,0:T(8,128)S(1)}, u32[]{:S(2)}, u32[]{:S(2)}) collective-permute-start(f32[128,1024]{1,0:T(8,128)S(1)} %get-tuple-element.81), channel_id=1, source_target_pairs={{0,2},{2,0},{1,3},{3,1},{4,6},{6,4},{5,7},{7,5},{8,10},{10,8},{9,1... | collective-permute-start | bytes 1572872 | tf_op jit(solution)/shard_map/ppermute | solution.py:55
  254.4 40.0 %collective-permute-start.13 = (f32[256,1024]{1,0:T(8,128)S(1)}, f32[256,1024]{1,0:T(8,128)S(1)}, u32[]{:S(2)}, u32[]{:S(2)}) collective-permute-start(f32[256,1024]{1,0:T(8,128)S(1)} %pad_maximum_fusion.9), channel_id=1, source_target_pairs={{0,1},{1,0},{2,3},{3,2},{4,5},{5,4},{6,7},{7,6},{8,9},{9,8},{10,11... | collective-permute-start | bytes 3145736 | tf_op jit(solution)/shard_map/ppermute | solution.py:51
  256.3 47.2 %collective-permute-start.9 = (f32[256,1024]{1,0:T(8,128)}, f32[256,1024]{1,0:T(8,128)}, u32[]{:S(2)}, u32[]{:S(2)}) collective-permute-start(f32[256,1024]{1,0:T(8,128)} %pad_maximum_fusion.8), channel_id=1, source_target_pairs={{0,1},{1,0},{2,3},{3,2},{4,5},{5,4},{6,7},{7,6},{8,9},{9,8},{10,11... | collective-permute-start | bytes 3145736 | tf_op jit(solution)/shard_map/ppermute | solution.py:51
  287.6 58.9 %collective-permute-start.40 = (f32[2,4,16,768]{3,2,1,0:T(8,128)}, f32[2,4,16,768]{3,2,1,0:T(8,128)}, u32[]{:S(2)}, u32[]{:S(2)}) collective-permute-start(f32[2,4,16,768]{3,2,1,0:T(8,128)} %pad_maximum_fusion.16), channel_id=1, source_target_pairs={{0,32},{4,36},{8,40},{12,44},{16,48},{20,52},{24,56},{28,60},{32,6... | collective-permute-start | bytes 1179656 | tf_op jit(solution)/shard_map/ppermute | solution.py:353
  294.4 43.1 %collective-permute-start.34 = (f32[4,2,16,768]{3,2,1,0:T(8,128)}, f32[4,2,16,768]{3,2,1,0:T(8,128)}, u32[]{:S(2)}, u32[]{:S(2)}) collective-permute-start(f32[4,2,16,768]{3,2,1,0:T(8,128)} %pad_maximum_fusion.13), channel_id=1, source_target_pairs={{0,4},{4,8},{8,12},{12,0},{16,20},{20,24},{24,28},{28,16},{32,36},... | collective-permute-start | bytes 1179656 | tf_op jit(solution)/shard_map/ppermute | solution.py:353
  298.1 29.9 %collective-permute-start.23 = (f32[256,1024]{1,0:T(8,128)}, f32[256,1024]{1,0:T(8,128)}, u32[]{:S(2)}, u32[]{:S(2)}) collective-permute-start(f32[256,1024]{1,0:T(8,128)} %constant_dynamic-slice_fusion.4), channel_id=1, source_target_pairs={{0,2},{2,0},{1,3},{3,1},{4,6},{6,4},{5,7},{7,5},{8,10},{10,8},{9,1... | collective-permute-start | bytes 3145736 | tf_op jit(solution)/shard_map/ppermute | solution.py:55
  303.5 34.3 %collective-permute-start.33 = (f32[4,2,16,768]{3,2,1,0:T(8,128)}, f32[4,2,16,768]{3,2,1,0:T(8,128)S(1)}, u32[]{:S(2)}, u32[]{:S(2)}) collective-permute-start(f32[4,2,16,768]{3,2,1,0:T(8,128)} %pad_maximum_fusion.12), channel_id=1, source_target_pairs={{0,8},{4,12},{8,0},{12,4},{16,24},{20,28},{24,16},{28,20},{32,40},... | collective-permute-start | bytes 1179656 | tf_op jit(solution)/shard_map/ppermute | solution.py:353
  337.9 31.3 %collective-permute-start.24 = (f32[256,1024]{1,0:T(8,128)S(1)}, f32[256,1024]{1,0:T(8,128)S(1)}, u32[]{:S(2)}, u32[]{:S(2)}) collective-permute-start(f32[256,1024]{1,0:T(8,128)S(1)} %fusion.17), channel_id=1, source_target_pairs={{0,2},{2,0},{1,3},{3,1},{4,6},{6,4},{5,7},{7,5},{8,10},{10,8},{9,1... | collective-permute-start | bytes 3145736 | tf_op jit(solution)/shard_map/ppermute | solution.py:55
  (73 other events, 866.9 us)

commit v2 on v1

v2 whole, which is shorter than its diff:
```python
import functools

import jax
import jax.numpy as jnp
from jax import lax
from jax.experimental import pallas as pl
from jax.experimental.pallas import tpu as pltpu
from jax.sharding import PartitionSpec as P

BLK = 64
CH = 256
EPS = 1e-6
SCALE = 128 ** -0.5
F32 = jnp.float32
BF16 = jnp.bfloat16
VMEM_BYTES = 63_400_000
BACK_US = 8
FWD_ROWS = 256
BWD_ROWS = 256


def weight(us):
    return pl.CostEstimate(flops=int(us * 1.0e4), bytes_accessed=1024, transcendentals=0)


def nn(a, b, **kw):
    return lax.dot_general(a, b, (((1,), (0,)), ((), ())), preferred_element_type=F32, **kw)


def nt(a, b, **kw):
    return lax.dot_general(a, b, (((1,), (1,)), ((), ())), preferred_element_type=F32, **kw)


def tn(a, b, **kw):
    return lax.dot_general(a, b, (((0,), (0,)), ((), ())), preferred_element_type=F32, **kw)


HIGH = dict(precision=lax.Precision.HIGHEST)


CORE = [(0, 1), (1, 0), (2, 3), (3, 2)]
ZLO = [(0, 2), (2, 0), (1, 3), (3, 1)]


def dp_perm(dy, dz, dx):
    out = []
    for y in range(4):
        for z in range(2):
            for x in range(4):
                out.append(((y * 2 + z) * 4 + x, (((y + dy) % 4) * 2 + (z + dz) % 2) * 4 + (x + dx) % 4))
    return out


XS = {1: dp_perm(0, 0, 1), 3: dp_perm(0, 0, -1), 2: dp_perm(0, 0, 2)}
YS = {1: dp_perm(1, 0, 0), 3: dp_perm(-1, 0, 0), 2: dp_perm(2, 0, 0)}
ZH = dp_perm(0, 1, 0)


def core_swap(v):
    return lax.ppermute(v, "mp", CORE)


def z_swap(v):
    return lax.ppermute(v, "mp", ZLO)


def rows_of(v, start, size):
    return lax.dynamic_slice_in_dim(v, start, size, 0)


def item_starts(len_ref):
    starts, total = [], jnp.int32(0)
    for j in range(8):
        starts.append(total)
        total = total + len_ref[0, j]
    return starts


def start_at(starts, place):
    best = jnp.int32(0)
    for s in starts[1:]:
        best = jnp.where(s <= place, jnp.maximum(best, s), best)
    return best


def chunk_masks(starts, base):
    row = lax.broadcasted_iota(jnp.int32, (CH, CH), 0)
    col = lax.broadcasted_iota(jnp.int32, (CH, CH), 1)
    blk = jnp.bitwise_and(row, -BLK)
    row1 = lax.broadcasted_iota(jnp.int32, (CH, 128), 0)
    place = row1 + base
    low = jnp.zeros_like(place)
    for s in starts[1:]:
        low = jnp.where(place >= s, jnp.maximum(low, s), low)
    low = low - base
    blk1 = jnp.bitwise_and(row1, -BLK)
    carried = low < blk1
    low_wide = jnp.concatenate([low, low], axis=1)
    causal = (col <= row) & (col >= blk)
    visible = causal & (col >= low_wide)
    return visible, carried


def causal_ones():
    row = lax.broadcasted_iota(jnp.int32, (CH, CH), 0)
    col = lax.broadcasted_iota(jnp.int32, (CH, CH), 1)
    return jnp.where((col <= row) & (col >= jnp.bitwise_and(row, -BLK)), 1.0, 0.0).astype(BF16)


def two_parts(v):
    high = v.astype(BF16)
    return high, (v - high.astype(F32)).astype(BF16)


def block_scalars(starts, base, b):
    first = base + b * BLK
    origin = start_at(starts, first + BLK - 1)
    keep = jnp.where(origin < first, 1.0, 0.0).astype(F32)
    place = lax.broadcasted_iota(jnp.int32, (BLK, 128), 0) + first
    return keep, place >= origin


def scaled_parts(q, k, cum):
    last = jnp.broadcast_to(cum.reshape(CH // BLK, BLK, 128)[:, BLK - 1 :, :], (CH // BLK, BLK, 128))
    last = last.reshape(CH, 128)
    e, en, ef = jnp.exp(cum), jnp.exp(-cum), jnp.exp(last - cum)
    qf = q.astype(F32) * SCALE * e
    ks = k.astype(F32) * en
    kf = k.astype(F32) * ef
    return last, e, en, ef, qf, ks, kf


def mixer_forward(
    len_ref, tok_ref, g1_ref, wq_ref, wk_ref, wv_ref, wgd_ref, wgu_ref, bias_ref,
    n_ref, q_ref, k_ref, v_ref, low_ref, logit_ref, cum_ref, mixed_lo_ref, mixed_hi_ref, st_ref, state,
):
    step = pl.program_id(0)
    rows = tok_ref.shape[0]
    starts = item_starts(len_ref)

    @pl.when(step == 0)
    def _():
        state[...] = jnp.zeros_like(state)

    ones = causal_ones()
    s = state[...]
    for c in range(rows // CH):
        base = step * rows + c * CH
        at = slice(c * CH, (c + 1) * CH)
        x = tok_ref[at, :].astype(F32)
        r = lax.rsqrt(jnp.mean(x * x, axis=-1, keepdims=True) + EPS)
        n = (x * r * g1_ref[...]).astype(BF16)
        n_ref[at, :] = n
        low = nt(n, wgd_ref[...]).astype(BF16)
        low_ref[at, :] = low
        logits = nn(low, wgu_ref[...]) + bias_ref[...]
        logit_ref[at, :] = logits
        decays = (jnp.minimum(logits, 0.0) - jnp.log1p(jnp.exp(-jnp.abs(logits)))) * (1.0 / 16.0)
        high, rest = two_parts(decays)
        cum = nn(ones, high) + nn(ones, rest)
        cum_ref[at, :] = cum
        q = nn(n, wq_ref[...]).astype(BF16)
        k = nn(n, wk_ref[...]).astype(BF16)
        v = nn(n, wv_ref[...]).astype(BF16)
        q_ref[at, :] = q
        k_ref[at, :] = k
        v_ref[at, :] = v
        visible, carried = chunk_masks(starts, base)
        last, e, en, ef, qf, ks, kf = scaled_parts(q, k, cum)
        scores = jnp.where(visible, nt(qf.astype(BF16), ks.astype(BF16)), 0.0).astype(BF16)
        out = nn(scores, v)
        q_carried = jnp.where(carried, qf, 0.0).astype(BF16)
        mixed_parts = []
        for b in range(CH // BLK):
            sl = slice(b * BLK, (b + 1) * BLK)
            keep, tail = block_scalars(starts, base, b)
            st_ref[c * (CH // BLK) + b] = s
            inter = nt(q_carried[sl], s.astype(BF16))
            mixed_parts.append((out[sl] + inter).astype(BF16).astype(F32))
            k_tail = jnp.where(tail, kf[sl], 0.0).astype(BF16)
            s = keep * jnp.exp(last[b * BLK : b * BLK + 1]) * s + tn(v[sl], k_tail)
        mixed = jnp.concatenate(mixed_parts, axis=0)

        @pl.when(step < 2)
        def _(mixed=mixed):
            mixed_lo_ref[...] = mixed

        @pl.when(step >= 2)
        def _(mixed=mixed):
            mixed_hi_ref[...] = mixed

    state[...] = s


def run_mixer_forward(lengths, tokens, g1, wq, wk, wv, wgd, wgu, bias):
    t = tokens.shape[0]
    whole = lambda a: pl.BlockSpec(a.shape, lambda i: (0,) * a.ndim)
    rows = lambda c: pl.BlockSpec((CH, c), lambda i: (i, 0))
    nb = CH // BLK
    outs = [
        ((t, 1024), BF16), ((t, 128), BF16), ((t, 128), BF16), ((t, 256), BF16), ((t, 16), BF16), ((t, 128), F32), ((t, 128), F32),
    ]
    sds = jax.ShapeDtypeStruct
    return pl.pallas_call(
        mixer_forward,
        grid=(t // CH,),
        in_specs=[pl.BlockSpec(memory_space=pltpu.SMEM), rows(1024), whole(g1), whole(wq), whole(wk), whole(wv),
                  whole(wgd), whole(wgu), whole(bias)],
        out_specs=[rows(s[1]) for s, _ in outs]
        + [pl.BlockSpec((CH, 256), lambda i: (jnp.minimum(i, 1), 0)), pl.BlockSpec((CH, 256), lambda i: (jnp.maximum(i - 2, 0), 0)),
           pl.BlockSpec((nb, 256, 128), lambda i: (i, 0, 0))],
        out_shape=[sds(s, d) for s, d in outs] + [sds((t // 2, 256), F32)] * 2 + [sds((t // BLK, 256, 128), F32)],
        scratch_shapes=[pltpu.VMEM((256, 128), F32)],
        compiler_params=pltpu.CompilerParams(vmem_limit_bytes=VMEM_BYTES),
        cost_estimate=weight(10),
        name="mixer_forward",
    )(lengths, tokens, g1, wq, wk, wv, wgd, wgu, bias)


def before_feed_kernel(w0_ref, w1_ref, w2_ref, w3_ref, cot_ref, wd_ref, wo_ref, gh_ref):
    for j, w_ref in enumerate((w0_ref, w1_ref, w2_ref, w3_ref)):

        @pl.when(pl.program_id(0) == j)
        def _(w_ref=w_ref):
            wo_ref[...] = w_ref[...].astype(BF16)

    gh_ref[...] = nt(cot_ref[...], wd_ref[...])


def run_before_feed(wo, cot, wd):
    t = cot.shape[0]
    whole = lambda a: pl.BlockSpec(a.shape, lambda s: (0,) * a.ndim)
    rows = lambda c: pl.BlockSpec((CH, c), lambda s: (s, 0))
    return pl.pallas_call(
        before_feed_kernel,
        grid=(t // CH,),
        in_specs=[whole(w) for w in wo] + [rows(1024), whole(wd)],
        out_specs=[rows(1024), rows(704)],
        out_shape=[jax.ShapeDtypeStruct((t, 1024), BF16), jax.ShapeDtypeStruct((t, 704), F32)],
        compiler_params=pltpu.CompilerParams(vmem_limit_bytes=VMEM_BYTES),
        cost_estimate=weight(1),
        name="before_feed",
    )(*wo, cot, wd)


def feed_kernel(
    at_ref, tok_ref, gh_ref, m0_ref, m1_ref, m2_ref, m3_ref, wo_ref, g2_ref, wg_ref, wu_ref, wd_ref,
    mid_ref, n_ref, hid_ref, gg_ref, feed_out_ref, feed_keep_ref, part_out_ref, part_keep_ref,
):
    step = pl.program_id(0)

    mixed = jnp.concatenate([m0_ref[...], m1_ref[...], m2_ref[...], m3_ref[...]], axis=1).astype(BF16)
    mid = tok_ref[...].astype(F32) + nn(mixed, wo_ref[...])
    mid_ref[...] = mid
    r = lax.rsqrt(jnp.mean(mid * mid, axis=-1, keepdims=True) + EPS)
    n = (mid * r * g2_ref[...]).astype(BF16)
    n_ref[...] = n
    pre = nt(n, wg_ref[...])
    up = nt(n, wu_ref[...])
    sg = jax.nn.sigmoid(pre)
    act = pre * sg
    hid = (act * up).astype(BF16)
    hid_ref[...] = hid
    gh = gh_ref[...]
    gg = (gh * up * sg * (1.0 + pre * (1.0 - sg))).astype(BF16)
    gu = (gh * act).astype(BF16)
    gg_ref[:, 0:704] = gg
    gg_ref[:, 704:1408] = gu
    feed = nn(hid, wd_ref[...])
    part = nn(gg, wg_ref[...]) + nn(gu, wu_ref[...])

    @pl.when(step == 0)
    def _():
        feed_out_ref[...] = feed
        part_out_ref[...] = part

    @pl.when(step == 1)
    def _():
        feed_keep_ref[...] = feed
        part_keep_ref[...] = part


def run_feed(at, chunk, tokens, gh, mixed, wo, g2, wg, wu, wd):
    t = tokens.shape[0] // 2
    whole = lambda a: pl.BlockSpec(a.shape, lambda s, at: (0,) * a.ndim)
    half = lambda s, at: jnp.bitwise_xor(1 - at[2], s)
    rows = lambda c: pl.BlockSpec((CH, c), lambda s, at: (half(s, at), 0))
    from_all = lambda c: pl.BlockSpec((CH, c), lambda s, at: (2 * chunk + half(s, at), 0))
    once = pl.BlockSpec((CH, 1024), lambda s, at: (0, 0))
    sds = jax.ShapeDtypeStruct
    return pl.pallas_call(
        feed_kernel,
        grid_spec=pltpu.PrefetchScalarGridSpec(
            num_scalar_prefetch=1,
            grid=(t // CH,),
            in_specs=[from_all(1024), from_all(704)] + [rows(256)] * 4 + [whole(wo), whole(g2), whole(wg), whole(wu), whole(wd)],
            out_specs=[rows(1024), rows(1024), rows(704), rows(1408), once, once, once, once],
        ),
        out_shape=[sds((t, 1024), F32), sds((t, 1024), BF16), sds((t, 704), BF16), sds((t, 1408), BF16)] + [sds((CH, 1024), F32)] * 4,
        compiler_params=pltpu.CompilerParams(vmem_limit_bytes=VMEM_BYTES),
        cost_estimate=weight(10),
        name="feed_both_ways",
    )(at, tokens, gh, *mixed, wo, g2, wg, wu, wd)


def mixer_backward(
    at_ref, len_ref, *refs,
):
    gm_refs, gain_refs, refs = refs[:8], refs[8:10], refs[10:]
    (tok_ref, n_ref, q_ref, k_ref, v_ref, low_ref, logit_ref, cum_ref,
     st_ref, wo_ref, wq_ref, wk_ref, wv_ref, wgd_ref, wgu_ref,
     dqkv_ref, part_out_ref, part_keep_ref, ga_ref, small_ref, gup_ref, bias_ref, dstate) = refs
    step = pl.program_id(0)
    steps = pl.num_programs(0)
    rows = tok_ref.shape[0]
    starts = item_starts(len_ref)

    core, z = at_ref[2], at_ref[3]
    here = steps - 1 - step
    mine = jnp.equal(lax.rem(here, 2), core)

    @pl.when(step == 0)
    def _():
        dstate[...] = jnp.zeros_like(dstate)
        small_ref[...] = jnp.zeros_like(small_ref)
        small_ref[17:18, :] = gain_refs[0][0:1, :] + gain_refs[1][0:1, :]
        gup_ref[...] = jnp.zeros_like(gup_ref)
        bias_ref[...] = jnp.zeros_like(bias_ref)

    first = pl.multiple_of(z * 128, 128)
    second = pl.multiple_of((1 - z) * 128, 128)
    for chunk in range(2):
        for other in range(2):
            wanted = jnp.logical_not(mine) if other else mine

            @pl.when(jnp.logical_and(jnp.equal(lax.div(here, 2), chunk), wanted))
            def _(chunk=chunk, other=other):
                ga_ref[pl.ds(first, 128), :] = gm_refs[4 * chunk + 2 * other][...].astype(BF16)
                ga_ref[pl.ds(second, 128), :] = gm_refs[4 * chunk + 2 * other + 1][...].astype(BF16)

    ones = causal_ones()
    ds = dstate[...]
    for c in reversed(range(rows // CH)):
        base = here * rows + c * CH
        at = slice(c * CH, (c + 1) * CH)
        g = nt(ga_ref[at, :], wo_ref[...]).astype(BF16)
        q, k, v, cum = q_ref[at, :], k_ref[at, :], v_ref[at, :], cum_ref[at, :]
        visible, carried = chunk_masks(starts, base)
        last, e, en, ef, qf, ksf, kff = scaled_parts(q, k, cum)
        qs, ks = qf.astype(BF16), ksf.astype(BF16)
        scores = jnp.where(visible, nt(qs, ks), 0.0).astype(BF16)
        dscores = jnp.where(visible, nt(g, v), 0.0).astype(BF16)
        dv = tn(scores, g)
        dqs = nn(dscores, ks)
        dks = tn(dscores, qs)
        q_carried = jnp.where(carried, qf, 0.0).astype(BF16)
        dvs, dkfs, dqss, dls = [], [], [], []
        for b in reversed(range(CH // BLK)):
            sl = slice(b * BLK, (b + 1) * BLK)
            keep, tail = block_scalars(starts, base, b)
            dsb = ds.astype(BF16)
            s = st_ref[c * (CH // BLK) + b]
            k_tail = jnp.where(tail, kff[sl], 0.0).astype(BF16)
            dvs.append(dv[sl] + nt(k_tail, dsb))
            dkf = jnp.where(tail, nn(v[sl], dsb), 0.0)
            dkfs.append(dkf)
            dqss.append(dqs[sl] + jnp.where(carried[sl], nn(g[sl], s.astype(BF16)), 0.0))
            grow = keep * jnp.exp(last[b * BLK : b * BLK + 1])
            dlast = grow * jnp.sum(s * ds, axis=0, keepdims=True) + jnp.sum(dkf * kff[sl], axis=0, keepdims=True)
            dls.append(jnp.broadcast_to(dlast, (BLK, 128)))
            ds = grow * ds + tn(g[sl], q_carried[sl])
        join = lambda parts: jnp.concatenate(parts[::-1], axis=0)
        dqs, dkf, dl = join(dqss), join(dkfs), join(dls)
        dq = (dqs * (SCALE * e)).astype(BF16)
        dk = (dks * en + dkf * ef).astype(BF16)
        dv = join(dvs).astype(BF16)
        dqkv_ref[at, 0:128] = dq
        dqkv_ref[at, 128:256] = dk
        dqkv_ref[at, 256:512] = dv
        high, rest = two_parts(dqs * qf - dks * ksf - dkf * kff)
        ddec = tn(ones, high) + tn(ones, rest) + dl
        glog = ddec * jax.nn.sigmoid(-logit_ref[at, :]) * (1.0 / 16.0)
        bias_ref[0:1, :] += jnp.sum(glog, axis=0, keepdims=True)
        high, rest = two_parts(glog)
        gup_ref[...] += tn(low_ref[at, :], high) + tn(low_ref[at, :], rest)
        glr = (nt(high, wgu_ref[...]) + nt(rest, wgu_ref[...])).astype(BF16)
        part = nt(dq, wq_ref[...]) + nt(dk, wk_ref[...]) + nt(dv, wv_ref[...]) + nn(glr, wgd_ref[...])
        @pl.when(mine)
        def _(part=part):
            part_keep_ref[...] = part

        @pl.when(jnp.logical_not(mine))
        def _(part=part):
            part_out_ref[...] = part

        small_ref[0:16, :] += tn(glr, n_ref[at, :])
        x = tok_ref[at, :].astype(F32)
        r = lax.rsqrt(jnp.mean(x * x, axis=-1, keepdims=True) + EPS)
        small_ref[16:17, :] += jnp.sum(part * x * r, axis=0, keepdims=True)
    dstate[...] = ds


def run_mixer_backward(at, lengths, gm, gains, tokens, n, q, k, v, low, logits, cum, st, wo, wq, wk, wv, wgd, wgu):
    t = tokens.shape[0]
    steps = t // CH
    whole = lambda a: pl.BlockSpec(a.shape, lambda i, at: (0,) * a.ndim)
    rows = lambda c: pl.BlockSpec((CH, c), lambda i, at: (steps - 1 - i, 0))
    split = pl.BlockSpec((CH, 1024), lambda i, at: (lax.div(steps - 1 - i, 2), 0))
    nb = CH // BLK
    fixed = lambda s: pl.BlockSpec(s, lambda i, at: (0, 0))
    sds = jax.ShapeDtypeStruct
    return pl.pallas_call(
        mixer_backward,
        grid_spec=pltpu.PrefetchScalarGridSpec(
            num_scalar_prefetch=1,
            grid=(steps,),
            in_specs=[pl.BlockSpec(memory_space=pltpu.SMEM)] + [whole(g) for g in (*gm, *gains)]
            + [rows(1024), rows(1024), rows(128), rows(128), rows(256), rows(16), rows(128), rows(128),
               pl.BlockSpec((nb, 256, 128), lambda i, at: (steps - 1 - i, 0, 0)),
               whole(wo), whole(wq), whole(wk), whole(wv), whole(wgd), whole(wgu)],
            out_specs=[rows(512), split, split, rows(1024), fixed((24, 1024)), fixed((16, 128)), fixed((8, 128))],
            scratch_shapes=[pltpu.VMEM((256, 128), F32)],
        ),
        out_shape=[sds((t, 512), BF16), sds((t // 2, 1024), F32), sds((t // 2, 1024), F32), sds((t, 1024), BF16),
                   sds((24, 1024), F32), sds((16, 128), F32), sds((8, 128), F32)],
        compiler_params=pltpu.CompilerParams(vmem_limit_bytes=VMEM_BYTES),
        cost_estimate=weight(BACK_US),
        name="mixer_backward",
    )(at, lengths, *gm, *gains, tokens, n, q, k, v, low, logits, cum, st, wo, wq, wk, wv, wgd, wgu)


SMALL = dict(
    compiler_params=pltpu.CompilerParams(vmem_limit_bytes=VMEM_BYTES),
    cost_estimate=weight(0.1),
)


def add_kernel(at_ref, *refs):
    out_ref = refs[-1]
    n = out_ref.shape[0] // (len(refs) // 2)
    for j in range(len(refs) // 2):
        out_ref[j * n : (j + 1) * n] = refs[2 * j][...] + refs[2 * j + 1][...]


def add_quarter(at, *pairs):
    ops, specs = [], []
    for pair in pairs:
        for j in range(pair[0].shape[0] // 256):
            ops += pair
            specs += [pl.BlockSpec((128, 1024), lambda s, at, j=j: (2 * j + 1 - at[3], 0))] * 2
    n = 64 * len(ops)
    return pl.pallas_call(
        add_kernel,
        grid_spec=pltpu.PrefetchScalarGridSpec(
            num_scalar_prefetch=1, grid=(1,), in_specs=specs, out_specs=pl.BlockSpec((n, 1024), lambda s, at: (0, 0))),
        out_shape=jax.ShapeDtypeStruct((n, 1024), F32),
        name="add_quarter",
        **SMALL,
    )(at, *ops)


def quarter_sum_kernel(at_ref, a0_ref, b0_ref, a1_ref, b1_ref, c_ref, o_ref):
    o_ref[0:128] = a0_ref[...] + b0_ref[...] + c_ref[0:128]
    o_ref[128:256] = a1_ref[...] + b1_ref[...] + c_ref[128:256]


def run_quarter_sum(at, pairs, c):
    of_half = pl.BlockSpec((128, 1024), lambda s, at: (at[3], 0))
    own = pl.BlockSpec((256, 1024), lambda s, at: (0, 0))
    return pl.pallas_call(
        quarter_sum_kernel,
        grid_spec=pltpu.PrefetchScalarGridSpec(
            num_scalar_prefetch=1, grid=(1,), in_specs=[of_half] * 4 + [own], out_specs=own),
        out_shape=jax.ShapeDtypeStruct((256, 1024), F32),
        name="quarter_sum",
        **SMALL,
    )(at, *pairs[0], *pairs[1], c)


def norm_gradient(dn, y, gain):
    r = lax.rsqrt(jnp.mean(y * y, axis=-1, keepdims=True) + EPS)
    gd = dn * gain
    dy = r * gd - (r * r * r) * y * jnp.mean(gd * y, axis=-1, keepdims=True)
    return dy, jnp.sum(dn * y * r, axis=0, keepdims=True)


def second_norm_kernel(at_ref, a_ref, b_ref, c_ref, y_ref, gain_ref, base_ref, o_ref, s_ref):
    dn = a_ref[...] + b_ref[...] + c_ref[...]
    dy, dgain = norm_gradient(dn, y_ref[...], gain_ref[...])
    o_ref[...] = base_ref[...].astype(F32) + dy
    s_ref[0:1, :] = dgain


def run_second_norm(at, chunk, a, b, c, middle, gain, cot):
    of_half = pl.BlockSpec((128, 1024), lambda s, at: (at[3], 0))
    of_chunk = pl.BlockSpec((128, 1024), lambda s, at: (2 * at[2] + at[3], 0))
    of_all = pl.BlockSpec((128, 1024), lambda s, at: (4 * chunk + 2 * at[2] + at[3], 0))
    fixed = lambda s: pl.BlockSpec(s, lambda s, at: (0, 0))
    return pl.pallas_call(
        second_norm_kernel,
        grid_spec=pltpu.PrefetchScalarGridSpec(
            num_scalar_prefetch=1, grid=(1,),
            in_specs=[of_half, of_half, fixed((128, 1024)), of_chunk, fixed((1, 1024)), of_all],
            out_specs=[fixed((128, 1024)), fixed((8, 1024))]),
        out_shape=[jax.ShapeDtypeStruct((128, 1024), F32), jax.ShapeDtypeStruct((8, 1024), F32)],
        name="second_norm_back",
        **SMALL,
    )(at, a, b, c, middle, gain, cot)


def first_norm_kernel(at_ref, a_ref, b_ref, c_ref, y_ref, gain_ref, o_ref):
    o_ref[...] = norm_gradient(a_ref[...] + b_ref[...] + c_ref[...], y_ref[...].astype(F32), gain_ref[...])[0]


def run_first_norm(at, a, b, c, tokens, gain):
    of_half = pl.BlockSpec((128, 1024), lambda s, at: (2 * s + at[3], 0))
    of_all = pl.BlockSpec((128, 1024), lambda s, at: (4 * s + 2 * at[2] + at[3], 0))
    own = pl.BlockSpec((128, 1024), lambda s, at: (s, 0))
    return pl.pallas_call(
        first_norm_kernel,
        grid_spec=pltpu.PrefetchScalarGridSpec(
            num_scalar_prefetch=1, grid=(2,),
            in_specs=[of_half, of_half, own, of_all, pl.BlockSpec((1, 1024), lambda s, at: (0, 0))], out_specs=own),
        out_shape=jax.ShapeDtypeStruct((256, 1024), F32),
        name="first_norm_back",
        **SMALL,
    )(at, a, b, c, tokens, gain)


def join_kernel(at_ref, *refs, pieces):
    step = pl.program_id(0)
    out_ref = refs[-1]
    for chunk in range(2):
        for j in range(2):

            @pl.when(step == chunk * 2 + j)
            def _(j=j, chunk=chunk):
                other = refs[2 + 2 * chunk + j] if pieces else refs[2 + chunk]
                out_ref[...] = (refs[j][...] + other[...]).astype(out_ref.dtype)


def run_join(at, odd, first, second, dtype, into=None):
    pieces = len(second) == 4
    chunk = lambda s: lax.div(s, 2)
    place = lambda s, at: jnp.bitwise_xor(2 * at[2] + at[3], 2 * lax.rem(s, 2) + odd)
    own = pl.BlockSpec((128, 1024), lambda s, at: (chunk(s), 0))
    whole = pl.BlockSpec((128, 1024), lambda s, at: (0, 0))
    low = pl.BlockSpec((128, 1024), lambda s, at: (place(jnp.minimum(s, 1), at), 0))
    high = pl.BlockSpec((128, 1024), lambda s, at: (place(jnp.maximum(s, 2), at), 0))
    placed = pl.BlockSpec((128, 1024), lambda s, at: (4 * chunk(s) + place(s, at), 0))
    more = [] if into is None else [into]
    ops = [*first, *second, *more]
    return pl.pallas_call(
        functools.partial(join_kernel, pieces=pieces),
        grid_spec=pltpu.PrefetchScalarGridSpec(
            num_scalar_prefetch=1, grid=(4,),
            in_specs=[own] * 2 + ([whole] * 4 if pieces else [low, high]) + [pl.BlockSpec(memory_space=pl.ANY)] * len(more),
            out_specs=placed),
        out_shape=jax.ShapeDtypeStruct((1024, 1024), dtype),
        input_output_aliases={len(ops): 0} if more else {},
        name="join_rows",
        **SMALL,
    )(at, *ops)


def feed_grads_kernel(at_ref, *refs):
    (l0_ref, l1_ref, r0_ref, r1_ref, c0_ref, c1_ref, h0_ref, h1_ref), outs = refs[:8], refs[8:]
    step = pl.program_id(0)
    w1 = r0_ref.shape[1]
    first = tn(l0_ref[...], r0_ref[...]) + tn(l1_ref[...], r1_ref[...])
    second = tn(c0_ref[...], h0_ref[...]) + tn(c1_ref[...], h1_ref[...])

    def write(ref, x):
        for zh in range(2):
            row = zh * 128 + x * 32
            ref[0, zh, :, 0:w1] = first[row : row + 32]
            ref[0, zh, :, w1:] = second[row : row + 32]

    for x in range(4):
        offset = lax.rem(x - at_ref[0] + 4, 4)
        for k, ref in ((0, outs[0]), (1, outs[1]), (3, outs[4])):

            @pl.when(offset == k)
            def _(x=x, ref=ref):
                write(ref, x)

        @pl.when(jnp.logical_and(offset == 2, step < 2))
        def _(x=x):
            write(outs[2], x)

        @pl.when(jnp.logical_and(offset == 2, step >= 2))
        def _(x=x):
            write(outs[3], x)


def run_feed_grads(at, n2, gg, cot, hid):
    t = cot.shape[0] // 2
    c = gg[0].shape[1] + hid[0].shape[1]
    cols = lambda j: pl.BlockSpec((t, CH), lambda s, at: (j, s))
    whole = lambda a: pl.BlockSpec(a.shape, lambda s, at: (0, 0))
    along = lambda f: pl.BlockSpec((1, 2, 32, c), lambda s, at: (f(s), 0, 0, 0))
    each = along(lambda s: s)
    return pl.pallas_call(
        feed_grads_kernel,
        grid_spec=pltpu.PrefetchScalarGridSpec(
            num_scalar_prefetch=1, grid=(4,),
            in_specs=[cols(0), cols(0), whole(gg[0]), whole(gg[1]), cols(0), cols(1), whole(hid[0]), whole(hid[1])],
            out_specs=[each, each, along(lambda s: jnp.minimum(s, 1)), along(lambda s: jnp.maximum(s - 2, 0)), each]),
        out_shape=[jax.ShapeDtypeStruct((n, 2, 32, c), F32) for n in (4, 4, 2, 2, 4)],
        compiler_params=pltpu.CompilerParams(vmem_limit_bytes=VMEM_BYTES),
        cost_estimate=weight(1),
        name="feed_weight_grads",
    )(at, n2[0], n2[1], gg[0], gg[1], cot, cot, hid[0], hid[1])


def mixer_grads_kernel(at_ref, l_ref, r0_ref, a0_ref, m0_ref, m1_ref, small_ref, core_ref, far_ref, gup_ref, bias_ref, *outs):
    step = pl.program_id(0)
    w1 = r0_ref.shape[1]

    @pl.when(step < 4)
    def _():
        n = m0_ref.shape[0]
        first = tn(l_ref[...], r0_ref[...])
        second = tn(a0_ref[0:n], m0_ref[...].astype(BF16)) + tn(a0_ref[n:], m1_ref[...].astype(BF16))

        def write(ref, x, to):
            for zh in range(2):
                row = zh * 128 + x * 32
                ref[2 * to + zh, :, 0:w1] = first[row : row + 32]
                ref[2 * to + zh, :, w1:] = second[row : row + 32]

        offset = lax.rem(step - at_ref[1] + 4, 4)
        for k, ref in ((0, outs[0]), (1, outs[1]), (3, outs[4])):

            @pl.when(offset == k)
            def _(ref=ref):
                for x in range(4):
                    write(ref, x, x)

        @pl.when(offset == 2)
        def _():
            for x in range(4):
                write(outs[2 if x < 2 else 3], x, x % 2)

    @pl.when(step == 4)
    def _():
        small = small_ref[...] + core_ref[...] + far_ref[...]
        for out in (outs[0], outs[1], outs[3], outs[4]):
            last = out.shape[0] - 1
            out[last] = jnp.zeros(out.shape[1:], F32)
            out[last, 0:16, :] = small[0:16, 0:768]
            for j in range(3):
                n = min(6, 16 - 6 * j)
                out[last, 16 : 16 + n, 256 * j : 256 * (j + 1)] = small[6 * j : 6 * j + n, 768:1024]
            for j in range(6):
                n = min(3, 16 - 3 * j)
                out[last, 22 : 22 + n, 128 * j : 128 * (j + 1)] = gup_ref[3 * j : 3 * j + n, :]
            out[last, 25:26, :] = small[16:17, 0:768]
            out[last, 26:27, :] = small[17:18, 0:768]
            out[last, 27:28, 0:256] = small[16:17, 768:1024]
            out[last, 27:28, 256:512] = small[17:18, 768:1024]
            out[last, 27:28, 512:640] = bias_ref[0:1, :]


def run_mixer_grads(at, n1, dqkv, ga, mixed, small, gup, bias):
    t, c = n1.shape[0], dqkv.shape[1] + mixed[0].shape[1]
    cols = pl.BlockSpec((t, CH), lambda s, at: (0, jnp.minimum(s, 3)))
    whole = lambda a: pl.BlockSpec(a.shape, lambda s, at: (0, 0))
    rest = [*small, gup, bias]
    counts = [9, 9, 4, 5, 9]
    return pl.pallas_call(
        mixer_grads_kernel,
        grid_spec=pltpu.PrefetchScalarGridSpec(
            num_scalar_prefetch=1, grid=(5,),
            in_specs=[cols, whole(dqkv), cols, whole(mixed[0]), whole(mixed[1])] + [whole(a) for a in rest],
            out_specs=[pl.BlockSpec((n, 32, c), lambda s, at: (0, 0, 0)) for n in counts]),
        out_shape=[jax.ShapeDtypeStruct((n, 32, c), F32) for n in counts],
        compiler_params=pltpu.CompilerParams(vmem_limit_bytes=VMEM_BYTES),
        cost_estimate=weight(1),
        name="mixer_weight_grads",
    )(at, n1, dqkv, ga, mixed[0], mixed[1], *rest)


def unpack_kernel(rows_ref, g1_ref, down_ref, up_ref, bias_ref, g2_ref, q_ref, k_ref, v_ref, o_ref):
    sums = rows_ref[1]
    wide = jnp.concatenate([sums[16:22, 0:256], sums[16:22, 256:512], sums[16:20, 512:768]], axis=0)
    down_ref[...] = jnp.concatenate([sums[0:16], wide], axis=1)
    for j in range(6):
        n = min(3, 16 - 3 * j)
        up_ref[3 * j : 3 * j + n, :] = sums[22 : 22 + n, 128 * j : 128 * (j + 1)]
    g1_ref[:, 0:768] = sums[25:26]
    g1_ref[:, 768:1024] = sums[27:28, 0:256]
    g2_ref[:, 0:768] = sums[26:27]
    g2_ref[:, 768:1024] = sums[27:28, 256:512]
    bias_ref[...] = sums[27:28, 512:640]
    q_ref[...] = rows_ref[0, :, 0:128]
    k_ref[...] = rows_ref[0, :, 128:256]
    v_ref[...] = rows_ref[0, :, 256:512]
    o_ref[...] = rows_ref[0, :, 512:768]


def unpack(rows):
    shapes = [(1, 1024), (16, 1024), (16, 128), (1, 128), (1, 1024), (32, 128), (32, 128), (32, 256), (32, 256)]
    return pl.pallas_call(
        unpack_kernel, out_shape=[jax.ShapeDtypeStruct(s, F32) for s in shapes], name="unpack", **SMALL,
    )(rows)


def after(value, *others):
    return lax.optimization_barrier((value, others))[0]


def send(v, shifts, d):
    return lax.ppermute(v, "dp", shifts[d])


def ring_one(v, shifts):
    return lax.ppermute(v[2], "dp", shifts[1]), lax.ppermute(v[3], "dp", shifts[3])


def ring_add(v, got):
    up, down = got
    return v[1].at[: up.shape[0]].add(up), v[4].at[v[4].shape[0] - down.shape[0] :].add(down)


def ring_two(v, shifts):
    return lax.ppermute(v[0], "dp", shifts[1]), lax.ppermute(v[1], "dp", shifts[3])


def pick(v, i, dim):
    return lax.dynamic_index_in_dim(v, i, dim, False)


def swap_zh(v, zh, dim):
    return pick(v, zh, dim) + lax.ppermute(pick(v, 1 - zh, dim), "dp", ZH)


def local(tokens, lengths, g1, wq, wk, wv, wgd, wgu, bias, wout, g2, wg, wu, wd, cot):
    mp, dp = lax.axis_index("mp"), lax.axis_index("dp")
    core, z = mp % 2, mp // 2
    ix, zh, iy = dp % 4, (dp // 4) % 2, dp // 8
    at = jnp.stack([ix, iy, core, z]).astype(jnp.int32)
    g1r, g2r, biasr = g1.reshape(1, -1), g2.reshape(1, -1), bias.reshape(1, -1)
    wgd_t, wg_t, wu_t = wgd.T, wg.T, wu.T

    with jax.named_scope("out_weights"):
        wide = wout.astype(F32)
        wout_z = z_swap(wide)
        wout_c = core_swap(wide)
    n1, q, k, v, low, logits, cum, mixed_lo, mixed_hi, st = run_mixer_forward(
        lengths, after(tokens, wide), g1r, wq, wk, wv, wgd_t, wgu, biasr)
    mixed = (mixed_lo, mixed_hi)
    with jax.named_scope("mixed_heads"):
        mixed_c = [core_swap(m) for m in mixed]
        wout_cz = core_swap(after(wout_z, mixed_hi))
        mixed_z = [None, z_swap(after(mixed_hi, wout_z))]
        mixed_z[0] = z_swap(after(mixed_lo, wout_z))
    wo, gh = run_before_feed((wout, wout_z, wout_c, wout_cz), cot, wd)

    middle, n2, hid, gg, feed_out, feed_keep, part_out, part_keep = [[None, None] for _ in range(8)]
    part_in, dn2_out, dn2_z, feed_in = [[None, None] for _ in range(4)]
    gm, gains = [None, None], [None, None]

    def feed_half(j, ready):
        with jax.named_scope("mixed_heads"):
            here = after(mixed_z[j], ready)
            pieces = (mixed[j], here, mixed_c[j], core_swap(here))
        (middle[j], n2[j], hid[j], gg[j], feed_out[j], feed_keep[j], part_out[j], part_keep[j]) = run_feed(
            at, j, tokens, gh, pieces, wo, g2r, wg_t, wu_t, wd)

    def norm_sum(j, ready):
        with jax.named_scope("second_norm_sum"):
            part_in[j] = core_swap(after(part_out[j], ready))
            dn2_out[j] = add_quarter(at, (part_keep[j], part_in[j]))
            dn2_z[j] = z_swap(dn2_out[j])

    def norm_join(j, ready):
        with jax.named_scope("second_norm_join"):
            gm0, gains[j] = run_second_norm(at, j, part_keep[j], part_in[j], after(dn2_z[j], ready), middle[j], g2r, cot)
            gm[j] = [gm0, z_swap(gm0), core_swap(gm0), None]

    feed_half(1, gh)
    norm_sum(1, mixed_z[0])
    feed_half(0, dn2_out[1])
    norm_sum(0, dn2_z[1])
    norm_join(1, dn2_out[0])

    a = run_feed_grads(at, *after((n2, gg), gm[1][0]), cot, hid)
    norm_join(0, (a[0], gm[1][1]))
    with jax.named_scope("feed_grads_one"):
        a = after(a, gm[1][1])
        a_on = ring_one(a, XS)

    with jax.named_scope("feed_sum"):
        feed_in = [core_swap(feed_out[j]) for j in range(2)]
        feed_pairs = [(feed_keep[j], feed_in[j]) for j in range(2)]
        feed_z_out = add_quarter(at, *after(feed_pairs, gm[0][0]))
        feed_z = z_swap(after(feed_z_out, gm[0][1]))

    with jax.named_scope("second_norm_join"):
        for j in range(2):
            gm[j][3] = core_swap(after(gm[j][1], (gm[0][1], feed_z_out, a_on)))

    dqkv, part1_out, part1_keep, ga, small, gup, gbias = run_mixer_backward(
        at, lengths, gm[0] + gm[1], gains, tokens, n1, q, k, v, low, logits, cum, st, wout, wq, wk, wv, wgd_t, wgu)

    with jax.named_scope("first_norm_sum"):
        part1_in = core_swap(after(part1_out, feed_z))
    with jax.named_scope("small_sums"):
        small_core = core_swap(small)
        small_far = z_swap(small + small_core)
    with jax.named_scope("feed_grads_one"):
        a_on = ring_add(a, after(a_on, part1_out))
    with jax.named_scope("first_norm_sum"):
        dn1_out = add_quarter(at, after((part1_keep, part1_in), a_on))
        dn1_z = z_swap(dn1_out)
    with jax.named_scope("feed_grads_one"):
        a_in = ring_two(a_on, XS)

    c = run_mixer_grads(at, n1, dqkv, ga, after(mixed, dn1_out), (small, small_core, small_far), gup, gbias)
    with jax.named_scope("mixer_grads_one"):
        c_on = ring_one(c, YS)

    with jax.named_scope("feed_join"):
        feed_own = run_quarter_sum(at, feed_pairs, after(feed_z, c))
        feed1 = z_swap(after(feed_own, dn1_z))
        feed2 = core_swap(feed_own)

    with jax.named_scope("mixer_grads_one"):
        c_on = ring_add(c, after(c_on, feed_own))
        c_in = ring_two(c_on, YS)

    with jax.named_scope("first_norm_join"):
        dx0 = run_first_norm(at, part1_keep, part1_in, after(dn1_z, c_on), tokens, g1r)
        dx1 = z_swap(after(dx0, feed1))
        dx2 = core_swap(dx0)

    def across(v, at_here, shifts, take):
        return take(v, at_here) + send(take(v, (at_here + 1) % 4), shifts, 1) + send(take(v, (at_here + 3) % 4), shifts, 3) \
            + send(take(v, (at_here + 2) % 4), shifts, 2)

    with jax.named_scope("mixer_grads_two"):
        c, c_in = after((c, c_in), dx0)
        c = c_sum = c[0] + c_in[0] + c_in[1]

        def with_small(v, i):
            return jnp.concatenate([lax.dynamic_slice_in_dim(v, 2 * i, 2, 0), v[8:9]], axis=0)

        c = across(c, ix, XS, with_small)

    with jax.named_scope("feed_grads_two"):
        a, a_in = after((a, a_in), c_sum)
        a = a_sum = a[0] + a_in[0] + a_in[1]
        a = across(a, iy, YS, lambda v, i: pick(v, i, 0))

    with jax.named_scope("first_norm_join"):
        grad_tokens = run_join(at, 0, after((dx0, dx2), a_sum), (gm[0][0], gm[0][2], gm[1][0], gm[1][2]), F32)

    with jax.named_scope("mixer_grads_two"):
        c = after(c, grad_tokens)
        turned = lambda i: jnp.stack([pick(c, i, 0), c[2]])
        rows = turned(zh) + lax.ppermute(turned(1 - zh), "dp", ZH)

    with jax.named_scope("feed_join"):
        result = run_join(at, 0, (feed_own, feed2), after(middle, c), BF16)

    with jax.named_scope("feed_grads_two"):
        mlp_rows = swap_zh(after(a, result), zh, 0)

    with jax.named_scope("feed_join"):
        feed3 = core_swap(after(feed1, a))
        result = run_join(at, 1, (feed1, feed3), middle, BF16, result)

    with jax.named_scope("small_sums"):
        gain_one, gate_down, gate_up, gate_bias, gain_two, d_query, d_key, d_value, d_out = unpack(rows)

    with jax.named_scope("first_norm_join"):
        dx3 = core_swap(dx1)
        grad_tokens = run_join(at, 1, (dx1, dx3), (gm[0][1], gm[0][3], gm[1][1], gm[1][3]), F32, grad_tokens)

    return (
        result,
        grad_tokens,
        gain_one.reshape(1024),
        d_query,
        d_key,
        d_value,
        gate_down.T,
        gate_up,
        gate_bias.reshape(128),
        d_out.T,
        gain_two.reshape(1024),
        mlp_rows[:, 0:704],
        mlp_rows[:, 704:1408],
        mlp_rows[:, 1408:2112].T,
    )


def solution(mesh):
    placed = (
        P("dp", None), P("dp", None), P(), P(None, "mp"), P(None, "mp"), P(None, "mp"), P(), P(None, "mp"),
        P("mp"), P("mp", None), P(), P(None, "mp"), P(None, "mp"), P("mp", None), P("dp", None),
    )
    outs = (
        P("dp", None), P("dp", None), P(), P("dp", "mp"), P("dp", "mp"), P("dp", "mp"), P(), P(None, "mp"),
        P("mp"), P("mp", "dp"), P(), P("dp", "mp"), P("dp", "mp"), P("mp", "dp"),
    )
    return jax.shard_map(local, mesh=mesh, in_specs=placed, out_specs=outs, check_vma=False)
```

time: 402 us -> 317 us (0.79)
  Pallas kernels: 57.2 us -> 132 us
  waiting for transfers between devices: 166 us -> 102 us
  starting transfers between devices: 91.6 us -> 37.9 us
  matrix products: 14 us -> 0 us
  other arithmetic: 33.7 us -> 20.9 us
  local copies, waits for them, and re-layouts: 32.9 us -> 22.2 us
    pallas_call x3 -> x19, Pallas kernels: 44.6 us -> 120 us  [the longest x2 28.2 us: run_feed(): pl.pallas_call(feed_kernel, grid_spec=pltpu.PrefetchScalarGridSpec(num_sc...]
    ppermute x13 -> x12, waiting for transfers between devices: 98.7 us -> 40.2 us  [z_swap(): return lax.ppermute(v, 'mp', ZLO)]
    ppermute x31 -> x16, starting transfers between devices: 73.2 us -> 19.2 us  [the longest x2 4.79 us: ring_one(): lax.ppermute(v[3], 'dp', shifts[3])]
    ppermute x31 -> x16, waiting for transfers between devices: 67.4 us -> 52.2 us  [the longest x6 22.2 us: send(): return lax.ppermute(v, 'dp', shifts[d])]
    dot_general x4 -> x0, matrix products: 14 us -> none  [tn(): lax.dot_general(a, b, (((0,), (0,)), ((), ())), preferred_element_type=F3...]
    concatenate x20 -> x1, other arithmetic: 10 us -> 0.07 us  [with_small(): jnp.concatenate([lax.dynamic_slice_in_dim(v, 2 * i, 2, 0), v[8:9]], axis=0)]
    ppermute x15 -> x20, waiting for transfers between devices: 0.28 us -> 9.38 us  [core_swap(): return lax.ppermute(v, 'mp', CORE)]
    squeeze x45 -> x2, local copies, waits for them, and re-layouts: 9.21 us -> 1.24 us  [pick(): return lax.dynamic_index_in_dim(v, i, dim, False)]
  transfers between devices with their start and end apart: 59 -> 48, of which waited for: 22 -> 22; matrix products, arithmetic and copies ran while one was open for 13% -> 8% of each run, Pallas kernels for 7% -> 36%
where the time goes in v2:
time: 317 us; the launch traced here: 315 us
  Pallas kernels  132 us (42%)
  waiting for transfers between devices  102 us (32%)
  starting transfers between devices  37.9 us (12%)
  local copies, waits for them, and re-layouts  22.2 us (7%)
  other arithmetic  20.9 us (7%)
    ppermute x12, waiting for transfers between devices, z_swap(): return lax.ppermute(v, 'mp', ZLO)  40.2 us
    pallas_call x2, Pallas kernels, run_feed(): pl.pallas_call(feed_kernel, grid_spec=pltpu.PrefetchScalarGridSpec(num_sc...  28.2 us
    ppermute x6, waiting for transfers between devices, send(): return lax.ppermute(v, 'dp', shifts[d])  22.2 us
    pallas_call x4, Pallas kernels, run_join(): pl.pallas_call(functools.partial(join_kernel, pieces=pieces), grid_spec=p...  20.3 us
    unnamed x80, local copies, waits for them, and re-layouts  19.4 us
    pallas_call x1, Pallas kernels, run_mixer_backward(): pl.pallas_call(mixer_backward, grid_spec=pltpu.PrefetchScalarGridSpec(num...  16.9 us
    ppermute x12, starting transfers between devices, z_swap(): return lax.ppermute(v, 'mp', ZLO)  15.3 us
    ppermute x2, waiting for transfers between devices, ring_two(): lax.ppermute(v[1], 'dp', shifts[3])  12.9 us
  transfers between devices with their start and end apart: 48, of which 22 were waited for; matrix products, arithmetic and copies ran while one was open for 8% of the time, Pallas kernels for 36%

profile of v2, /device:TPU:0, one launch (start us, length us, event | category | flops | bytes accessed | tf_op | source)
XLA Modules:
  0.0 315.3 jit_solution(12876154776576907240)
XLA Ops:
  4.8 11.4 %mixer_forward.1 = (bf16[1024,1024]{1,0:T(8,128)(2,1)}, bf16[1024,128]{1,0:T(8,128)(2,1)}, bf16[1024,128]{1,0:T(8,128)(2,1)}, bf16[1024,256]{1,0:T(8,128)(2,1)},...) custom-call(s32[1,8]{1,0:T(1,128)} %len_ref.3, ...), custom_call_target="tpu_custom_call" | custom-call | flops 100000 | bytes 1024 | tf_op jit(solution)/shard_map/mixer_forward/pallas_call | solution.py:204
  16.2 12.0 %collective-permute-done.w1_ref = f32[256,1024]{1,0:T(8,128)S(1)} collective-permute-done((f32[256,1024]{1,0:T(8,128)}, f32[256,1024]{1,0:T(8,128)S(1)}, u32[]{:S(2)}, u32[]{:S(2)}) %collective-permute-start) | collective-permute-done | bytes 1048608 | tf_op jit(solution)/shard_map/out_weights/ppermute | solution.py:64
  31.1 7.0 %before_feed.1 = (bf16[1024,1024]{1,0:T(8,128)(2,1)}, f32[1024,704]{1,0:T(8,128)}) custom-call(bf16[256,1024]{1,0:T(8,128)(2,1)} %refs_19_.1, f32[256,1024]{1,0:T(8,128)} %copy-done.21, f32[256,1024]{1,0:T(8,128)} %copy-done.22, f32[256,1024]{1,0:T(8,128)} %collective-permute-done.2.w3_ref, bf16[1024,1024]{1,0:T(8,128)(2,1)} %base_ref.3, ...), custom_call_target="tpu_custom_call" | custom-call | flops 10000 | bytes 1024 | tf_op jit(solution)/shard_map/before_feed/pallas_call | solution.py:234
  38.1 4.6 %collective-permute-done.4.m1_ref = f32[512,256]{1,0:T(8,128)S(1)} collective-permute-done((f32[512,256]{1,0:T(8,128)}, f32[512,256]{1,0:T(8,128)S(1)}, u32[]{:S(2)}, u32[]{:S(2)}) %collective-permute-start.4) | collective-permute-done | bytes 524320 | tf_op jit(solution)/shard_map/mixed_heads/ppermute | solution.py:64
  46.0 14.1 %feed_both_ways.2 = (f32[512,1024]{1,0:T(8,128)}, bf16[512,1024]{1,0:T(8,128)(2,1)}, bf16[512,704]{1,0:T(8,128)(2,1)}, bf16[512,1408]{1,0:T(8,128)(2,1)}, f32[25...) custom-call(s32[4]{0:T(128)} %pad_add_fusion.at_ref, ...), custom_call_target="tpu_custom_call" | custom-call | flops 100000 | bytes 1024 | tf_op jit(solution)/shard_map/feed_both_ways/pallas_call | solution.py:291
  69.9 14.2 %feed_both_ways.3 = (f32[512,1024]{1,0:T(8,128)}, bf16[512,1024]{1,0:T(8,128)(2,1)}, bf16[512,704]{1,0:T(8,128)(2,1)}, bf16[512,1408]{1,0:T(8,128)(2,1)}, f32[25...) custom-call(s32[4]{0:T(128)} %pad_add_fusion.at_ref, ...), custom_call_target="tpu_custom_call" | custom-call | flops 100000 | bytes 1024 | tf_op jit(solution)/shard_map/feed_both_ways/pallas_call | solution.py:291
  96.6 12.0 %feed_weight_grads.1 = (f32[4,2,32,2112]{3,2,1,0:T(8,128)}, f32[4,2,32,2112]{3,2,1,0:T(8,128)}, f32[2,2,32,2112]{3,2,1,0:T(8,128)}, f32[2,2,32,2112]{3,2,1,0:T(8,128)}, f32[4,2,32,2112]{3,2,1,0:T(8,128)}) custom-call(s32[4]{0:T(128)} %pad_add_fusion.at_ref, bf16[512,1024]{1,0:T(8,128)(2,1)} %get-tuple-element.199.refs_0_, ...), custom_call_target="tpu_custom_call" | custom-call | flops 10000 | bytes 1024 | tf_op jit(solution)/shard_map/feed_weight_grads/pallas_call | solution.py:603
  112.2 7.2 %collective-permute-done.14.c_ref = f32[128,1024]{1,0:T(8,128)S(1)} collective-permute-done((f32[128,1024]{1,0:T(8,128)}, f32[128,1024]{1,0:T(8,128)S(1)}, u32[]{:S(2)}, u32[]{:S(2)}) %collective-permute-start.14) | collective-permute-done | bytes 524320 | tf_op jit(solution)/shard_map/second_norm_sum/ppermute | solution.py:64
  129.2 7.9 %collective-permute-done.16.refs_1_.refs_2_ = f32[128,1024]{1,0:T(8,128)S(1)} collective-permute-done((f32[128,1024]{1,0:T(8,128)}, f32[128,1024]{1,0:T(8,128)S(1)}, u32[]{:S(2)}, u32[]{:S(2)}) %collective-permute-start.16) | collective-permute-done | bytes 524320 | tf_op jit(solution)/shard_map/second_norm_join/ppermute | solution.py:64
  143.0 16.9 %mixer_backward.1 = (bf16[1024,512]{1,0:T(8,128)(2,1)}, f32[512,1024]{1,0:T(8,128)}, f32[512,1024]{1,0:T(8,128)}, bf16[1024,1024]{1,0:T(8,128)(2,1)}, f32[24,102...) custom-call(s32[4]{0:T(128)} %pad_add_fusion.at_ref, s32[1,8]{1,0:T(1,128)} %len_ref.3, ...), custom_call_target="tpu_custom_call" | custom-call | flops 80000 | bytes 1024 | tf_op jit(solution)/shard_map/mixer_backward/pallas_call | solution.py:412
  174.9 8.0 %mixer_weight_grads.1 = (f32[9,32,768]{2,1,0:T(8,128)}, f32[9,32,768]{2,1,0:T(8,128)}, f32[4,32,768]{2,1,0:T(8,128)}, f32[5,32,768]{2,1,0:T(8,128)}, f32[9,32,768]{2,1,0:T(8,128)}) custom-call(s32[4]{0:T(128)} %pad_add_fusion.at_ref, bf16[1024,1024]{1,0:T(8,128)(2,1)} %get-tuple-element.214.refs_11_.l_ref, bf16[1024,512]{1,0:T(8,128)(2,1)} %get-tuple-element.232.r0_ref, ...), custom_call_target="tpu_custom_call" | custom-call | flops 10000 | bytes 1024 | tf_op jit(solution)/shard_map/mixer_weight_grads/pallas_call | solution.py:671
  192.8 3.7 %quarter_sum.1.refs_0_ = f32[256,1024]{1,0:T(8,128)} custom-call(s32[4]{0:T(128)} %pad_add_fusion.at_ref, f32[256,1024]{1,0:T(8,128)} %get-tuple-element.209.refs_0_.a0_ref, f32[256,1024]{1,0:T(8,128)} %copy-done.8, f32[256,1024]{1,0:T(8,128)} %get-tuple-element.211.refs_2_.a1_ref, f32[256,1024]{1,0:T(8,128)} %copy-done.7, ...), custom_call_target="tpu_custom_call" | custom-call | flops 1000 | bytes 1024 | tf_op jit(solution)/shard_map/feed_join/quarter_sum/pallas_call | solution.py:470
  196.5 4.2 %collective-permute-done.31 = f32[4,32,768]{2,1,0:T(8,128)} collective-permute-done((f32[4,32,768]{2,1,0:T(8,128)}, f32[4,32,768]{2,1,0:T(8,128)}, u32[]{:S(2)}, u32[]{:S(2)}) %collective-permute-start.31) | collective-permute-done | bytes 393248 | tf_op jit(solution)/shard_map/mixer_grads_one/ppermute | solution.py:718
  206.8 6.9 %collective-permute-done.27.c_ref = f32[256,1024]{1,0:T(8,128)} collective-permute-done((f32[256,1024]{1,0:T(8,128)}, f32[256,1024]{1,0:T(8,128)}, u32[]{:S(2)}, u32[]{:S(2)}) %collective-permute-start.27) | collective-permute-done | bytes 1048608 | tf_op jit(solution)/shard_map/first_norm_sum/ppermute | solution.py:64
  214.8 3.7 %first_norm_back.1.refs_0_ = f32[256,1024]{1,0:T(8,128)} custom-call(s32[4]{0:T(128)} %pad_add_fusion.at_ref, f32[512,1024]{1,0:T(8,128)} %get-tuple-element.241.refs_0_.refs_2_.a_ref, f32[512,1024]{1,0:T(8,128)} %copy-done, f32[256,1024]{1,0:T(8,128)} %collective-permute-done.27.c_ref, bf16[1024,1024]{1,0:T(8,128)(2,1)} %y_ref.1, f32[1,1024]{1,0:T(1,128)} %bitcast.44), custom_call_target="tpu_custom_call" | custom-call | flops 1000 | bytes 1024 | tf_op jit(solution)/shard_map/first_norm_join/first_norm_back/pallas_call | solution.py:519
  218.5 5.0 %collective-permute-done.34 = f32[9,32,768]{2,1,0:T(8,128)} collective-permute-done((f32[9,32,768]{2,1,0:T(8,128)}, f32[9,32,768]{2,1,0:T(8,128)}, u32[]{:S(2)}, u32[]{:S(2)}) %collective-permute-start.34) | collective-permute-done | bytes 884768 | tf_op jit(solution)/shard_map/mixer_grads_one/ppermute | solution.py:727
  228.8 7.9 %collective-permute-done.30 = f32[4,2,32,2112]{3,2,1,0:T(8,128)} collective-permute-done((f32[4,2,32,2112]{3,2,1,0:T(8,128)}, f32[4,2,32,2112]{3,2,1,0:T(8,128)}, u32[]{:S(2)}, u32[]{:S(2)}) %collective-permute-start.30) | collective-permute-done | bytes 2162720 | tf_op jit(solution)/shard_map/feed_grads_one/ppermute | solution.py:727
  247.9 8.1 %collective-permute-done.40 = f32[3,32,768]{2,1,0:T(8,128)S(1)} collective-permute-done((f32[3,32,768]{2,1,0:T(8,128)S(1)}, f32[3,32,768]{2,1,0:T(8,128)S(1)}, u32[]{:S(2)}, u32[]{:S(2)}) %collective-permute-start.40) | collective-permute-done | bytes 294944 | tf_op jit(solution)/shard_map/mixer_grads_two/ppermute | solution.py:714
  260.1 14.0 %collective-permute-done.35 = f32[2,32,2112]{2,1,0:T(8,128)} collective-permute-done((f32[2,32,2112]{2,1,0:T(8,128)}, f32[2,32,2112]{2,1,0:T(8,128)}, u32[]{:S(2)}, u32[]{:S(2)}) %collective-permute-start.35) | collective-permute-done | bytes 540704 | tf_op jit(solution)/shard_map/feed_grads_two/ppermute | solution.py:714
  277.5 5.2 %join_rows.4.refs_6_ = f32[1024,1024]{1,0:T(8,128)} custom-call(s32[4]{0:T(128)} %pad_add_fusion.at_ref, f32[256,1024]{1,0:T(8,128)} %first_norm_back.1.refs_0_, f32[256,1024]{1,0:T(8,128)} %collective-permute-done.43.refs_1_, f32[128,1024]{1,0:T(8,128)} %get-tuple-element.208.refs_0_.refs_2_, f32[128,1024]{1,0:T(8,128)} %copy-done.17, ...), custom_call_target="tpu_custom_call" | custom-call | flops 1000 | bytes 1024 | tf_op jit(solution)/shard_map/first_norm_join/join_rows/pallas_call | solution.py:553
  282.7 5.0 %join_rows.5.refs_4_ = bf16[1024,1024]{1,0:T(8,128)(2,1)} custom-call(s32[4]{0:T(128)} %pad_add_fusion.at_ref, f32[256,1024]{1,0:T(8,128)} %quarter_sum.1.refs_0_, f32[256,1024]{1,0:T(8,128)} %collective-permute-done.39.refs_1_, f32[512,1024]{1,0:T(8,128)} %get-tuple-element.269.y_ref.refs_2_, f32[512,1024]{1,0:T(8,128)} %get-tuple-element.270.y_ref.refs_3_), custom_call_target="tpu_custom_call" | custom-call | flops 1000 | bytes 1024 | tf_op jit(solution)/shard_map/feed_join/join_rows/pallas_call | solution.py:553
  292.8 6.3 %collective-permute-done.46 = f32[2,32,768]{2,1,0:T(8,128)} collective-permute-done((f32[2,32,768]{2,1,0:T(8,128)}, f32[2,32,768]{2,1,0:T(8,128)}, u32[]{:S(2)}, u32[]{:S(2)}) %collective-permute-start.46) | collective-permute-done | bytes 196640 | tf_op jit(solution)/shard_map/mixer_grads_two/ppermute | solution.py:862
  304.2 4.8 %join_rows.6 = bf16[1024,1024]{1,0:T(8,128)(2,1)} custom-call(s32[4]{0:T(128)} %pad_add_fusion.at_ref, f32[256,1024]{1,0:T(8,128)} %collective-permute-done.28.refs_0_, f32[256,1024]{1,0:T(8,128)} %copy-done.23, f32[512,1024]{1,0:T(8,128)} %get-tuple-element.269.y_ref.refs_2_, ...), custom_call_target="tpu_custom_call", output_to_operand_aliasing={{}: (5, {})} | custom-call | flops 1000 | bytes 1024 | tf_op jit(solution)/shard_map/feed_join/join_rows/pallas_call | solution.py:553
  310.0 5.2 %join_rows.7 = f32[1024,1024]{1,0:T(8,128)} custom-call(s32[4]{0:T(128)} %pad_add_fusion.at_ref, f32[256,1024]{1,0:T(8,128)} %collective-permute-done.44.refs_0_, f32[256,1024]{1,0:T(8,128)} %copy-done.20, f32[128,1024]{1,0:T(8,128)} %copy-done.13, f32[128,1024]{1,0:T(8,128)} %copy-done.15, f32[128,1024]{1,0:T(8,128)} %copy-done.12, ...), custom_call_target="tpu_custom_call", output_to_operand_aliasing={{}: (7, {})} | custom-call | flops 1000 | bytes 1024 | tf_op jit(solution)/shard_map/first_norm_join/join_rows/pallas_call | solution.py:553
  (193 shorter events, 118.8 us)
Async XLA Ops:
  2.8 25.4 %collective-permute-start = (f32[256,1024]{1,0:T(8,128)}, f32[256,1024]{1,0:T(8,128)S(1)}, u32[]{:S(2)}, u32[]{:S(2)}) collective-permute-start(f32[256,1024]{1,0:T(8,128)} %convert_element_type.3), channel_id=1, source_target_pairs={{0,2},{2,0},{1,3},{3,1},{4,6},{6,4},{5,7},{7,5},{8,10},{10,8},{9,1... | collective-permute-start | bytes 3145736 | tf_op jit(solution)/shard_map/out_weights/ppermute | solution.py:64
  4.8 25.4 %collective-permute-start.1 = (f32[256,1024]{1,0:T(8,128)}, f32[256,1024]{1,0:T(8,128)S(1)}, u32[]{:S(2)}, u32[]{:S(2)}) collective-permute-start(f32[256,1024]{1,0:T(8,128)} %convert_element_type.3), channel_id=1, source_target_pairs={{0,1},{1,0},{2,3},{3,2},{4,5},{5,4},{6,7},{7,6},{8,9},{9,8},{10,11... | collective-permute-start | bytes 3145736 | tf_op jit(solution)/shard_map/out_weights/ppermute | solution.py:60
  42.7 17.4 %collective-permute-start.3 = (f32[512,256]{1,0:T(8,128)S(1)}, f32[512,256]{1,0:T(8,128)S(1)}, u32[]{:S(2)}, u32[]{:S(2)}) collective-permute-start(f32[512,256]{1,0:T(8,128)S(1)} %copy-done.18), channel_id=1, source_target_pairs={{0,2},{2,0},{1,3},{3,1},{4,6},{6,4},{5,7},{7,5},{8,10},{10,8},{9,1... | collective-permute-start | bytes 1572872 | tf_op jit(solution)/shard_map/mixed_heads/ppermute | solution.py:64
  66.9 17.2 %collective-permute-start.12 = (f32[128,1024]{1,0:T(8,128)}, f32[128,1024]{1,0:T(8,128)S(1)}, u32[]{:S(2)}, u32[]{:S(2)}) collective-permute-start(f32[128,1024]{1,0:T(8,128)} %add_quarter.4), channel_id=1, source_target_pairs={{0,2},{2,0},{1,3},{3,1},{4,6},{6,4},{5,7},{7,5},{8,10},{10,8},{9,1... | collective-permute-start | bytes 1572872 | tf_op jit(solution)/shard_map/second_norm_sum/ppermute | solution.py:64
  95.0 29.6 %collective-permute-start.11 = (f32[256,1024]{1,0:T(8,128)}, f32[256,1024]{1,0:T(8,128)S(1)}, u32[]{:S(2)}, u32[]{:S(2)}) collective-permute-start(f32[256,1024]{1,0:T(8,128)} %get-tuple-element.188), channel_id=1, source_target_pairs={{0,1},{1,0},{2,3},{3,2},{4,5},{5,4},{6,7},{7,6},{8,9},{9,8},{10,11... | collective-permute-start | bytes 3145736 | tf_op jit(solution)/shard_map/feed_sum/ppermute | solution.py:60
  95.0 29.6 %collective-permute-start.10 = (f32[256,1024]{1,0:T(8,128)}, f32[256,1024]{1,0:T(8,128)S(1)}, u32[]{:S(2)}, u32[]{:S(2)}) collective-permute-start(f32[256,1024]{1,0:T(8,128)} %get-tuple-element.186), channel_id=1, source_target_pairs={{0,1},{1,0},{2,3},{3,2},{4,5},{5,4},{6,7},{7,6},{8,9},{9,8},{10,11... | collective-permute-start | bytes 3145736 | tf_op jit(solution)/shard_map/feed_sum/ppermute | solution.py:60
  95.5 23.9 %collective-permute-start.14 = (f32[128,1024]{1,0:T(8,128)}, f32[128,1024]{1,0:T(8,128)S(1)}, u32[]{:S(2)}, u32[]{:S(2)}) collective-permute-start(f32[128,1024]{1,0:T(8,128)} %add_quarter.5), channel_id=1, source_target_pairs={{0,2},{2,0},{1,3},{3,1},{4,6},{6,4},{5,7},{7,5},{8,10},{10,8},{9,1... | collective-permute-start | bytes 1572872 | tf_op jit(solution)/shard_map/second_norm_sum/ppermute | solution.py:64
  109.0 29.5 %collective-permute-start.19 = (f32[2,2,32,2112]{3,2,1,0:T(8,128)}, f32[2,2,32,2112]{3,2,1,0:T(8,128)}, u32[]{:S(2)}, u32[]{:S(2)}) collective-permute-start(f32[2,2,32,2112]{3,2,1,0:T(8,128)} %get-tuple-element.219), channel_id=1, source_target_pairs={{0,4},{4,8},{8,12},{12,0},{16,20},{20,24},{24,28},{28,16},{32,36},... | collective-permute-start | bytes 3244040 | tf_op jit(solution)/shard_map/feed_grads_one/ppermute | solution.py:718
  110.4 28.1 %collective-permute-start.20 = (f32[2,2,32,2112]{3,2,1,0:T(8,128)}, f32[2,2,32,2112]{3,2,1,0:T(8,128)}, u32[]{:S(2)}, u32[]{:S(2)}) collective-permute-start(f32[2,2,32,2112]{3,2,1,0:T(8,128)} %get-tuple-element.220), channel_id=1, source_target_pairs={{0,12},{4,0},{8,4},{12,8},{16,28},{20,16},{24,20},{28,24},{32,44},... | collective-permute-start | bytes 3244040 | tf_op jit(solution)/shard_map/feed_grads_one/ppermute | solution.py:718
  137.0 24.0 %collective-permute-start.17 = (f32[256,1024]{1,0:T(8,128)}, f32[256,1024]{1,0:T(8,128)}, u32[]{:S(2)}, u32[]{:S(2)}) collective-permute-start(f32[256,1024]{1,0:T(8,128)} %add_quarter.6), channel_id=1, source_target_pairs={{0,2},{2,0},{1,3},{3,1},{4,6},{6,4},{5,7},{7,5},{8,10},{10,8},{9,1... | collective-permute-start | bytes 3145736 | tf_op jit(solution)/shard_map/feed_sum/ppermute | solution.py:64
  182.9 17.9 %collective-permute-start.32 = (f32[5,32,768]{2,1,0:T(8,128)}, f32[5,32,768]{2,1,0:T(8,128)}, u32[]{:S(2)}, u32[]{:S(2)}) collective-permute-start(f32[5,32,768]{2,1,0:T(8,128)} %get-tuple-element.251), channel_id=1, source_target_pairs={{0,96},{4,100},{8,104},{12,108},{16,112},{20,116},{24,120},{28,124... | collective-permute-start | bytes 1474568 | tf_op jit(solution)/shard_map/mixer_grads_one/ppermute | solution.py:718
  185.9 50.8 %collective-permute-start.30 = (f32[4,2,32,2112]{3,2,1,0:T(8,128)}, f32[4,2,32,2112]{3,2,1,0:T(8,128)}, u32[]{:S(2)}, u32[]{:S(2)}) collective-permute-start(f32[4,2,32,2112]{3,2,1,0:T(8,128)} %copy-done.3), channel_id=1, source_target_pairs={{0,12},{4,0},{8,4},{12,8},{16,28},{20,16},{24,20},{28,24},{32,44},... | collective-permute-start | bytes 6488072 | tf_op jit(solution)/shard_map/feed_grads_one/ppermute | solution.py:727
  188.6 51.3 %collective-permute-start.29 = (f32[4,2,32,2112]{3,2,1,0:T(8,128)S(1)}, f32[4,2,32,2112]{3,2,1,0:T(8,128)}, u32[]{:S(2)}, u32[]{:S(2)}) collective-permute-start(f32[4,2,32,2112]{3,2,1,0:T(8,128)S(1)} %copy-done.2), channel_id=1, source_target_pairs={{0,4},{4,8},{8,12},{12,0},{16,20},{20,24},{24,28},{28,16},{32,36},... | collective-permute-start | bytes 6488072 | tf_op jit(solution)/shard_map/feed_grads_one/ppermute | solution.py:727
  188.6 25.1 %collective-permute-start.27 = (f32[256,1024]{1,0:T(8,128)}, f32[256,1024]{1,0:T(8,128)}, u32[]{:S(2)}, u32[]{:S(2)}) collective-permute-start(f32[256,1024]{1,0:T(8,128)} %add_quarter.7), channel_id=1, source_target_pairs={{0,2},{2,0},{1,3},{3,1},{4,6},{6,4},{5,7},{7,5},{8,10},{10,8},{9,1... | collective-permute-start | bytes 3145736 | tf_op jit(solution)/shard_map/first_norm_sum/ppermute | solution.py:64
  202.8 20.6 %collective-permute-start.34 = (f32[9,32,768]{2,1,0:T(8,128)}, f32[9,32,768]{2,1,0:T(8,128)}, u32[]{:S(2)}, u32[]{:S(2)}) collective-permute-start(f32[9,32,768]{2,1,0:T(8,128)} %add_dynamic-update-slice_fusion.2), channel_id=1, source_target_pairs={{0,96},{4,100},{8,104},{12,108},{16,112},{20,116},{24,120},{28,124... | collective-permute-start | bytes 2654216 | tf_op jit(solution)/shard_map/mixer_grads_one/ppermute | solution.py:727
  204.7 22.2 %collective-permute-start.33 = (f32[9,32,768]{2,1,0:T(8,128)}, f32[9,32,768]{2,1,0:T(8,128)}, u32[]{:S(2)}, u32[]{:S(2)}) collective-permute-start(f32[9,32,768]{2,1,0:T(8,128)} %add_dynamic-update-slice_fusion.3), channel_id=1, source_target_pairs={{0,32},{4,36},{8,40},{12,44},{16,48},{20,52},{24,56},{28,60},{32,6... | collective-permute-start | bytes 2654216 | tf_op jit(solution)/shard_map/mixer_grads_one/ppermute | solution.py:727
  213.7 43.5 %collective-permute-start.28 = (f32[256,1024]{1,0:T(8,128)S(1)}, f32[256,1024]{1,0:T(8,128)}, u32[]{:S(2)}, u32[]{:S(2)}) collective-permute-start(f32[256,1024]{1,0:T(8,128)S(1)} %copy-done.4), channel_id=1, source_target_pairs={{0,2},{2,0},{1,3},{3,1},{4,6},{6,4},{5,7},{7,5},{8,10},{10,8},{9,1... | collective-permute-start | bytes 3145736 | tf_op jit(solution)/shard_map/feed_join/ppermute | solution.py:64
  247.9 26.2 %collective-permute-start.35 = (f32[2,32,2112]{2,1,0:T(8,128)}, f32[2,32,2112]{2,1,0:T(8,128)}, u32[]{:S(2)}, u32[]{:S(2)}) collective-permute-start(f32[2,32,2112]{2,1,0:T(8,128)} %get-tuple-element.282), channel_id=1, source_target_pairs={{0,32},{4,36},{8,40},{12,44},{16,48},{20,52},{24,56},{28,60},{32,6... | collective-permute-start | bytes 1622024 | tf_op jit(solution)/shard_map/feed_grads_two/ppermute | solution.py:714
  256.0 19.1 %collective-permute-start.36 = (f32[2,32,2112]{2,1,0:T(8,128)}, f32[2,32,2112]{2,1,0:T(8,128)}, u32[]{:S(2)}, u32[]{:S(2)}) collective-permute-start(f32[2,32,2112]{2,1,0:T(8,128)} %get-tuple-element.284), channel_id=1, source_target_pairs={{0,96},{4,100},{8,104},{12,108},{16,112},{20,116},{24,120},{28,124... | collective-permute-start | bytes 1622024 | tf_op jit(solution)/shard_map/feed_grads_two/ppermute | solution.py:714
  256.8 18.4 %collective-permute-start.37 = (f32[2,32,2112]{2,1,0:T(8,128)}, f32[2,32,2112]{2,1,0:T(8,128)}, u32[]{:S(2)}, u32[]{:S(2)}) collective-permute-start(f32[2,32,2112]{2,1,0:T(8,128)} %get-tuple-element.283), channel_id=1, source_target_pairs={{0,64},{4,68},{8,72},{12,76},{16,80},{20,84},{24,88},{28,92},{32,9... | collective-permute-start | bytes 1622024 | tf_op jit(solution)/shard_map/feed_grads_two/ppermute | solution.py:714
  257.2 20.2 %collective-permute-start.43 = (f32[256,1024]{1,0:T(8,128)}, f32[256,1024]{1,0:T(8,128)}, u32[]{:S(2)}, u32[]{:S(2)}) collective-permute-start(f32[256,1024]{1,0:T(8,128)} %first_norm_back.1.refs_0_), channel_id=1, source_target_pairs={{0,1},{1,0},{2,3},{3,2},{4,5},{5,4},{6,7},{7,6},{8,9},{9,8},{10,11... | collective-permute-start | bytes 3145736 | tf_op jit(solution)/shard_map/first_norm_join/ppermute | solution.py:60
  258.0 24.7 %collective-permute-start.39 = (f32[256,1024]{1,0:T(8,128)S(1)}, f32[256,1024]{1,0:T(8,128)}, u32[]{:S(2)}, u32[]{:S(2)}) collective-permute-start(f32[256,1024]{1,0:T(8,128)S(1)} %copy-done.4), channel_id=1, source_target_pairs={{0,1},{1,0},{2,3},{3,2},{4,5},{5,4},{6,7},{7,6},{8,9},{9,8},{10,11... | collective-permute-start | bytes 3145736 | tf_op jit(solution)/shard_map/feed_join/ppermute | solution.py:60
  274.1 18.2 %collective-permute-start.44 = (f32[256,1024]{1,0:T(8,128)}, f32[256,1024]{1,0:T(8,128)}, u32[]{:S(2)}, u32[]{:S(2)}) collective-permute-start(f32[256,1024]{1,0:T(8,128)} %first_norm_back.1.refs_0_), channel_id=1, source_target_pairs={{0,2},{2,0},{1,3},{3,1},{4,6},{6,4},{5,7},{7,5},{8,10},{10,8},{9,1... | collective-permute-start | bytes 3145736 | tf_op jit(solution)/shard_map/first_norm_join/ppermute | solution.py:64
  292.3 16.7 %collective-permute-start.45 = (f32[256,1024]{1,0:T(8,128)}, f32[256,1024]{1,0:T(8,128)S(1)}, u32[]{:S(2)}, u32[]{:S(2)}) collective-permute-start(f32[256,1024]{1,0:T(8,128)} %collective-permute-done.44.refs_0_), channel_id=1, source_target_pairs={{0,1},{1,0},{2,3},{3,2},{4,5},{5,4},{6,7},{7,6},{8,9},{9,8},{10,11... | collective-permute-start | bytes 3145736 | tf_op jit(solution)/shard_map/first_norm_join/ppermute | solution.py:60
  (62 other events, 372.1 us)

commit v3 on v2

--- a/solution.py
+++ b/solution.py
@@ -14,13 +14,13 @@
 F32 = jnp.float32
 BF16 = jnp.bfloat16
 VMEM_BYTES = 63_400_000
-BACK_US = 8
+BACK_US = 16
 FWD_ROWS = 256
 BWD_ROWS = 256
 
 
 def weight(us):
-    return pl.CostEstimate(flops=int(us * 1.0e4), bytes_accessed=1024, transcendentals=0)
+    return pl.CostEstimate(flops=int(us * 1.0e9), bytes_accessed=1024, transcendentals=0)
 
 
 def nn(a, b, **kw):
@@ -54,6 +54,8 @@
 XS = {1: dp_perm(0, 0, 1), 3: dp_perm(0, 0, -1), 2: dp_perm(0, 0, 2)}
 YS = {1: dp_perm(1, 0, 0), 3: dp_perm(-1, 0, 0), 2: dp_perm(2, 0, 0)}
 ZH = dp_perm(0, 1, 0)
+Y_PAIR = [((y * 2 + z) * 4 + x, ((y ^ 1) * 2 + z) * 4 + x) for y in range(4) for z in range(2) for x in range(4)]
+X_PAIR = [((y * 2 + z) * 4 + x, (y * 2 + z) * 4 + (x ^ 1)) for y in range(4) for z in range(2) for x in range(4)]
 
 
 def core_swap(v):
@@ -238,7 +240,7 @@
         out_specs=[rows(1024), rows(704)],
         out_shape=[jax.ShapeDtypeStruct((t, 1024), BF16), jax.ShapeDtypeStruct((t, 704), F32)],
         compiler_params=pltpu.CompilerParams(vmem_limit_bytes=VMEM_BYTES),
-        cost_estimate=weight(1),
+        cost_estimate=weight(7),
         name="before_feed",
     )(*wo, cot, wd)
 
@@ -298,7 +300,7 @@
         ),
         out_shape=[sds((t, 1024), F32), sds((t, 1024), BF16), sds((t, 704), BF16), sds((t, 1408), BF16)] + [sds((CH, 1024), F32)] * 4,
         compiler_params=pltpu.CompilerParams(vmem_limit_bytes=VMEM_BYTES),
-        cost_estimate=weight(10),
+        cost_estimate=weight(14),
         name="feed_both_ways",
     )(at, tokens, gh, *mixed, wo, g2, wg, wu, wd)
 
@@ -306,10 +308,10 @@
 def mixer_backward(
     at_ref, len_ref, *refs,
 ):
-    gm_refs, gain_refs, refs = refs[:8], refs[8:10], refs[10:]
+    gm_refs, gain_ref, refs = refs[:4], refs[4], refs[5:]
     (tok_ref, n_ref, q_ref, k_ref, v_ref, low_ref, logit_ref, cum_ref,
      st_ref, wo_ref, wq_ref, wk_ref, wv_ref, wgd_ref, wgu_ref,
-     dqkv_ref, part_out_ref, part_keep_ref, ga_ref, small_ref, gup_ref, bias_ref, dstate) = refs
+     dqkv_ref, far0_ref, far1_ref, near0_ref, near1_ref, part_keep_ref, ga_ref, small_ref, gup_ref, bias_ref, dstate, whole) = refs
     step = pl.program_id(0)
     steps = pl.num_programs(0)
     rows = tok_ref.shape[0]
@@ -323,20 +325,18 @@
     def _():
         dstate[...] = jnp.zeros_like(dstate)
         small_ref[...] = jnp.zeros_like(small_ref)
-        small_ref[17:18, :] = gain_refs[0][0:1, :] + gain_refs[1][0:1, :]
+        small_ref[17:18, :] = gain_ref[0:1, :]
         gup_ref[...] = jnp.zeros_like(gup_ref)
         bias_ref[...] = jnp.zeros_like(bias_ref)
 
     first = pl.multiple_of(z * 128, 128)
     second = pl.multiple_of((1 - z) * 128, 128)
-    for chunk in range(2):
-        for other in range(2):
-            wanted = jnp.logical_not(mine) if other else mine
-
-            @pl.when(jnp.logical_and(jnp.equal(lax.div(here, 2), chunk), wanted))
-            def _(chunk=chunk, other=other):
-                ga_ref[pl.ds(first, 128), :] = gm_refs[4 * chunk + 2 * other][...].astype(BF16)
-                ga_ref[pl.ds(second, 128), :] = gm_refs[4 * chunk + 2 * other + 1][...].astype(BF16)
+    for other in range(2):
+
+        @pl.when(jnp.logical_not(mine) if other else mine)
+        def _(other=other):
+            ga_ref[pl.ds(first, 128), :] = gm_refs[2 * other][...].astype(BF16)
+            ga_ref[pl.ds(second, 128), :] = gm_refs[2 * other + 1][...].astype(BF16)
 
     ones = causal_ones()
     ds = dstate[...]
@@ -389,9 +389,13 @@
         def _(part=part):
             part_keep_ref[...] = part
 
-        @pl.when(jnp.logical_not(mine))
-        def _(part=part):
-            part_out_ref[...] = part
+        for chunk, (far_ref, near_ref) in enumerate(((far0_ref, near0_ref), (far1_ref, near1_ref))):
+
+            @pl.when(jnp.logical_and(jnp.logical_not(mine), jnp.equal(lax.div(here, 2), chunk)))
+            def _(part=part, far_ref=far_ref, near_ref=near_ref):
+                whole[...] = part
+                far_ref[...] = whole[pl.ds(second, 128), :]
+                near_ref[...] = whole[pl.ds(first, 128), :]
 
         small_ref[0:16, :] += tn(glr, n_ref[at, :])
         x = tok_ref[at, :].astype(F32)
@@ -400,7 +404,7 @@
     dstate[...] = ds
 
 
-def run_mixer_backward(at, lengths, gm, gains, tokens, n, q, k, v, low, logits, cum, st, wo, wq, wk, wv, wgd, wgu):
+def run_mixer_backward(at, lengths, gm, gain, tokens, n, q, k, v, low, logits, cum, st, wo, wq, wk, wv, wgd, wgu):
     t = tokens.shape[0]
     steps = t // CH
     whole = lambda a: pl.BlockSpec(a.shape, lambda i, at: (0,) * a.ndim)
@@ -414,24 +418,24 @@
         grid_spec=pltpu.PrefetchScalarGridSpec(
             num_scalar_prefetch=1,
             grid=(steps,),
-            in_specs=[pl.BlockSpec(memory_space=pltpu.SMEM)] + [whole(g) for g in (*gm, *gains)]
+            in_specs=[pl.BlockSpec(memory_space=pltpu.SMEM)] + [pl.BlockSpec((128, 1024), lambda i, at: (lax.div(steps - 1 - i, 2), 0))] * 4 + [whole(gain)]
             + [rows(1024), rows(1024), rows(128), rows(128), rows(256), rows(16), rows(128), rows(128),
                pl.BlockSpec((nb, 256, 128), lambda i, at: (steps - 1 - i, 0, 0)),
                whole(wo), whole(wq), whole(wk), whole(wv), whole(wgd), whole(wgu)],
-            out_specs=[rows(512), split, split, rows(1024), fixed((24, 1024)), fixed((16, 128)), fixed((8, 128))],
-            scratch_shapes=[pltpu.VMEM((256, 128), F32)],
+            out_specs=[rows(512)] + [fixed((128, 1024))] * 4 + [split, rows(1024), fixed((24, 1024)), fixed((16, 128)), fixed((8, 128))],
+            scratch_shapes=[pltpu.VMEM((256, 128), F32), pltpu.VMEM((CH, 1024), F32)],
         ),
-        out_shape=[sds((t, 512), BF16), sds((t // 2, 1024), F32), sds((t // 2, 1024), F32), sds((t, 1024), BF16),
+        out_shape=[sds((t, 512), BF16)] + [sds((128, 1024), F32)] * 4 + [sds((t // 2, 1024), F32), sds((t, 1024), BF16),
                    sds((24, 1024), F32), sds((16, 128), F32), sds((8, 128), F32)],
         compiler_params=pltpu.CompilerParams(vmem_limit_bytes=VMEM_BYTES),
         cost_estimate=weight(BACK_US),
         name="mixer_backward",
-    )(at, lengths, *gm, *gains, tokens, n, q, k, v, low, logits, cum, st, wo, wq, wk, wv, wgd, wgu)
+    )(at, lengths, *gm, gain, tokens, n, q, k, v, low, logits, cum, st, wo, wq, wk, wv, wgd, wgu)
 
 
 SMALL = dict(
     compiler_params=pltpu.CompilerParams(vmem_limit_bytes=VMEM_BYTES),
-    cost_estimate=weight(0.1),
+    cost_estimate=weight(3),
 )
 
 
@@ -459,22 +463,23 @@
     )(at, *ops)
 
 
-def quarter_sum_kernel(at_ref, a0_ref, b0_ref, a1_ref, b1_ref, c_ref, o_ref):
-    o_ref[0:128] = a0_ref[...] + b0_ref[...] + c_ref[0:128]
-    o_ref[128:256] = a1_ref[...] + b1_ref[...] + c_ref[128:256]
-
-
-def run_quarter_sum(at, pairs, c):
+def quarter_sum_kernel(at_ref, a0_ref, b0_ref, y0_ref, a1_ref, b1_ref, y1_ref, c_ref, o_ref):
+    o_ref[0:128] = a0_ref[...] + b0_ref[...] + c_ref[0:128] + y0_ref[...]
+    o_ref[128:256] = a1_ref[...] + b1_ref[...] + c_ref[128:256] + y1_ref[...]
+
+
+def run_quarter_sum(at, keep, got, far, middle):
     of_half = pl.BlockSpec((128, 1024), lambda s, at: (at[3], 0))
+    of_chunk = pl.BlockSpec((128, 1024), lambda s, at: (2 * at[2] + at[3], 0))
     own = pl.BlockSpec((256, 1024), lambda s, at: (0, 0))
     return pl.pallas_call(
         quarter_sum_kernel,
         grid_spec=pltpu.PrefetchScalarGridSpec(
-            num_scalar_prefetch=1, grid=(1,), in_specs=[of_half] * 4 + [own], out_specs=own),
+            num_scalar_prefetch=1, grid=(1,), in_specs=[of_half, of_half, of_chunk] * 2 + [own], out_specs=own),
         out_shape=jax.ShapeDtypeStruct((256, 1024), F32),
         name="quarter_sum",
         **SMALL,
-    )(at, *pairs[0], *pairs[1], c)
+    )(at, keep[0], got[0], middle[0], keep[1], got[1], middle[1], far)
 
 
 def norm_gradient(dn, y, gain):
@@ -484,136 +489,146 @@
     return dy, jnp.sum(dn * y * r, axis=0, keepdims=True)
 
 
-def second_norm_kernel(at_ref, a_ref, b_ref, c_ref, y_ref, gain_ref, base_ref, o_ref, s_ref):
-    dn = a_ref[...] + b_ref[...] + c_ref[...]
-    dy, dgain = norm_gradient(dn, y_ref[...], gain_ref[...])
-    o_ref[...] = base_ref[...].astype(F32) + dy
-    s_ref[0:1, :] = dgain
-
-
-def run_second_norm(at, chunk, a, b, c, middle, gain, cot):
+def second_norm_kernel(at_ref, a0_ref, b0_ref, c0_ref, y0_ref, a1_ref, b1_ref, c1_ref, y1_ref, gain_ref, base0_ref, base1_ref, o_ref, s_ref):
+    halves = ((a0_ref, b0_ref, c0_ref, y0_ref, base0_ref), (a1_ref, b1_ref, c1_ref, y1_ref, base1_ref))
+    total = jnp.zeros((1, 1024), F32)
+    for j, (a_ref, b_ref, c_ref, y_ref, base_ref) in enumerate(halves):
+        dy, dgain = norm_gradient(a_ref[...] + b_ref[...] + c_ref[...], y_ref[...], gain_ref[...])
+        o_ref[128 * j : 128 * (j + 1)] = base_ref[...].astype(F32) + dy
+        total = total + dgain
+    s_ref[0:1, :] = total
+
+
+def run_second_norm(at, keep, got, far, middle, gain, cot):
     of_half = pl.BlockSpec((128, 1024), lambda s, at: (at[3], 0))
     of_chunk = pl.BlockSpec((128, 1024), lambda s, at: (2 * at[2] + at[3], 0))
-    of_all = pl.BlockSpec((128, 1024), lambda s, at: (4 * chunk + 2 * at[2] + at[3], 0))
-    fixed = lambda s: pl.BlockSpec(s, lambda s, at: (0, 0))
+    of_all = lambda j: pl.BlockSpec((128, 1024), lambda s, at: (4 * j + 2 * at[2] + at[3], 0))
+    fixed = lambda *s: pl.BlockSpec(s, lambda s, at: (0, 0))
+    ops = [v for j in range(2) for v in (keep[j], got[j], far[j], middle[j])]
     return pl.pallas_call(
         second_norm_kernel,
         grid_spec=pltpu.PrefetchScalarGridSpec(
             num_scalar_prefetch=1, grid=(1,),
-            in_specs=[of_half, of_half, fixed((128, 1024)), of_chunk, fixed((1, 1024)), of_all],
-            out_specs=[fixed((128, 1024)), fixed((8, 1024))]),
-        out_shape=[jax.ShapeDtypeStruct((128, 1024), F32), jax.ShapeDtypeStruct((8, 1024), F32)],
+            in_specs=[of_half, of_half, fixed(128, 1024), of_chunk] * 2 + [fixed(1, 1024), of_all(0), of_all(1)],
+            out_specs=[fixed(256, 1024), fixed(8, 1024)]),
+        out_shape=[jax.ShapeDtypeStruct((256, 1024), F32), jax.ShapeDtypeStruct((8, 1024), F32)],
         name="second_norm_back",
         **SMALL,
-    )(at, a, b, c, middle, gain, cot)
-
-
-def first_norm_kernel(at_ref, a_ref, b_ref, c_ref, y_ref, gain_ref, o_ref):
-    o_ref[...] = norm_gradient(a_ref[...] + b_ref[...] + c_ref[...], y_ref[...].astype(F32), gain_ref[...])[0]
-
-
-def run_first_norm(at, a, b, c, tokens, gain):
+    )(at, *ops, gain, cot, cot)
+
+
+def far_sum_kernel(at_ref, keep_ref, got0_ref, got1_ref, o_ref):
+    for j, got_ref in enumerate((got0_ref, got1_ref)):
+
+        @pl.when(pl.program_id(0) == j)
+        def _(got_ref=got_ref):
+            o_ref[...] = keep_ref[...] + got_ref[...]
+
+
+def run_far_sum(at, keep, got):
+    fixed = pl.BlockSpec((128, 1024), lambda s, at: (0, 0))
+    return pl.pallas_call(
+        far_sum_kernel,
+        grid_spec=pltpu.PrefetchScalarGridSpec(
+            num_scalar_prefetch=1, grid=(2,), in_specs=[pl.BlockSpec((128, 1024), lambda s, at: (2 * s + 1 - at[3], 0)), fixed, fixed],
+            out_specs=pl.BlockSpec((128, 1024), lambda s, at: (s, 0))),
+        out_shape=jax.ShapeDtypeStruct((256, 1024), F32),
+        name="far_sum",
+        **SMALL,
+    )(at, keep, *got)
+
+
+def first_norm_kernel(at_ref, a_ref, b0_ref, b1_ref, c_ref, y_ref, base_ref, gain_ref, own_ref):
+    for j, b_ref in enumerate((b0_ref, b1_ref)):
+
+        @pl.when(pl.program_id(0) == j)
+        def _(b_ref=b_ref):
+            dy, _ = norm_gradient(a_ref[...] + b_ref[...] + c_ref[...], y_ref[...].astype(F32), gain_ref[...])
+            own_ref[...] = dy + base_ref[...]
+
+
+def run_first_norm(at, keep, got, far, tokens, base, gain):
     of_half = pl.BlockSpec((128, 1024), lambda s, at: (2 * s + at[3], 0))
     of_all = pl.BlockSpec((128, 1024), lambda s, at: (4 * s + 2 * at[2] + at[3], 0))
     own = pl.BlockSpec((128, 1024), lambda s, at: (s, 0))
+    fixed = lambda *n: pl.BlockSpec(n, lambda s, at: (0, 0))
     return pl.pallas_call(
         first_norm_kernel,
         grid_spec=pltpu.PrefetchScalarGridSpec(
             num_scalar_prefetch=1, grid=(2,),
-            in_specs=[of_half, of_half, own, of_all, pl.BlockSpec((1, 1024), lambda s, at: (0, 0))], out_specs=own),
+            in_specs=[of_half, fixed(128, 1024), fixed(128, 1024), own, of_all, own, fixed(1, 1024)], out_specs=own),
         out_shape=jax.ShapeDtypeStruct((256, 1024), F32),
         name="first_norm_back",
         **SMALL,
-    )(at, a, b, c, tokens, gain)
-
-
-def join_kernel(at_ref, *refs, pieces):
-    step = pl.program_id(0)
-    out_ref = refs[-1]
-    for chunk in range(2):
-        for j in range(2):
-
-            @pl.when(step == chunk * 2 + j)
-            def _(j=j, chunk=chunk):
-                other = refs[2 + 2 * chunk + j] if pieces else refs[2 + chunk]
-                out_ref[...] = (refs[j][...] + other[...]).astype(out_ref.dtype)
-
-
-def run_join(at, odd, first, second, dtype, into=None):
-    pieces = len(second) == 4
+    )(at, keep, *got, far, tokens, base, gain)
+
+
+def place_kernel(at_ref, r0_ref, g0_ref, r1_ref, g1_ref, *rest):
+    result_ref, grad_ref = rest[-2:]
+
+    @pl.when(lax.rem(pl.program_id(0), 2) == 0)
+    def _():
+        result_ref[...] = r0_ref[...].astype(BF16)
+        grad_ref[...] = g0_ref[...]
+
+    @pl.when(lax.rem(pl.program_id(0), 2) == 1)
+    def _():
+        result_ref[...] = r1_ref[...].astype(BF16)
+        grad_ref[...] = g1_ref[...]
+
+
+def run_place(at, odd, pieces, into=()):
     chunk = lambda s: lax.div(s, 2)
     place = lambda s, at: jnp.bitwise_xor(2 * at[2] + at[3], 2 * lax.rem(s, 2) + odd)
-    own = pl.BlockSpec((128, 1024), lambda s, at: (chunk(s), 0))
-    whole = pl.BlockSpec((128, 1024), lambda s, at: (0, 0))
-    low = pl.BlockSpec((128, 1024), lambda s, at: (place(jnp.minimum(s, 1), at), 0))
-    high = pl.BlockSpec((128, 1024), lambda s, at: (place(jnp.maximum(s, 2), at), 0))
+    piece = pl.BlockSpec((128, 1024), lambda s, at: (chunk(s), 0))
     placed = pl.BlockSpec((128, 1024), lambda s, at: (4 * chunk(s) + place(s, at), 0))
-    more = [] if into is None else [into]
-    ops = [*first, *second, *more]
-    return pl.pallas_call(
-        functools.partial(join_kernel, pieces=pieces),
+    return pl.pallas_call(
+        place_kernel,
         grid_spec=pltpu.PrefetchScalarGridSpec(
             num_scalar_prefetch=1, grid=(4,),
-            in_specs=[own] * 2 + ([whole] * 4 if pieces else [low, high]) + [pl.BlockSpec(memory_space=pl.ANY)] * len(more),
-            out_specs=placed),
-        out_shape=jax.ShapeDtypeStruct((1024, 1024), dtype),
-        input_output_aliases={len(ops): 0} if more else {},
-        name="join_rows",
+            in_specs=[piece] * 4 + [pl.BlockSpec(memory_space=pl.ANY)] * len(into),
+            out_specs=[placed, placed]),
+        out_shape=[jax.ShapeDtypeStruct((1024, 1024), BF16), jax.ShapeDtypeStruct((1024, 1024), F32)],
+        input_output_aliases={5: 0, 6: 1} if into else {},
+        name="place_rows",
         **SMALL,
-    )(at, *ops)
-
-
-def feed_grads_kernel(at_ref, *refs):
-    (l0_ref, l1_ref, r0_ref, r1_ref, c0_ref, c1_ref, h0_ref, h1_ref), outs = refs[:8], refs[8:]
-    step = pl.program_id(0)
-    w1 = r0_ref.shape[1]
+    )(at, *pieces, *into)
+
+
+def feed_grads_kernel(l0_ref, l1_ref, r0_ref, r1_ref, c0_ref, c1_ref, h0_ref, h1_ref, out):
+    w1, w2 = r0_ref.shape[1], h0_ref.shape[1]
     first = tn(l0_ref[...], r0_ref[...]) + tn(l1_ref[...], r1_ref[...])
     second = tn(c0_ref[...], h0_ref[...]) + tn(c1_ref[...], h1_ref[...])
-
-    def write(ref, x):
+    for x in range(4):
         for zh in range(2):
             row = zh * 128 + x * 32
-            ref[0, zh, :, 0:w1] = first[row : row + 32]
-            ref[0, zh, :, w1:] = second[row : row + 32]
-
-    for x in range(4):
-        offset = lax.rem(x - at_ref[0] + 4, 4)
-        for k, ref in ((0, outs[0]), (1, outs[1]), (3, outs[4])):
-
-            @pl.when(offset == k)
-            def _(x=x, ref=ref):
-                write(ref, x)
-
-        @pl.when(jnp.logical_and(offset == 2, step < 2))
-        def _(x=x):
-            write(outs[2], x)
-
-        @pl.when(jnp.logical_and(offset == 2, step >= 2))
-        def _(x=x):
-            write(outs[3], x)
-
-
-def run_feed_grads(at, n2, gg, cot, hid):
+            out[x, 0, zh, :, 0:w1] = first[row : row + 32]
+            out[x, 0, zh, :, w1 : w1 + w2] = second[row : row + 32]
+            out[x, 0, zh, :, w1 + w2 :] = jnp.zeros((32, out.shape[-1] - w1 - w2), F32)
+
+
+def run_feed_grads(n2, gg, cot, hid):
     t = cot.shape[0] // 2
     c = gg[0].shape[1] + hid[0].shape[1]
-    cols = lambda j: pl.BlockSpec((t, CH), lambda s, at: (j, s))
-    whole = lambda a: pl.BlockSpec(a.shape, lambda s, at: (0, 0))
-    along = lambda f: pl.BlockSpec((1, 2, 32, c), lambda s, at: (f(s), 0, 0, 0))
-    each = along(lambda s: s)
+    wide = -(-c // 128) * 128
+    cols = lambda j: pl.BlockSpec((t, CH), lambda s: (j, s))
+    whole = lambda a: pl.BlockSpec(a.shape, lambda s: (0, 0))
     return pl.pallas_call(
         feed_grads_kernel,
-        grid_spec=pltpu.PrefetchScalarGridSpec(
-            num_scalar_prefetch=1, grid=(4,),
-            in_specs=[cols(0), cols(0), whole(gg[0]), whole(gg[1]), cols(0), cols(1), whole(hid[0]), whole(hid[1])],
-            out_specs=[each, each, along(lambda s: jnp.minimum(s, 1)), along(lambda s: jnp.maximum(s - 2, 0)), each]),
-        out_shape=[jax.ShapeDtypeStruct((n, 2, 32, c), F32) for n in (4, 4, 2, 2, 4)],
+        grid=(4,),
+        in_specs=[cols(0), cols(0), whole(gg[0]), whole(gg[1]), cols(0), cols(1), whole(hid[0]), whole(hid[1])],
+        out_specs=pl.BlockSpec((4, 1, 2, 32, wide), lambda s: (0, s, 0, 0, 0)),
+        out_shape=jax.ShapeDtypeStruct((4, 4, 2, 32, wide), F32),
         compiler_params=pltpu.CompilerParams(vmem_limit_bytes=VMEM_BYTES),
-        cost_estimate=weight(1),
+        cost_estimate=weight(12),
         name="feed_weight_grads",
-    )(at, n2[0], n2[1], gg[0], gg[1], cot, cot, hid[0], hid[1])
-
-
-def mixer_grads_kernel(at_ref, l_ref, r0_ref, a0_ref, m0_ref, m1_ref, small_ref, core_ref, far_ref, gup_ref, bias_ref, *outs):
+    )(n2[0], n2[1], gg[0], gg[1], cot, cot, hid[0], hid[1])
+
+
+RING_OUTS = ((0, None, 0), (2, 0, 1), (1, 1, 1), (3, 0, 2), (2, 1, 2), (1, 0, 3), (3, 1, 4))
+
+
+def mixer_grads_kernel(at_ref, l_ref, r0_ref, a0_ref, m0_ref, m1_ref, small_ref, gup_ref, bias_ref, *outs):
     step = pl.program_id(0)
     w1 = r0_ref.shape[1]
 
@@ -630,22 +645,19 @@
                 ref[2 * to + zh, :, w1:] = second[row : row + 32]
 
         offset = lax.rem(step - at_ref[1] + 4, 4)
-        for k, ref in ((0, outs[0]), (1, outs[1]), (3, outs[4])):
+
+        for k, late, ref in RING_OUTS:
 
             @pl.when(offset == k)
-            def _(ref=ref):
+            def _(late=late, ref=ref):
                 for x in range(4):
-                    write(ref, x, x)
-
-        @pl.when(offset == 2)
-        def _():
-            for x in range(4):
-                write(outs[2 if x < 2 else 3], x, x % 2)
+                    if late is None or late == x // 2:
+                        write(outs[ref], x, x if ref < 3 else x % 2)
 
     @pl.when(step == 4)
     def _():
-        small = small_ref[...] + core_ref[...] + far_ref[...]
-        for out in (outs[0], outs[1], outs[3], outs[4]):
+        small = small_ref[...]
+        for out in (outs[0], outs[1], outs[2], outs[4]):
             last = out.shape[0] - 1
             out[last] = jnp.zeros(out.shape[1:], F32)
             out[last, 0:16, :] = small[0:16, 0:768]
@@ -666,8 +678,8 @@
     t, c = n1.shape[0], dqkv.shape[1] + mixed[0].shape[1]
     cols = pl.BlockSpec((t, CH), lambda s, at: (0, jnp.minimum(s, 3)))
     whole = lambda a: pl.BlockSpec(a.shape, lambda s, at: (0, 0))
-    rest = [*small, gup, bias]
-    counts = [9, 9, 4, 5, 9]
+    rest = [small, gup, bias]
+    counts = [9, 9, 9, 4, 5]
     return pl.pallas_call(
         mixer_grads_kernel,
         grid_spec=pltpu.PrefetchScalarGridSpec(
@@ -676,34 +688,43 @@
             out_specs=[pl.BlockSpec((n, 32, c), lambda s, at: (0, 0, 0)) for n in counts]),
         out_shape=[jax.ShapeDtypeStruct((n, 32, c), F32) for n in counts],
         compiler_params=pltpu.CompilerParams(vmem_limit_bytes=VMEM_BYTES),
-        cost_estimate=weight(1),
+        cost_estimate=weight(8),
         name="mixer_weight_grads",
     )(at, n1, dqkv, ga, mixed[0], mixed[1], *rest)
 
 
-def unpack_kernel(rows_ref, g1_ref, down_ref, up_ref, bias_ref, g2_ref, q_ref, k_ref, v_ref, o_ref):
-    sums = rows_ref[1]
+def unpack_kernel(
+    own_ref, got_ref, a_ref, b_ref, sums_ref, far_ref,
+    g1_ref, down_ref, up_ref, bias_ref, g2_ref, q_ref, k_ref, v_ref, o_ref, gate_ref, mup_ref, mdown_ref,
+):
+    rows = own_ref[...] + got_ref[...]
+    feed = a_ref[...] + b_ref[...]
+    own = rows[:, 768:1536]
+    sums = sums_ref[...] + far_ref[...]
     wide = jnp.concatenate([sums[16:22, 0:256], sums[16:22, 256:512], sums[16:20, 512:768]], axis=0)
     down_ref[...] = jnp.concatenate([sums[0:16], wide], axis=1)
     for j in range(6):
         n = min(3, 16 - 3 * j)
-        up_ref[3 * j : 3 * j + n, :] = sums[22 : 22 + n, 128 * j : 128 * (j + 1)]
+        up_ref[3 * j : 3 * j + n, :] = own[22 : 22 + n, 128 * j : 128 * (j + 1)]
     g1_ref[:, 0:768] = sums[25:26]
     g1_ref[:, 768:1024] = sums[27:28, 0:256]
     g2_ref[:, 0:768] = sums[26:27]
     g2_ref[:, 768:1024] = sums[27:28, 256:512]
-    bias_ref[...] = sums[27:28, 512:640]
-    q_ref[...] = rows_ref[0, :, 0:128]
-    k_ref[...] = rows_ref[0, :, 128:256]
-    v_ref[...] = rows_ref[0, :, 256:512]
-    o_ref[...] = rows_ref[0, :, 512:768]
-
-
-def unpack(rows):
-    shapes = [(1, 1024), (16, 1024), (16, 128), (1, 128), (1, 1024), (32, 128), (32, 128), (32, 256), (32, 256)]
+    bias_ref[...] = own[27:28, 512:640]
+    q_ref[...] = rows[:, 0:128]
+    k_ref[...] = rows[:, 128:256]
+    v_ref[...] = rows[:, 256:512]
+    o_ref[...] = rows[:, 512:768]
+    gate_ref[...] = feed[:, 0:704]
+    mup_ref[...] = feed[:, 704:1408]
+    mdown_ref[...] = feed[:, 1408:2112]
+
+
+def unpack(own, got, feed_own, feed_got, sums, far):
+    shapes = [(1, 1024), (16, 1024), (16, 128), (1, 128), (1, 1024), (32, 128), (32, 128), (32, 256), (32, 256)] + [(32, 704)] * 3
     return pl.pallas_call(
         unpack_kernel, out_shape=[jax.ShapeDtypeStruct(s, F32) for s in shapes], name="unpack", **SMALL,
-    )(rows)
+    )(own, got, feed_own, feed_got, sums, far)
 
 
 def after(value, *others):
@@ -714,17 +735,30 @@
     return lax.ppermute(v, "dp", shifts[d])
 
 
-def ring_one(v, shifts):
-    return lax.ppermute(v[2], "dp", shifts[1]), lax.ppermute(v[3], "dp", shifts[3])
-
-
-def ring_add(v, got):
-    up, down = got
-    return v[1].at[: up.shape[0]].add(up), v[4].at[v[4].shape[0] - down.shape[0] :].add(down)
-
-
-def ring_two(v, shifts):
-    return lax.ppermute(v[0], "dp", shifts[1]), lax.ppermute(v[1], "dp", shifts[3])
+GX = [[(y * 2 + z) * 4 + x for x in range(4)] for y in range(4) for z in range(2)]
+GY = [[(y * 2 + z) * 4 + x for y in range(4)] for x in range(4) for z in range(2)]
+
+
+def scatter_rows(v, groups):
+    return lax.psum_scatter(v, "dp", scatter_dimension=0, tiled=True, axis_index_groups=groups)
+
+
+def ring_first(v, shifts):
+    return lax.ppermute(v[1], "dp", shifts[1]), lax.ppermute(v[2], "dp", shifts[3])
+
+
+def ring_on(v, got):
+    n = v[3].shape[0]
+    return v[3] + got[0][:n], v[4] + got[1][n:]
+
+
+def ring_last(on, shifts):
+    return lax.ppermute(on[0], "dp", shifts[1]), lax.ppermute(on[1], "dp", shifts[3])
+
+
+def ring_total(v, got, last):
+    n = last[0].shape[0]
+    return jnp.concatenate([v[0][:n] + last[0] + got[1][:n], v[0][n:] + got[0][n:] + last[1]], axis=0)
 
 
 def pick(v, i, dim):
@@ -743,140 +777,131 @@
     g1r, g2r, biasr = g1.reshape(1, -1), g2.reshape(1, -1), bias.reshape(1, -1)
     wgd_t, wg_t, wu_t = wgd.T, wg.T, wu.T
 
+    def phase(*values):
+        return lax.optimization_barrier(values)
+
+    def across(v, at_here, shifts, take):
+        return [take(v, at_here)] + [send(take(v, (at_here + k) % 4), shifts, k) for k in (1, 3, 2)]
+
     with jax.named_scope("out_weights"):
         wide = wout.astype(F32)
         wout_z = z_swap(wide)
         wout_c = core_swap(wide)
     n1, q, k, v, low, logits, cum, mixed_lo, mixed_hi, st = run_mixer_forward(
         lengths, after(tokens, wide), g1r, wq, wk, wv, wgd_t, wgu, biasr)
-    mixed = (mixed_lo, mixed_hi)
-    with jax.named_scope("mixed_heads"):
-        mixed_c = [core_swap(m) for m in mixed]
-        wout_cz = core_swap(after(wout_z, mixed_hi))
-        mixed_z = [None, z_swap(after(mixed_hi, wout_z))]
-        mixed_z[0] = z_swap(after(mixed_lo, wout_z))
+    wout_z, wout_c, mixed_lo, mixed_hi = phase(wout_z, wout_c, mixed_lo, mixed_hi)
+
+    with jax.named_scope("heads_one"):
+        hi_z = z_swap(mixed_hi)
+        hi_c = core_swap(mixed_hi)
+        lo_c = core_swap(mixed_lo)
+        wout_cz = core_swap(wout_z)
     wo, gh = run_before_feed((wout, wout_z, wout_c, wout_cz), cot, wd)
-
-    middle, n2, hid, gg, feed_out, feed_keep, part_out, part_keep = [[None, None] for _ in range(8)]
-    part_in, dn2_out, dn2_z, feed_in = [[None, None] for _ in range(4)]
-    gm, gains = [None, None], [None, None]
-
-    def feed_half(j, ready):
-        with jax.named_scope("mixed_heads"):
-            here = after(mixed_z[j], ready)
-            pieces = (mixed[j], here, mixed_c[j], core_swap(here))
-        (middle[j], n2[j], hid[j], gg[j], feed_out[j], feed_keep[j], part_out[j], part_keep[j]) = run_feed(
-            at, j, tokens, gh, pieces, wo, g2r, wg_t, wu_t, wd)
-
-    def norm_sum(j, ready):
-        with jax.named_scope("second_norm_sum"):
-            part_in[j] = core_swap(after(part_out[j], ready))
-            dn2_out[j] = add_quarter(at, (part_keep[j], part_in[j]))
-            dn2_z[j] = z_swap(dn2_out[j])
-
-    def norm_join(j, ready):
-        with jax.named_scope("second_norm_join"):
-            gm0, gains[j] = run_second_norm(at, j, part_keep[j], part_in[j], after(dn2_z[j], ready), middle[j], g2r, cot)
-            gm[j] = [gm0, z_swap(gm0), core_swap(gm0), None]
-
-    feed_half(1, gh)
-    norm_sum(1, mixed_z[0])
-    feed_half(0, dn2_out[1])
-    norm_sum(0, dn2_z[1])
-    norm_join(1, dn2_out[0])
-
-    a = run_feed_grads(at, *after((n2, gg), gm[1][0]), cot, hid)
-    norm_join(0, (a[0], gm[1][1]))
-    with jax.named_scope("feed_grads_one"):
-        a = after(a, gm[1][1])
-        a_on = ring_one(a, XS)
-
+    hi_z, hi_c, lo_c, mixed_lo, wo, gh = phase(hi_z, hi_c, lo_c, mixed_lo, wo, gh)
+
+    with jax.named_scope("heads_two"):
+        lo_z = z_swap(mixed_lo)
+        hi_cz = core_swap(hi_z)
+    one = run_feed(at, 1, tokens, gh, (mixed_hi, hi_z, hi_c, hi_cz), wo, g2r, wg_t, wu_t, wd)
+    lo_z, one = phase(lo_z, one)
+
+    with jax.named_scope("second_norm_core"):
+        part_in1 = core_swap(one[6])
+        dn2_out1 = add_quarter(at, (one[7], part_in1))
+    dn2_out1, part_in1, one, lo_z = phase(dn2_out1, part_in1, one, lo_z)
+
+    with jax.named_scope("second_norm_z"):
+        dn2_z1 = z_swap(dn2_out1)
+        lo_cz = core_swap(lo_z)
+    zero = run_feed(at, 0, tokens, gh, (mixed_lo, lo_z, lo_c, lo_cz), wo, g2r, wg_t, wu_t, wd)
+    dn2_z1, zero = phase(dn2_z1, zero)
+
+    with jax.named_scope("second_norm_core"):
+        part_in0 = core_swap(zero[6])
+        dn2_out0 = add_quarter(at, (zero[7], part_in0))
+    dn2_out0, part_in0, one, zero = phase(dn2_out0, part_in0, one, zero)
+
+    middle, n2, hid, gg, feed_out, feed_keep, _, part_keep = zip(zero, one)
+    with jax.named_scope("second_norm_z"):
+        dn2_z0 = z_swap(dn2_out0)
+        feed_in = [core_swap(f) for f in feed_out]
+    a = run_feed_grads(n2, gg, cot, hid)
+    dn2_z0, feed_in, a = phase(dn2_z0, feed_in, a)
+
+    gm0, gain2 = run_second_norm(at, part_keep, (part_in0, part_in1), (dn2_z0, dn2_z1), middle, g2r, cot)
+    gm0, a, feed_in = phase(gm0, a, feed_in)
+    with jax.named_scope("second_norm_join"):
+        gm1 = z_swap(gm0)
+        gm2 = core_swap(gm0)
+    with jax.named_scope("feed_grads_x"):
+        a = scatter_rows(a.reshape(1024, a.shape[-1]), GX)
     with jax.named_scope("feed_sum"):
-        feed_in = [core_swap(feed_out[j]) for j in range(2)]
-        feed_pairs = [(feed_keep[j], feed_in[j]) for j in range(2)]
-        feed_z_out = add_quarter(at, *after(feed_pairs, gm[0][0]))
-        feed_z = z_swap(after(feed_z_out, gm[0][1]))
+        feed_z_out = add_quarter(at, (feed_keep[0], feed_in[0]), (feed_keep[1], feed_in[1]))
+    gm1, gm2, feed_z_out = phase(gm1, gm2, feed_z_out)
 
     with jax.named_scope("second_norm_join"):
-        for j in range(2):
-            gm[j][3] = core_swap(after(gm[j][1], (gm[0][1], feed_z_out, a_on)))
-
-    dqkv, part1_out, part1_keep, ga, small, gup, gbias = run_mixer_backward(
-        at, lengths, gm[0] + gm[1], gains, tokens, n1, q, k, v, low, logits, cum, st, wout, wq, wk, wv, wgd_t, wgu)
-
-    with jax.named_scope("first_norm_sum"):
-        part1_in = core_swap(after(part1_out, feed_z))
+        gm3 = core_swap(gm1)
+    gm3, gm1, feed_z_out = phase(gm3, gm1, feed_z_out)
+
+    with jax.named_scope("feed_sum"):
+        feed_z = z_swap(feed_z_out)
+    gm = (gm0, gm1, gm2, gm3)
+    dqkv, *part1_out, part1_keep, ga, small, gup, gbias = run_mixer_backward(
+        at, lengths, gm, gain2, tokens, n1, q, k, v, low, logits, cum, st, wout, wq, wk, wv, wgd_t, wgu)
+    with jax.named_scope("first_norm_core"):
+        part1_in = [core_swap(p) for p in part1_out]
+    c = run_mixer_grads(at, n1, dqkv, ga, (mixed_lo, mixed_hi), small, gup, gbias)
+    feed_z, part1_in, part1_keep, c = phase(feed_z, part1_in, part1_keep, c)
+
+    dn1_out = run_far_sum(at, part1_keep, part1_in[:2])
+    dn1_out, c = phase(dn1_out, c)
+    with jax.named_scope("first_norm_z"):
+        dn1_z = z_swap(dn1_out)
+    with jax.named_scope("mixer_grads_first"):
+        c_got = ring_first(c, YS)
+    feed_own = run_quarter_sum(at, feed_keep, feed_in, feed_z, middle)
+    with jax.named_scope("result_join"):
+        feed1 = z_swap(feed_own)
+    grad0 = run_first_norm(at, part1_keep, part1_in[2:], dn1_z, tokens, gm0, g1r)
+    with jax.named_scope("mixer_grads_last"):
+        c_last = ring_last(ring_on(c, c_got), YS)
+        c = ring_total(c, c_got, c_last)
+    feed1, grad0, c, feed_own, a = phase(feed1, grad0, c, feed_own, a)
+
+    with jax.named_scope("grad_join"):
+        grad1 = z_swap(grad0)
+        grad2 = core_swap(grad0)
+    with jax.named_scope("result_join"):
+        feed2 = core_swap(feed_own)
+    with jax.named_scope("feed_grads_y"):
+        a = scatter_rows(a, GY).reshape(2, 32, -1)
+    with jax.named_scope("mixer_grads_two"):
+        x_pair, x_one = ix // 2, ix % 2
+        c_far = lax.ppermute(jnp.concatenate([rows_of(c, 4 * (1 - x_pair), 4), c[8:9]], axis=0), "dp", XS[2])
+    placed = run_place(at, 0, after((feed_own, grad0, feed2, grad2), c))
+    with jax.named_scope("mixer_grads_two"):
+        c = jnp.concatenate([rows_of(c, 4 * x_pair, 4), c[8:9]], axis=0) + c_far
+        c = after(c, placed)
+        c_near = lax.ppermute(jnp.concatenate([rows_of(c, 2 * (1 - x_one), 2), c[4:5]], axis=0), "dp", X_PAIR)
+        c = jnp.concatenate([rows_of(c, 2 * x_one, 2), c[4:5]], axis=0) + c_near
+    with jax.named_scope("rows"):
+        c = after(c, grad1)
+        turned = lambda i: jnp.concatenate([pick(c, i, 0), c[2]], axis=1)
+        own = turned(zh)
+        got = lax.ppermute(turned(1 - zh), "dp", ZH)
+        a_own = pick(a, zh, 0)
+        a_got = lax.ppermute(after(pick(a, 1 - zh, 0), c), "dp", ZH)
+    with jax.named_scope("result_join"):
+        feed3 = core_swap(feed1)
+    with jax.named_scope("grad_join"):
+        grad3 = core_swap(grad1)
+    result, grad_tokens = run_place(at, 1, (feed1, grad1, feed3, grad3), placed)
     with jax.named_scope("small_sums"):
-        small_core = core_swap(small)
-        small_far = z_swap(small + small_core)
-    with jax.named_scope("feed_grads_one"):
-        a_on = ring_add(a, after(a_on, part1_out))
-    with jax.named_scope("first_norm_sum"):
-        dn1_out = add_quarter(at, after((part1_keep, part1_in), a_on))
-        dn1_z = z_swap(dn1_out)
-    with jax.named_scope("feed_grads_one"):
-        a_in = ring_two(a_on, XS)
-
-    c = run_mixer_grads(at, n1, dqkv, ga, after(mixed, dn1_out), (small, small_core, small_far), gup, gbias)
-    with jax.named_scope("mixer_grads_one"):
-        c_on = ring_one(c, YS)
-
-    with jax.named_scope("feed_join"):
-        feed_own = run_quarter_sum(at, feed_pairs, after(feed_z, c))
-        feed1 = z_swap(after(feed_own, dn1_z))
-        feed2 = core_swap(feed_own)
-
-    with jax.named_scope("mixer_grads_one"):
-        c_on = ring_add(c, after(c_on, feed_own))
-        c_in = ring_two(c_on, YS)
-
-    with jax.named_scope("first_norm_join"):
-        dx0 = run_first_norm(at, part1_keep, part1_in, after(dn1_z, c_on), tokens, g1r)
-        dx1 = z_swap(after(dx0, feed1))
-        dx2 = core_swap(dx0)
-
-    def across(v, at_here, shifts, take):
-        return take(v, at_here) + send(take(v, (at_here + 1) % 4), shifts, 1) + send(take(v, (at_here + 3) % 4), shifts, 3) \
-            + send(take(v, (at_here + 2) % 4), shifts, 2)
-
-    with jax.named_scope("mixer_grads_two"):
-        c, c_in = after((c, c_in), dx0)
-        c = c_sum = c[0] + c_in[0] + c_in[1]
-
-        def with_small(v, i):
-            return jnp.concatenate([lax.dynamic_slice_in_dim(v, 2 * i, 2, 0), v[8:9]], axis=0)
-
-        c = across(c, ix, XS, with_small)
-
-    with jax.named_scope("feed_grads_two"):
-        a, a_in = after((a, a_in), c_sum)
-        a = a_sum = a[0] + a_in[0] + a_in[1]
-        a = across(a, iy, YS, lambda v, i: pick(v, i, 0))
-
-    with jax.named_scope("first_norm_join"):
-        grad_tokens = run_join(at, 0, after((dx0, dx2), a_sum), (gm[0][0], gm[0][2], gm[1][0], gm[1][2]), F32)
-
-    with jax.named_scope("mixer_grads_two"):
-        c = after(c, grad_tokens)
-        turned = lambda i: jnp.stack([pick(c, i, 0), c[2]])
-        rows = turned(zh) + lax.ppermute(turned(1 - zh), "dp", ZH)
-
-    with jax.named_scope("feed_join"):
-        result = run_join(at, 0, (feed_own, feed2), after(middle, c), BF16)
-
-    with jax.named_scope("feed_grads_two"):
-        mlp_rows = swap_zh(after(a, result), zh, 0)
-
-    with jax.named_scope("feed_join"):
-        feed3 = core_swap(after(feed1, a))
-        result = run_join(at, 1, (feed1, feed3), middle, BF16, result)
-
-    with jax.named_scope("small_sums"):
-        gain_one, gate_down, gate_up, gate_bias, gain_two, d_query, d_key, d_value, d_out = unpack(rows)
-
-    with jax.named_scope("first_norm_join"):
-        dx3 = core_swap(dx1)
-        grad_tokens = run_join(at, 1, (dx1, dx3), (gm[0][1], gm[0][3], gm[1][1], gm[1][3]), F32, grad_tokens)
+        sums = own[:, 768:1536] + got[:, 768:1536]
+        sums = sums + core_swap(sums)
+        far = z_swap(sums)
+        (gain_one, gate_down, gate_up, gate_bias, gain_two, d_query, d_key, d_value, d_out, d_gate, d_up, d_down) = unpack(
+            own, got, a_own, a_got, sums, after(far, result))
 
     return (
         result,
@@ -890,9 +915,9 @@
         gate_bias.reshape(128),
         d_out.T,
         gain_two.reshape(1024),
-        mlp_rows[:, 0:704],
-        mlp_rows[:, 704:1408],
-        mlp_rows[:, 1408:2112].T,
+        d_gate,
+        d_up,
+        d_down.T,
     )
 
 

time: 317 us -> 293 us (0.924)
  other arithmetic: 20.9 us -> 4.68 us
  between operations: 1.01 us -> 14.5 us
  Pallas kernels: 132 us -> 120 us
  local copies, waits for them, and re-layouts: 22.2 us -> 12.6 us
    ppermute x12 -> x11, waiting for transfers between devices: 40.2 us -> 60.3 us  [z_swap(): return lax.ppermute(v, 'mp', ZLO)]
    ppermute x16 -> x8, waiting for transfers between devices: 52.2 us -> 33 us  [the longest x1 13.6 us: ring_first(): lax.ppermute(v[1], 'dp', shifts[1])]
    unnamed x80 -> x62, local copies, waits for them, and re-layouts: 19.4 us -> 10.7 us
    add x7 -> x8, other arithmetic: 10.4 us -> 2.11 us  [the longest x1 1.08 us: ring_total(): v[0][:n] + last[0] + got[1][:n]]
    pallas_call x5 -> x4, Pallas kernels: 32.3 us -> 24.9 us  [the longest x2 11.2 us: run_place(): pl.pallas_call(place_kernel, grid_spec=pltpu.PrefetchScalarGridSpec(num_s...]
    scatter-add x4 -> x0, other arithmetic: 6.91 us -> none  [the longest x2 3.52 us: ring_add(): v[4].at[v[4].shape[0] - down.shape[0]:].add(down)]
    pallas_call x4 -> x3, Pallas kernels: 11.9 us -> 8.77 us  [add_quarter(): pl.pallas_call(add_kernel, grid_spec=pltpu.PrefetchScalarGridSpec(num_sca...]
    pallas_call x2 -> x1, Pallas kernels: 6.67 us -> 4.46 us  [run_second_norm(): pl.pallas_call(second_norm_kernel, grid_spec=pltpu.PrefetchScalarGridSpec...]
  transfers between devices with their start and end apart: 48 -> 42, of which waited for: 22 -> 20; matrix products, arithmetic and copies ran while one was open for 8% -> 2% of each run, Pallas kernels for 36% -> 37%
where the time goes in v3:
time: 293 us; the launch traced here: 292 us
  Pallas kernels  120 us (41%)
  waiting for transfers between devices  104 us (35%)
  starting transfers between devices  35.8 us (12%)
  between operations  14.5 us (5%)
  local copies, waits for them, and re-layouts  12.6 us (4%)
  other arithmetic  4.68 us (2%)
    ppermute x11, waiting for transfers between devices, z_swap(): return lax.ppermute(v, 'mp', ZLO)  60.3 us
    pallas_call x2, Pallas kernels, run_feed(): pl.pallas_call(feed_kernel, grid_spec=pltpu.PrefetchScalarGridSpec(num_sc...  28.6 us
    pallas_call x1, Pallas kernels, run_mixer_backward(): pl.pallas_call(mixer_backward, grid_spec=pltpu.PrefetchScalarGridSpec(num...  16.6 us
    ppermute x11, starting transfers between devices, z_swap(): return lax.ppermute(v, 'mp', ZLO)  14.5 us
    ppermute x1, waiting for transfers between devices, ring_first(): lax.ppermute(v[1], 'dp', shifts[1])  13.6 us
    pallas_call x1, Pallas kernels, run_mixer_forward(): pl.pallas_call(mixer_forward, grid=(t // CH,), in_specs=[pl.BlockSpec(mem...  11.3 us
    ppermute x1, waiting for transfers between devices, local(): lax.ppermute(jnp.concatenate([rows_of(c, 4 * (1 - x_pair), 4), c[8:9]], a...  11.3 us
    pallas_call x2, Pallas kernels, run_place(): pl.pallas_call(place_kernel, grid_spec=pltpu.PrefetchScalarGridSpec(num_s...  11.2 us
  transfers between devices with their start and end apart: 42, of which 20 were waited for; matrix products, arithmetic and copies ran while one was open for 2% of the time, Pallas kernels for 37%

profile of v3, /device:TPU:0, one launch (start us, length us, event | category | flops | bytes accessed | tf_op | source)
XLA Modules:
  0.0 291.8 jit_solution(9300996146290329110)
XLA Ops:
  10.6 11.3 %mixer_forward.1 = (bf16[1024,1024]{1,0:T(8,128)(2,1)}, bf16[1024,128]{1,0:T(8,128)(2,1)}, bf16[1024,128]{1,0:T(8,128)(2,1)}, bf16[1024,256]{1,0:T(8,128)(2,1)},...) custom-call(s32[1,8]{1,0:T(1,128)} %len_ref.3, ...), custom_call_target="tpu_custom_call" | custom-call | flops 10000000000 | bytes 1024 | tf_op jit(solution)/shard_map/mixer_forward/pallas_call | solution.py:206
  21.9 12.4 %collective-permute-done.w1_ref = f32[256,1024]{1,0:T(8,128)S(1)} collective-permute-done((f32[256,1024]{1,0:T(8,128)S(1)}, f32[256,1024]{1,0:T(8,128)S(1)}, u32[]{:S(2)}, u32[]{:S(2)}) %collective-permute-start) | collective-permute-done | bytes 1048608 | tf_op jit(solution)/shard_map/out_weights/ppermute | solution.py:66
  38.7 7.0 %before_feed.1 = (bf16[1024,1024]{1,0:T(8,128)(2,1)}, f32[1024,704]{1,0:T(8,128)}) custom-call(bf16[256,1024]{1,0:T(8,128)(2,1)} %refs_14_.1, f32[256,1024]{1,0:T(8,128)} %copy-done.17, f32[256,1024]{1,0:T(8,128)} %copy-done.15, f32[256,1024]{1,0:T(8,128)} %copy-done.20, bf16[1024,1024]{1,0:T(8,128)(2,1)} %base1_ref.1, bf16[704,1024]{1,0:T(8,128)(2,1)} %wd_ref.5), custom_call_target="tpu_custom_call" | custom-call | flops 7000000000 | bytes 1024 | tf_op jit(solution)/shard_map/before_feed/pallas_call | solution.py:236
  45.7 3.3 %collective-permute-done.2.m1_ref = f32[512,256]{1,0:T(8,128)} collective-permute-done((f32[512,256]{1,0:T(8,128)}, f32[512,256]{1,0:T(8,128)}, u32[]{:S(2)}, u32[]{:S(2)}) %collective-permute-start.2) | collective-permute-done | bytes 524320 | tf_op jit(solution)/shard_map/heads_one/ppermute | solution.py:66
  52.1 14.2 %feed_both_ways.2 = (f32[512,1024]{1,0:T(8,128)}, bf16[512,1024]{1,0:T(8,128)(2,1)}, bf16[512,704]{1,0:T(8,128)(2,1)}, bf16[512,1408]{1,0:T(8,128)(2,1)}, f32[25...) custom-call(s32[4]{0:T(128)} %pad_add_fusion.at_ref, ...), custom_call_target="tpu_custom_call" | custom-call | flops 14000000000 | bytes 1024 | tf_op jit(solution)/shard_map/feed_both_ways/pallas_call | solution.py:293
  75.8 14.4 %feed_both_ways.3 = (f32[512,1024]{1,0:T(8,128)}, bf16[512,1024]{1,0:T(8,128)(2,1)}, bf16[512,704]{1,0:T(8,128)(2,1)}, bf16[512,1408]{1,0:T(8,128)(2,1)}, f32[25...) custom-call(s32[4]{0:T(128)} %pad_add_fusion.at_ref, ...), custom_call_target="tpu_custom_call" | custom-call | flops 14000000000 | bytes 1024 | tf_op jit(solution)/shard_map/feed_both_ways/pallas_call | solution.py:293
  98.8 10.4 %feed_weight_grads.1 = f32[4,4,2,32,2176]{4,3,2,1,0:T(8,128)} custom-call(bf16[512,1024]{1,0:T(8,128)(2,1)} %get-tuple-element.237.l0_ref, bf16[512,1024]{1,0:T(8,128)(2,1)} %get-tuple-element.238.l1_ref, bf16[512,1408]{1,0:T(8,128)(2,1)} %get-tuple-element.239.r0_ref, bf16[512,1408]{1,0:T(8,128)(2,1)} %get-tuple-element.240.r1_ref, ...), custom_call_target="tpu_custom_call" | custom-call | flops 12000000000 | bytes 1024 | tf_op jit(solution)/shard_map/feed_weight_grads/pallas_call | solution.py:616
  111.8 4.5 %second_norm_back.1 = (f32[256,1024]{1,0:T(8,128)}, f32[8,1024]{1,0:T(8,128)}) custom-call(s32[4]{0:T(128)} %pad_add_fusion.at_ref, f32[256,1024]{1,0:T(8,128)} %get-tuple-element.232.refs_0_.a0_ref, f32[256,1024]{1,0:T(8,128)} %copy-done.1, f32[128,1024]{1,0:T(8,128)} %copy-done.4, f32[512,1024]{1,0:T(8,128)} %get-tuple-element.244.y0_ref, ...), custom_call_target="tpu_custom_call" | custom-call | flops 3000000000 | bytes 1024 | tf_op jit(solution)/shard_map/second_norm_back/pallas_call | solution.py:508
  119.0 3.3 %add_quarter.5 = f32[256,1024]{1,0:T(8,128)} custom-call(s32[4]{0:T(128)} %pad_add_fusion.at_ref, f32[256,1024]{1,0:T(8,128)} %get-tuple-element.231.refs_0_.a0_ref, f32[256,1024]{1,0:T(8,128)} %copy-done.11, f32[256,1024]{1,0:T(8,128)} %get-tuple-element.254.refs_2_.a1_ref, f32[256,1024]{1,0:T(8,128)} %copy-done.12), custom_call_target="tpu_custom_call" | custom-call | flops 3000000000 | bytes 1024 | tf_op jit(solution)/shard_map/feed_sum/add_quarter/pallas_call | solution.py:456
  122.3 20.7 %collective-permute-done.15.refs_1_ = f32[256,1024]{1,0:T(8,128)S(1)} collective-permute-done((f32[256,1024]{1,0:T(8,128)S(1)}, f32[256,1024]{1,0:T(8,128)S(1)}, u32[]{:S(2)}, u32[]{:S(2)}) %collective-permute-start.15) | collective-permute-done | bytes 1048608 | tf_op jit(solution)/shard_map/second_norm_join/ppermute | solution.py:66
  148.2 16.6 %mixer_backward.1 = (bf16[1024,512]{1,0:T(8,128)(2,1)}, f32[128,1024]{1,0:T(8,128)}, f32[128,1024]{1,0:T(8,128)}, f32[128,1024]{1,0:T(8,128)}, f32[128,1024]{1,0...) custom-call(s32[4]{0:T(128)} %pad_add_fusion.at_ref, ...), custom_call_target="tpu_custom_call" | custom-call | flops 16000000000 | bytes 1024 | tf_op jit(solution)/shard_map/mixer_backward/pallas_call | solution.py:416
  165.9 8.3 %mixer_weight_grads.1 = (f32[9,32,768]{2,1,0:T(8,128)}, f32[9,32,768]{2,1,0:T(8,128)}, f32[9,32,768]{2,1,0:T(8,128)}, f32[4,32,768]{2,1,0:T(8,128)}, f32[5,32,768]{2,1,0:T(8,128)}) custom-call(s32[4]{0:T(128)} %pad_add_fusion.at_ref, bf16[1024,1024]{1,0:T(8,128)(2,1)} %get-tuple-element.264.refs_6_.l_ref, bf16[1024,512]{1,0:T(8,128)(2,1)} %get-tuple-element.277.r0_ref, ...), custom_call_target="tpu_custom_call" | custom-call | flops 8000000000 | bytes 1024 | tf_op jit(solution)/shard_map/mixer_weight_grads/pallas_call | solution.py:683
  175.7 3.3 %far_sum.1 = f32[256,1024]{1,0:T(8,128)} custom-call(s32[4]{0:T(128)} %pad_add_fusion.at_ref, f32[512,1024]{1,0:T(8,128)} %get-tuple-element.288.keep_ref.a_ref, f32[128,1024]{1,0:T(8,128)} %copy-done.26, f32[128,1024]{1,0:T(8,128)} %copy-done.27), custom_call_target="tpu_custom_call" | custom-call | flops 3000000000 | bytes 1024 | tf_op jit(solution)/shard_map/far_sum/pallas_call | solution.py:530
  182.5 4.0 %quarter_sum.1.r0_ref = f32[256,1024]{1,0:T(8,128)} custom-call(s32[4]{0:T(128)} %pad_add_fusion.at_ref, f32[256,1024]{1,0:T(8,128)} %get-tuple-element.231.refs_0_.a0_ref, f32[256,1024]{1,0:T(8,128)} %copy-done.11, f32[512,1024]{1,0:T(8,128)} %get-tuple-element.244.y0_ref, f32[256,1024]{1,0:T(8,128)} %get-tuple-element.254.refs_2_.a1_ref, ...), custom_call_target="tpu_custom_call" | custom-call | flops 3000000000 | bytes 1024 | tf_op jit(solution)/shard_map/quarter_sum/pallas_call | solution.py:475
  188.4 13.6 %collective-permute-done.25 = f32[9,32,768]{2,1,0:T(8,128)S(1)} collective-permute-done((f32[9,32,768]{2,1,0:T(8,128)}, f32[9,32,768]{2,1,0:T(8,128)S(1)}, u32[]{:S(2)}, u32[]{:S(2)}) %collective-permute-start.25) | collective-permute-done | bytes 884768 | tf_op jit(solution)/shard_map/mixer_grads_first/ppermute | solution.py:747
  208.8 4.1 %first_norm_back.1.g0_ref = f32[256,1024]{1,0:T(8,128)} custom-call(s32[4]{0:T(128)} %pad_add_fusion.at_ref, f32[512,1024]{1,0:T(8,128)} %get-tuple-element.288.keep_ref.a_ref, f32[128,1024]{1,0:T(8,128)} %copy-done.23, f32[128,1024]{1,0:T(8,128)} %copy-done.24, f32[256,1024]{1,0:T(8,128)} %collective-permute-done.24.c_ref, bf16[1024,1024]{1,0:T(8,128)(2,1)} %y_ref.1, ...), custom_call_target="tpu_custom_call" | custom-call | flops 3000000000 | bytes 1024 | tf_op jit(solution)/shard_map/first_norm_back/pallas_call | solution.py:555
  215.9 13.7 %collective-permute-done.23.r0_ref = f32[256,1024]{1,0:T(8,128)} collective-permute-done((f32[256,1024]{1,0:T(8,128)}, f32[256,1024]{1,0:T(8,128)}, u32[]{:S(2)}, u32[]{:S(2)}) %collective-permute-start.23) | collective-permute-done | bytes 1048608 | tf_op jit(solution)/shard_map/result_join/ppermute | solution.py:66
  233.8 11.3 %collective-permute-done.34 = f32[5,32,768]{2,1,0:T(8,128)S(1)} collective-permute-done((f32[5,32,768]{2,1,0:T(8,128)S(1)}, f32[5,32,768]{2,1,0:T(8,128)S(1)}, u32[]{:S(2)}, u32[]{:S(2)}) %collective-permute-start.34) | collective-permute-done | bytes 491552 | tf_op jit(solution)/shard_map/mixer_grads_two/ppermute | solution.py:880
  245.2 5.6 %place_rows.2 = (bf16[1024,1024]{1,0:T(8,128)(2,1)}, f32[1024,1024]{1,0:T(8,128)}) custom-call(s32[4]{0:T(128)} %pad_add_fusion.at_ref, f32[256,1024]{1,0:T(8,128)} %quarter_sum.1.r0_ref, f32[256,1024]{1,0:T(8,128)} %first_norm_back.1.g0_ref, f32[256,1024]{1,0:T(8,128)} %collective-permute-done.32.r1_ref, f32[256,1024]{1,0:T(8,128)} %collective-permute-done.33.g1_ref), custom_call_target="tpu_custom_call" | custom-call | flops 3000000000 | bytes 1024 | tf_op jit(solution)/shard_map/place_rows/pallas_call | solution.py:585
  252.3 5.9 %collective-permute-done.29.g0_ref = f32[256,1024]{1,0:T(8,128)} collective-permute-done((f32[256,1024]{1,0:T(8,128)S(1)}, f32[256,1024]{1,0:T(8,128)}, u32[]{:S(2)}, u32[]{:S(2)}) %collective-permute-start.29) | collective-permute-done | bytes 1048608 | tf_op jit(solution)/shard_map/grad_join/ppermute | solution.py:66
  260.0 3.4 %collective-permute-start.36 = (f32[32,1536]{1,0:T(8,128)S(1)}, f32[32,1536]{1,0:T(8,128)S(1)}, u32[]{:S(2)}, u32[]{:S(2)}) collective-permute-start(f32[32,1536]{1,0:T(8,128)S(1)} %get-tuple-element.343), channel_id=1, source_target_pairs={{0,16},{4,20},{8,24},{12,28},{16,0},{20,4},{24,8},{28,12},{32,48},... | collective-permute-start | bytes 589832 | tf_op jit(solution)/shard_map/rows/ppermute | solution.py:891
  263.4 4.9 %collective-permute-done.36.got_ref = f32[32,1536]{1,0:T(8,128)S(1)} collective-permute-done((f32[32,1536]{1,0:T(8,128)S(1)}, f32[32,1536]{1,0:T(8,128)S(1)}, u32[]{:S(2)}, u32[]{:S(2)}) %collective-permute-start.36) | collective-permute-done | bytes 196640 | tf_op jit(solution)/shard_map/rows/ppermute | solution.py:891
  271.7 3.5 %collective-permute-start.37 = (f32[32,2176]{1,0:T(8,128)S(1)}, f32[32,2176]{1,0:T(8,128)S(1)}, u32[]{:S(2)}, u32[]{:S(2)}) collective-permute-start(f32[32,2176]{1,0:T(8,128)S(1)} %get-tuple-element.320), channel_id=1, source_target_pairs={{0,16},{4,20},{8,24},{12,28},{16,0},{20,4},{24,8},{28,12},{32,48},... | collective-permute-start | bytes 835592 | tf_op jit(solution)/shard_map/rows/ppermute | solution.py:893
  276.2 5.6 %place_rows.3 = (bf16[1024,1024]{1,0:T(8,128)(2,1)}, f32[1024,1024]{1,0:T(8,128)}) custom-call(s32[4]{0:T(128)} %pad_add_fusion.at_ref, f32[256,1024]{1,0:T(8,128)} %collective-permute-done.23.r0_ref, f32[256,1024]{1,0:T(8,128)} %collective-permute-done.29.g0_ref, f32[256,1024]{1,0:T(8,128)} %copy-done.14, ...), custom_call_target="tpu_custom_call", output_to_operand_aliasing={{0}: (5, {}), {1}: (6, {})} | custom-call | flops 3000000000 | bytes 1024 | tf_op jit(solution)/shard_map/place_rows/pallas_call | solution.py:585
  (161 shorter events, 72.2 us)
Async XLA Ops:
  7.2 222.4 %reduce-scatter.3.cloned.1.call-start = ((), (), s32[]{:S(2)}) async-start(), calls=%async_computation.2 | async-start | bytes 11141120 | tf_op jit(solution)/shard_map/feed_grads_x/reduce_scatter | solution.py:743
  8.4 13.5 %collective-permute-start.1 = (f32[256,1024]{1,0:T(8,128)S(1)}, f32[256,1024]{1,0:T(8,128)S(1)}, u32[]{:S(2)}, u32[]{:S(2)}) collective-permute-start(f32[256,1024]{1,0:T(8,128)S(1)} %convert_element_type.3), channel_id=1, source_target_pairs={{0,1},{1,0},{2,3},{3,2},{4,5},{5,4},{6,7},{7,6},{8,9},{9,8},{10,11... | collective-permute-start | bytes 3145736 | tf_op jit(solution)/shard_map/out_weights/ppermute | solution.py:62
  8.5 25.8 %collective-permute-start = (f32[256,1024]{1,0:T(8,128)S(1)}, f32[256,1024]{1,0:T(8,128)S(1)}, u32[]{:S(2)}, u32[]{:S(2)}) collective-permute-start(f32[256,1024]{1,0:T(8,128)S(1)} %convert_element_type.3), channel_id=1, source_target_pairs={{0,2},{2,0},{1,3},{3,1},{4,6},{6,4},{5,7},{7,5},{8,10},{10,8},{9,1... | collective-permute-start | bytes 3145736 | tf_op jit(solution)/shard_map/out_weights/ppermute | solution.py:66
  34.8 14.2 %collective-permute-start.2 = (f32[512,256]{1,0:T(8,128)}, f32[512,256]{1,0:T(8,128)}, u32[]{:S(2)}, u32[]{:S(2)}) collective-permute-start(f32[512,256]{1,0:T(8,128)} %get-tuple-element.177.m0_ref.m1_ref), channel_id=1, source_target_pairs={{0,2},{2,0},{1,3},{3,1},{4,6},{6,4},{5,7},{7,5},{8,10},{10,8},{9,1... | collective-permute-start | bytes 1572872 | tf_op jit(solution)/shard_map/heads_one/ppermute | solution.py:66
  49.6 16.7 %collective-permute-start.6 = (f32[512,256]{1,0:T(8,128)}, f32[512,256]{1,0:T(8,128)S(1)}, u32[]{:S(2)}, u32[]{:S(2)}) collective-permute-start(f32[512,256]{1,0:T(8,128)} %get-tuple-element.183.m0_ref), channel_id=1, source_target_pairs={{0,2},{2,0},{1,3},{3,1},{4,6},{6,4},{5,7},{7,5},{8,10},{10,8},{9,1... | collective-permute-start | bytes 1572872 | tf_op jit(solution)/shard_map/heads_two/ppermute | solution.py:66
  73.2 16.9 %collective-permute-start.9 = (f32[128,1024]{1,0:T(8,128)}, f32[128,1024]{1,0:T(8,128)S(1)}, u32[]{:S(2)}, u32[]{:S(2)}) collective-permute-start(f32[128,1024]{1,0:T(8,128)} %add_quarter.3), channel_id=1, source_target_pairs={{0,2},{2,0},{1,3},{3,1},{4,6},{6,4},{5,7},{7,5},{8,10},{10,8},{9,1... | collective-permute-start | bytes 1572872 | tf_op jit(solution)/shard_map/second_norm_z/ppermute | solution.py:66
  96.8 14.2 %collective-permute-start.12 = (f32[128,1024]{1,0:T(8,128)}, f32[128,1024]{1,0:T(8,128)S(1)}, u32[]{:S(2)}, u32[]{:S(2)}) collective-permute-start(f32[128,1024]{1,0:T(8,128)} %add_quarter.4), channel_id=1, source_target_pairs={{0,2},{2,0},{1,3},{3,1},{4,6},{6,4},{5,7},{7,5},{8,10},{10,8},{9,1... | collective-permute-start | bytes 1572872 | tf_op jit(solution)/shard_map/second_norm_z/ppermute | solution.py:66
  98.3 12.7 %collective-permute-start.13 = (f32[256,1024]{1,0:T(8,128)}, f32[256,1024]{1,0:T(8,128)S(1)}, u32[]{:S(2)}, u32[]{:S(2)}) collective-permute-start(f32[256,1024]{1,0:T(8,128)} %get-tuple-element.235), channel_id=1, source_target_pairs={{0,1},{1,0},{2,3},{3,2},{4,5},{5,4},{6,7},{7,6},{8,9},{9,8},{10,11... | collective-permute-start | bytes 3145736 | tf_op jit(solution)/shard_map/second_norm_z/ppermute | solution.py:62
  98.3 12.7 %collective-permute-start.14 = (f32[256,1024]{1,0:T(8,128)}, f32[256,1024]{1,0:T(8,128)S(1)}, u32[]{:S(2)}, u32[]{:S(2)}) collective-permute-start(f32[256,1024]{1,0:T(8,128)} %get-tuple-element.236), channel_id=1, source_target_pairs={{0,1},{1,0},{2,3},{3,2},{4,5},{5,4},{6,7},{7,6},{8,9},{9,8},{10,11... | collective-permute-start | bytes 3145736 | tf_op jit(solution)/shard_map/second_norm_z/ppermute | solution.py:62
  116.3 153.7 %reduce-scatter.5.cloned.1.call-start = ((), (), s32[]{:S(2)}) async-start(), calls=%async_computation.3 | async-start | bytes 2785280 | tf_op jit(solution)/shard_map/feed_grads_y/reduce_scatter | solution.py:743
  117.5 25.6 %collective-permute-start.15 = (f32[256,1024]{1,0:T(8,128)S(1)}, f32[256,1024]{1,0:T(8,128)S(1)}, u32[]{:S(2)}, u32[]{:S(2)}) collective-permute-start(f32[256,1024]{1,0:T(8,128)S(1)} %copy-done.10), channel_id=1, source_target_pairs={{0,2},{2,0},{1,3},{3,1},{4,6},{6,4},{5,7},{7,5},{8,10},{10,8},{9,1... | collective-permute-start | bytes 3145736 | tf_op jit(solution)/shard_map/second_norm_join/ppermute | solution.py:66
  146.7 27.6 %collective-permute-start.18 = (f32[256,1024]{1,0:T(8,128)}, f32[256,1024]{1,0:T(8,128)S(1)}, u32[]{:S(2)}, u32[]{:S(2)}) collective-permute-start(f32[256,1024]{1,0:T(8,128)} %add_quarter.5), channel_id=1, source_target_pairs={{0,2},{2,0},{1,3},{3,1},{4,6},{6,4},{5,7},{7,5},{8,10},{10,8},{9,1... | collective-permute-start | bytes 3145736 | tf_op jit(solution)/shard_map/feed_sum/ppermute | solution.py:66
  179.0 23.0 %collective-permute-start.25 = (f32[9,32,768]{2,1,0:T(8,128)}, f32[9,32,768]{2,1,0:T(8,128)S(1)}, u32[]{:S(2)}, u32[]{:S(2)}) collective-permute-start(f32[9,32,768]{2,1,0:T(8,128)} %get-tuple-element.301), channel_id=1, source_target_pairs={{0,32},{4,36},{8,40},{12,44},{16,48},{20,52},{24,56},{28,60},{32,6... | collective-permute-start | bytes 2654216 | tf_op jit(solution)/shard_map/mixer_grads_first/ppermute | solution.py:747
  180.6 22.5 %collective-permute-start.27 = (f32[9,32,768]{2,1,0:T(8,128)S(1)}, f32[9,32,768]{2,1,0:T(8,128)S(1)}, u32[]{:S(2)}, u32[]{:S(2)}) collective-permute-start(f32[9,32,768]{2,1,0:T(8,128)S(1)} %copy-done.21), channel_id=1, source_target_pairs={{0,96},{4,100},{8,104},{12,108},{16,112},{20,116},{24,120},{28,124... | collective-permute-start | bytes 2654216 | tf_op jit(solution)/shard_map/mixer_grads_first/ppermute | solution.py:747
  182.3 26.4 %collective-permute-start.24 = (f32[256,1024]{1,0:T(8,128)}, f32[256,1024]{1,0:T(8,128)}, u32[]{:S(2)}, u32[]{:S(2)}) collective-permute-start(f32[256,1024]{1,0:T(8,128)} %far_sum.1), channel_id=1, source_target_pairs={{0,2},{2,0},{1,3},{3,1},{4,6},{6,4},{5,7},{7,5},{8,10},{10,8},{9,1... | collective-permute-start | bytes 3145736 | tf_op jit(solution)/shard_map/first_norm_z/ppermute | solution.py:66
  186.5 43.1 %collective-permute-start.23 = (f32[256,1024]{1,0:T(8,128)}, f32[256,1024]{1,0:T(8,128)}, u32[]{:S(2)}, u32[]{:S(2)}) collective-permute-start(f32[256,1024]{1,0:T(8,128)} %quarter_sum.1.r0_ref), channel_id=1, source_target_pairs={{0,2},{2,0},{1,3},{3,1},{4,6},{6,4},{5,7},{7,5},{8,10},{10,8},{9,1... | collective-permute-start | bytes 3145736 | tf_op jit(solution)/shard_map/result_join/ppermute | solution.py:66
  203.2 12.5 %collective-permute-start.28 = (f32[5,32,768]{2,1,0:T(8,128)S(1)}, f32[5,32,768]{2,1,0:T(8,128)S(1)}, u32[]{:S(2)}, u32[]{:S(2)}) collective-permute-start(f32[5,32,768]{2,1,0:T(8,128)S(1)} %slice_add_fusion), channel_id=1, source_target_pairs={{0,96},{4,100},{8,104},{12,108},{16,112},{20,116},{24,120},{28,124... | collective-permute-start | bytes 1474568 | tf_op jit(solution)/shard_map/mixer_grads_last/ppermute | solution.py:756
  229.6 15.6 %collective-permute-start.32 = (f32[256,1024]{1,0:T(8,128)}, f32[256,1024]{1,0:T(8,128)}, u32[]{:S(2)}, u32[]{:S(2)}) collective-permute-start(f32[256,1024]{1,0:T(8,128)} %quarter_sum.1.r0_ref), channel_id=1, source_target_pairs={{0,1},{1,0},{2,3},{3,2},{4,5},{5,4},{6,7},{7,6},{8,9},{9,8},{10,11... | collective-permute-start | bytes 3145736 | tf_op jit(solution)/shard_map/result_join/ppermute | solution.py:62
  229.7 15.5 %collective-permute-start.33 = (f32[256,1024]{1,0:T(8,128)S(1)}, f32[256,1024]{1,0:T(8,128)}, u32[]{:S(2)}, u32[]{:S(2)}) collective-permute-start(f32[256,1024]{1,0:T(8,128)S(1)} %copy-done.9), channel_id=1, source_target_pairs={{0,1},{1,0},{2,3},{3,2},{4,5},{5,4},{6,7},{7,6},{8,9},{9,8},{10,11... | collective-permute-start | bytes 3145736 | tf_op jit(solution)/shard_map/grad_join/ppermute | solution.py:62
  230.3 14.8 %collective-permute-start.34 = (f32[5,32,768]{2,1,0:T(8,128)S(1)}, f32[5,32,768]{2,1,0:T(8,128)S(1)}, u32[]{:S(2)}, u32[]{:S(2)}) collective-permute-start(f32[5,32,768]{2,1,0:T(8,128)S(1)} %pad_maximum_fusion.1), channel_id=1, source_target_pairs={{0,8},{4,12},{8,0},{12,4},{16,24},{20,28},{24,16},{28,20},{32,40},... | collective-permute-start | bytes 1474568 | tf_op jit(solution)/shard_map/mixer_grads_two/ppermute | solution.py:880
  233.2 25.0 %collective-permute-start.29 = (f32[256,1024]{1,0:T(8,128)S(1)}, f32[256,1024]{1,0:T(8,128)}, u32[]{:S(2)}, u32[]{:S(2)}) collective-permute-start(f32[256,1024]{1,0:T(8,128)S(1)} %copy-done.9), channel_id=1, source_target_pairs={{0,2},{2,0},{1,3},{3,1},{4,6},{6,4},{5,7},{7,5},{8,10},{10,8},{9,1... | collective-permute-start | bytes 3145736 | tf_op jit(solution)/shard_map/grad_join/ppermute | solution.py:66
  252.3 22.9 %collective-permute-start.30 = (f32[256,1024]{1,0:T(8,128)}, f32[256,1024]{1,0:T(8,128)S(1)}, u32[]{:S(2)}, u32[]{:S(2)}) collective-permute-start(f32[256,1024]{1,0:T(8,128)} %collective-permute-done.23.r0_ref), channel_id=1, source_target_pairs={{0,1},{1,0},{2,3},{3,2},{4,5},{5,4},{6,7},{7,6},{8,9},{9,8},{10,11... | collective-permute-start | bytes 3145736 | tf_op jit(solution)/shard_map/result_join/ppermute | solution.py:62
  258.2 17.0 %collective-permute-start.31 = (f32[256,1024]{1,0:T(8,128)}, f32[256,1024]{1,0:T(8,128)}, u32[]{:S(2)}, u32[]{:S(2)}) collective-permute-start(f32[256,1024]{1,0:T(8,128)} %collective-permute-done.29.g0_ref), channel_id=1, source_target_pairs={{0,1},{1,0},{2,3},{3,2},{4,5},{5,4},{6,7},{7,6},{8,9},{9,8},{10,11... | collective-permute-start | bytes 3145736 | tf_op jit(solution)/shard_map/grad_join/ppermute | solution.py:62
  269.7 12.0 %collective-permute-start.39 = (f32[32,768]{1,0:T(8,128)S(1)}, f32[32,768]{1,0:T(8,128)S(1)}, u32[]{:S(2)}, u32[]{:S(2)}) collective-permute-start(f32[32,768]{1,0:T(8,128)S(1)} %add.100.sums_ref), channel_id=1, source_target_pairs={{0,2},{2,0},{1,3},{3,1},{4,6},{6,4},{5,7},{7,5},{8,10},{10,8},{9,1... | collective-permute-start | bytes 294920 | tf_op jit(solution)/shard_map/small_sums/ppermute | solution.py:66
  (49 other events, 328.5 us)
Sparse Core Ops, SparseCore 0:
  116.4 86.7 reduce-scatter.2
  229.7 31.2 reduce-scatter.4

commit v4 on v3

--- a/solution.py
+++ b/solution.py
@@ -439,47 +439,8 @@
 )
 
 
-def add_kernel(at_ref, *refs):
-    out_ref = refs[-1]
-    n = out_ref.shape[0] // (len(refs) // 2)
-    for j in range(len(refs) // 2):
-        out_ref[j * n : (j + 1) * n] = refs[2 * j][...] + refs[2 * j + 1][...]
-
-
-def add_quarter(at, *pairs):
-    ops, specs = [], []
-    for pair in pairs:
-        for j in range(pair[0].shape[0] // 256):
-            ops += pair
-            specs += [pl.BlockSpec((128, 1024), lambda s, at, j=j: (2 * j + 1 - at[3], 0))] * 2
-    n = 64 * len(ops)
-    return pl.pallas_call(
-        add_kernel,
-        grid_spec=pltpu.PrefetchScalarGridSpec(
-            num_scalar_prefetch=1, grid=(1,), in_specs=specs, out_specs=pl.BlockSpec((n, 1024), lambda s, at: (0, 0))),
-        out_shape=jax.ShapeDtypeStruct((n, 1024), F32),
-        name="add_quarter",
-        **SMALL,
-    )(at, *ops)
-
-
-def quarter_sum_kernel(at_ref, a0_ref, b0_ref, y0_ref, a1_ref, b1_ref, y1_ref, c_ref, o_ref):
-    o_ref[0:128] = a0_ref[...] + b0_ref[...] + c_ref[0:128] + y0_ref[...]
-    o_ref[128:256] = a1_ref[...] + b1_ref[...] + c_ref[128:256] + y1_ref[...]
-
-
-def run_quarter_sum(at, keep, got, far, middle):
-    of_half = pl.BlockSpec((128, 1024), lambda s, at: (at[3], 0))
-    of_chunk = pl.BlockSpec((128, 1024), lambda s, at: (2 * at[2] + at[3], 0))
-    own = pl.BlockSpec((256, 1024), lambda s, at: (0, 0))
-    return pl.pallas_call(
-        quarter_sum_kernel,
-        grid_spec=pltpu.PrefetchScalarGridSpec(
-            num_scalar_prefetch=1, grid=(1,), in_specs=[of_half, of_half, of_chunk] * 2 + [own], out_specs=own),
-        out_shape=jax.ShapeDtypeStruct((256, 1024), F32),
-        name="quarter_sum",
-        **SMALL,
-    )(at, keep[0], got[0], middle[0], keep[1], got[1], middle[1], far)
+def quarter(v, j, which):
+    return rows_of(v, 256 * j + 128 * which, 128)
 
 
 def norm_gradient(dn, y, gain):
@@ -515,27 +476,6 @@
         name="second_norm_back",
         **SMALL,
     )(at, *ops, gain, cot, cot)
-
-
-def far_sum_kernel(at_ref, keep_ref, got0_ref, got1_ref, o_ref):
-    for j, got_ref in enumerate((got0_ref, got1_ref)):
-
-        @pl.when(pl.program_id(0) == j)
-        def _(got_ref=got_ref):
-            o_ref[...] = keep_ref[...] + got_ref[...]
-
-
-def run_far_sum(at, keep, got):
-    fixed = pl.BlockSpec((128, 1024), lambda s, at: (0, 0))
-    return pl.pallas_call(
-        far_sum_kernel,
-        grid_spec=pltpu.PrefetchScalarGridSpec(
-            num_scalar_prefetch=1, grid=(2,), in_specs=[pl.BlockSpec((128, 1024), lambda s, at: (2 * s + 1 - at[3], 0)), fixed, fixed],
-            out_specs=pl.BlockSpec((128, 1024), lambda s, at: (s, 0))),
-        out_shape=jax.ShapeDtypeStruct((256, 1024), F32),
-        name="far_sum",
-        **SMALL,
-    )(at, keep, *got)
 
 
 def first_norm_kernel(at_ref, a_ref, b0_ref, b1_ref, c_ref, y_ref, base_ref, gain_ref, own_ref):
@@ -807,7 +747,7 @@
 
     with jax.named_scope("second_norm_core"):
         part_in1 = core_swap(one[6])
-        dn2_out1 = add_quarter(at, (one[7], part_in1))
+        dn2_out1 = quarter(one[7], 0, 1 - z) + quarter(part_in1, 0, 1 - z)
     dn2_out1, part_in1, one, lo_z = phase(dn2_out1, part_in1, one, lo_z)
 
     with jax.named_scope("second_norm_z"):
@@ -818,7 +758,7 @@
 
     with jax.named_scope("second_norm_core"):
         part_in0 = core_swap(zero[6])
-        dn2_out0 = add_quarter(at, (zero[7], part_in0))
+        dn2_out0 = quarter(zero[7], 0, 1 - z) + quarter(part_in0, 0, 1 - z)
     dn2_out0, part_in0, one, zero = phase(dn2_out0, part_in0, one, zero)
 
     middle, n2, hid, gg, feed_out, feed_keep, _, part_keep = zip(zero, one)
@@ -836,7 +776,7 @@
     with jax.named_scope("feed_grads_x"):
         a = scatter_rows(a.reshape(1024, a.shape[-1]), GX)
     with jax.named_scope("feed_sum"):
-        feed_z_out = add_quarter(at, (feed_keep[0], feed_in[0]), (feed_keep[1], feed_in[1]))
+        feed_z_out = jnp.concatenate([quarter(feed_keep[j], 0, 1 - z) + quarter(feed_in[j], 0, 1 - z) for j in range(2)], axis=0)
     gm1, gm2, feed_z_out = phase(gm1, gm2, feed_z_out)
 
     with jax.named_scope("second_norm_join"):
@@ -853,13 +793,15 @@
     c = run_mixer_grads(at, n1, dqkv, ga, (mixed_lo, mixed_hi), small, gup, gbias)
     feed_z, part1_in, part1_keep, c = phase(feed_z, part1_in, part1_keep, c)
 
-    dn1_out = run_far_sum(at, part1_keep, part1_in[:2])
+    dn1_out = jnp.concatenate([quarter(part1_keep, j, 1 - z) + part1_in[j] for j in range(2)], axis=0)
     dn1_out, c = phase(dn1_out, c)
     with jax.named_scope("first_norm_z"):
         dn1_z = z_swap(dn1_out)
     with jax.named_scope("mixer_grads_first"):
         c_got = ring_first(c, YS)
-    feed_own = run_quarter_sum(at, feed_keep, feed_in, feed_z, middle)
+    feed_own = jnp.concatenate([
+        quarter(feed_keep[j], 0, z) + quarter(feed_in[j], 0, z) + feed_z[128 * j : 128 * (j + 1)]
+        + rows_of(middle[j], 256 * core + 128 * z, 128) for j in range(2)], axis=0)
     with jax.named_scope("result_join"):
         feed1 = z_swap(feed_own)
     grad0 = run_first_norm(at, part1_keep, part1_in[2:], dn1_z, tokens, gm0, g1r)
@@ -885,7 +827,8 @@
         c_near = lax.ppermute(jnp.concatenate([rows_of(c, 2 * (1 - x_one), 2), c[4:5]], axis=0), "dp", X_PAIR)
         c = jnp.concatenate([rows_of(c, 2 * x_one, 2), c[4:5]], axis=0) + c_near
     with jax.named_scope("rows"):
-        c = after(c, grad1)
+        turned_c = after(c, grad1)
+        c = turned_c
         turned = lambda i: jnp.concatenate([pick(c, i, 0), c[2]], axis=1)
         own = turned(zh)
         got = lax.ppermute(turned(1 - zh), "dp", ZH)
@@ -894,14 +837,15 @@
     with jax.named_scope("result_join"):
         feed3 = core_swap(feed1)
     with jax.named_scope("grad_join"):
-        grad3 = core_swap(grad1)
+        grad3 = core_swap(after(grad1, c))
     result, grad_tokens = run_place(at, 1, (feed1, grad1, feed3, grad3), placed)
     with jax.named_scope("small_sums"):
+        got = after(got, result)
         sums = own[:, 768:1536] + got[:, 768:1536]
         sums = sums + core_swap(sums)
         far = z_swap(sums)
         (gain_one, gate_down, gate_up, gate_bias, gain_two, d_query, d_key, d_value, d_out, d_gate, d_up, d_down) = unpack(
-            own, got, a_own, a_got, sums, after(far, result))
+            own, got, a_own, a_got, sums, far)
 
     return (
         result,

time: 293 us -> 286 us (0.976)
  Pallas kernels: 120 us -> 103 us
  other arithmetic: 4.68 us -> 17.7 us
  local copies, waits for them, and re-layouts: 12.6 us -> 7.33 us
  waiting for transfers between devices: 104 us -> 107 us
    pallas_call x5 -> x0, Pallas kernels: 16.1 us -> none  [the longest x3 8.77 us: add_quarter(): pl.pallas_call(add_kernel, grid_spec=pltpu.PrefetchScalarGridSpec(num_sca...]
    add x0 -> x5, other arithmetic: none -> 8.74 us  [the longest x1 2.25 us: local(): dn2_out0 = quarter(zero[7], 0, 1 - z) + quarter(part_in0, 0, 1 - z)]
    ppermute x1, waiting for transfers between devices: 0.96 us -> 6.67 us  [local(): lax.ppermute(jnp.concatenate([rows_of(c, 2 * (1 - x_one), 2), c[4:5]], ax...]
    unnamed x62 -> x46, local copies, waits for them, and re-layouts: 10.7 us -> 5.35 us
    ppermute x1, waiting for transfers between devices: 4.9 us -> 0.01 us  [local(): got = lax.ppermute(turned(1 - zh), 'dp', ZH)]
    ppermute x11, waiting for transfers between devices: 60.3 us -> 56.1 us  [z_swap(): return lax.ppermute(v, 'mp', ZLO)]
  transfers between devices with their start and end apart: 42 -> 42, of which waited for: 20 -> 19; matrix products, arithmetic and copies ran while one was open for 2% -> 5% of each run, Pallas kernels for 37% -> 34%
where the time goes in v4:
time: 286 us; the launch traced here: 285 us
  waiting for transfers between devices  107 us (37%)
  Pallas kernels  103 us (36%)
  starting transfers between devices  34.7 us (12%)
  other arithmetic  17.7 us (6%)
  between operations  14.5 us (5%)
  local copies, waits for them, and re-layouts  7.33 us (3%)
    ppermute x11, waiting for transfers between devices, z_swap(): return lax.ppermute(v, 'mp', ZLO)  56.1 us
    pallas_call x2, Pallas kernels, run_feed(): pl.pallas_call(feed_kernel, grid_spec=pltpu.PrefetchScalarGridSpec(num_sc...  28.3 us
    pallas_call x1, Pallas kernels, run_mixer_backward(): pl.pallas_call(mixer_backward, grid_spec=pltpu.PrefetchScalarGridSpec(num...  16.6 us
    ppermute x1, waiting for transfers between devices, ring_first(): lax.ppermute(v[1], 'dp', shifts[1])  15.9 us
    ppermute x11, starting transfers between devices, z_swap(): return lax.ppermute(v, 'mp', ZLO)  14.7 us
    pallas_call x1, Pallas kernels, run_mixer_forward(): pl.pallas_call(mixer_forward, grid=(t // CH,), in_specs=[pl.BlockSpec(mem...  11.3 us
    pallas_call x2, Pallas kernels, run_place(): pl.pallas_call(place_kernel, grid_spec=pltpu.PrefetchScalarGridSpec(num_s...  11.2 us
    ppermute x21, waiting for transfers between devices, core_swap(): return lax.ppermute(v, 'mp', CORE)  11 us
  transfers between devices with their start and end apart: 42, of which 19 were waited for; matrix products, arithmetic and copies ran while one was open for 5% of the time, Pallas kernels for 34%

profile of v4, /device:TPU:0, one launch (start us, length us, event | category | flops | bytes accessed | tf_op | source)
XLA Modules:
  0.0 284.9 jit_solution(12259311486766023530)
XLA Ops:
  10.6 11.3 %mixer_forward.1 = (bf16[1024,1024]{1,0:T(8,128)(2,1)}, bf16[1024,128]{1,0:T(8,128)(2,1)}, bf16[1024,128]{1,0:T(8,128)(2,1)}, bf16[1024,256]{1,0:T(8,128)(2,1)},...) custom-call(s32[1,8]{1,0:T(1,128)} %len_ref.3, ...), custom_call_target="tpu_custom_call" | custom-call | flops 10000000000 | bytes 1024 | tf_op jit(solution)/shard_map/mixer_forward/pallas_call | solution.py:206
  21.9 12.4 %collective-permute-done.w1_ref = f32[256,1024]{1,0:T(8,128)S(1)} collective-permute-done((f32[256,1024]{1,0:T(8,128)S(1)}, f32[256,1024]{1,0:T(8,128)S(1)}, u32[]{:S(2)}, u32[]{:S(2)}) %collective-permute-start) | collective-permute-done | bytes 1048608 | tf_op jit(solution)/shard_map/out_weights/ppermute | solution.py:66
  38.7 7.0 %before_feed.1 = (bf16[1024,1024]{1,0:T(8,128)(2,1)}, f32[1024,704]{1,0:T(8,128)}) custom-call(bf16[256,1024]{1,0:T(8,128)(2,1)} %refs_14_.1, f32[256,1024]{1,0:T(8,128)} %copy-done.16, f32[256,1024]{1,0:T(8,128)} %copy-done.15, f32[256,1024]{1,0:T(8,128)} %copy-done.17, bf16[1024,1024]{1,0:T(8,128)(2,1)} %base1_ref.1, bf16[704,1024]{1,0:T(8,128)(2,1)} %wd_ref.5), custom_call_target="tpu_custom_call" | custom-call | flops 7000000000 | bytes 1024 | tf_op jit(solution)/shard_map/before_feed/pallas_call | solution.py:236
  45.7 3.3 %collective-permute-done.2.m1_ref = f32[512,256]{1,0:T(8,128)} collective-permute-done((f32[512,256]{1,0:T(8,128)}, f32[512,256]{1,0:T(8,128)}, u32[]{:S(2)}, u32[]{:S(2)}) %collective-permute-start.2) | collective-permute-done | bytes 524320 | tf_op jit(solution)/shard_map/heads_one/ppermute | solution.py:66
  52.1 14.1 %feed_both_ways.2 = (f32[512,1024]{1,0:T(8,128)}, bf16[512,1024]{1,0:T(8,128)(2,1)}, bf16[512,704]{1,0:T(8,128)(2,1)}, bf16[512,1408]{1,0:T(8,128)(2,1)}, f32[25...) custom-call(s32[4]{0:T(128)} %pad_add_fusion.at_ref, ...), custom_call_target="tpu_custom_call" | custom-call | flops 14000000000 | bytes 1024 | tf_op jit(solution)/shard_map/feed_both_ways/pallas_call | solution.py:293
  73.5 14.2 %feed_both_ways.3 = (f32[512,1024]{1,0:T(8,128)}, bf16[512,1024]{1,0:T(8,128)(2,1)}, bf16[512,704]{1,0:T(8,128)(2,1)}, bf16[512,1408]{1,0:T(8,128)(2,1)}, f32[25...) custom-call(s32[4]{0:T(128)} %pad_add_fusion.at_ref, ...), custom_call_target="tpu_custom_call" | custom-call | flops 14000000000 | bytes 1024 | tf_op jit(solution)/shard_map/feed_both_ways/pallas_call | solution.py:293
  94.9 10.4 %feed_weight_grads.1 = f32[4,4,2,32,2176]{4,3,2,1,0:T(8,128)} custom-call(bf16[512,1024]{1,0:T(8,128)(2,1)} %get-tuple-element.238.l0_ref, bf16[512,1024]{1,0:T(8,128)(2,1)} %get-tuple-element.239.l1_ref, bf16[512,1408]{1,0:T(8,128)(2,1)} %get-tuple-element.240.r0_ref, bf16[512,1408]{1,0:T(8,128)(2,1)} %get-tuple-element.241.r1_ref, ...), custom_call_target="tpu_custom_call" | custom-call | flops 12000000000 | bytes 1024 | tf_op jit(solution)/shard_map/feed_weight_grads/pallas_call | solution.py:556
  107.2 4.5 %second_norm_back.1 = (f32[256,1024]{1,0:T(8,128)}, f32[8,1024]{1,0:T(8,128)}) custom-call(s32[4]{0:T(128)} %pad_add_fusion.at_ref, f32[256,1024]{1,0:T(8,128)} %get-tuple-element.233.a0_ref, f32[256,1024]{1,0:T(8,128)} %copy-done.1, f32[128,1024]{1,0:T(8,128)} %collective-permute-done.12.c0_ref, f32[512,1024]{1,0:T(8,128)} %get-tuple-element.245.y0_ref, ...), custom_call_target="tpu_custom_call" | custom-call | flops 3000000000 | bytes 1024 | tf_op jit(solution)/shard_map/second_norm_back/pallas_call | solution.py:469
  114.9 22.9 %collective-permute-done.15.refs_1_ = f32[256,1024]{1,0:T(8,128)} collective-permute-done((f32[256,1024]{1,0:T(8,128)}, f32[256,1024]{1,0:T(8,128)}, u32[]{:S(2)}, u32[]{:S(2)}) %collective-permute-start.15) | collective-permute-done | bytes 1048608 | tf_op jit(solution)/shard_map/second_norm_join/ppermute | solution.py:66
  137.8 3.0 %collective-permute-done.17.refs_3_ = f32[256,1024]{1,0:T(8,128)} collective-permute-done((f32[256,1024]{1,0:T(8,128)}, f32[256,1024]{1,0:T(8,128)}, u32[]{:S(2)}, u32[]{:S(2)}) %collective-permute-start.17) | collective-permute-done | bytes 1048608 | tf_op jit(solution)/shard_map/second_norm_join/ppermute | solution.py:62
  142.3 16.6 %mixer_backward.1 = (bf16[1024,512]{1,0:T(8,128)(2,1)}, f32[128,1024]{1,0:T(8,128)}, f32[128,1024]{1,0:T(8,128)}, f32[128,1024]{1,0:T(8,128)}, f32[128,1024]{1,0...) custom-call(s32[4]{0:T(128)} %pad_add_fusion.at_ref, ...), custom_call_target="tpu_custom_call" | custom-call | flops 16000000000 | bytes 1024 | tf_op jit(solution)/shard_map/mixer_backward/pallas_call | solution.py:416
  160.0 7.9 %mixer_weight_grads.1 = (f32[9,32,768]{2,1,0:T(8,128)}, f32[9,32,768]{2,1,0:T(8,128)}, f32[9,32,768]{2,1,0:T(8,128)}, f32[4,32,768]{2,1,0:T(8,128)}, f32[5,32,768]{2,1,0:T(8,128)}) custom-call(s32[4]{0:T(128)} %pad_add_fusion.at_ref, bf16[1024,1024]{1,0:T(8,128)(2,1)} %get-tuple-element.265.refs_6_.l_ref, bf16[1024,512]{1,0:T(8,128)(2,1)} %get-tuple-element.278.r0_ref, ...), custom_call_target="tpu_custom_call" | custom-call | flops 8000000000 | bytes 1024 | tf_op jit(solution)/shard_map/mixer_weight_grads/pallas_call | solution.py:623
  177.3 15.9 %collective-permute-done.25 = f32[9,32,768]{2,1,0:T(8,128)} collective-permute-done((f32[9,32,768]{2,1,0:T(8,128)}, f32[9,32,768]{2,1,0:T(8,128)}, u32[]{:S(2)}, u32[]{:S(2)}) %collective-permute-start.25) | collective-permute-done | bytes 884768 | tf_op jit(solution)/shard_map/mixer_grads_first/ppermute | solution.py:687
  197.1 3.0 %collective-permute-start.28 = (f32[5,32,768]{2,1,0:T(8,128)}, f32[5,32,768]{2,1,0:T(8,128)}, u32[]{:S(2)}, u32[]{:S(2)}) collective-permute-start(f32[5,32,768]{2,1,0:T(8,128)} %slice_add_fusion), channel_id=1, source_target_pairs={{0,96},{4,100},{8,104},{12,108},{16,112},{20,116},{24,120},{28,124... | collective-permute-start | bytes 1474568 | tf_op jit(solution)/shard_map/mixer_grads_last/ppermute | solution.py:696
  200.1 4.1 %first_norm_back.1.g0_ref = f32[256,1024]{1,0:T(8,128)} custom-call(s32[4]{0:T(128)} %pad_add_fusion.at_ref, f32[512,1024]{1,0:T(8,128)} %get-tuple-element.289.a_ref, f32[128,1024]{1,0:T(8,128)} %collective-permute-done.21.b0_ref, f32[128,1024]{1,0:T(8,128)} %collective-permute-done.22.b1_ref, f32[256,1024]{1,0:T(8,128)} %collective-permute-done.24.c_ref, ...), custom_call_target="tpu_custom_call" | custom-call | flops 3000000000 | bytes 1024 | tf_op jit(solution)/shard_map/first_norm_back/pallas_call | solution.py:495
  204.2 2.8 collective-permute-done.26
  211.7 8.8 %collective-permute-done.23.r0_ref = f32[256,1024]{1,0:T(8,128)} collective-permute-done((f32[256,1024]{1,0:T(8,128)S(1)}, f32[256,1024]{1,0:T(8,128)}, u32[]{:S(2)}, u32[]{:S(2)}) %collective-permute-start.23) | collective-permute-done | bytes 1048608 | tf_op jit(solution)/shard_map/result_join/ppermute | solution.py:66
  221.2 3.0 %collective-permute-start.31 = (f32[5,32,768]{2,1,0:T(8,128)S(1)}, f32[5,32,768]{2,1,0:T(8,128)S(1)}, u32[]{:S(2)}, u32[]{:S(2)}) collective-permute-start(f32[5,32,768]{2,1,0:T(8,128)S(1)} %pad_maximum_fusion.4), channel_id=1, source_target_pairs={{0,8},{4,12},{8,0},{12,4},{16,24},{20,28},{24,16},{28,20},{32,40},... | collective-permute-start | bytes 1474568 | tf_op jit(solution)/shard_map/mixer_grads_two/ppermute | solution.py:822
  225.0 11.0 %collective-permute-done.31 = f32[5,32,768]{2,1,0:T(8,128)S(1)} collective-permute-done((f32[5,32,768]{2,1,0:T(8,128)S(1)}, f32[5,32,768]{2,1,0:T(8,128)S(1)}, u32[]{:S(2)}, u32[]{:S(2)}) %collective-permute-start.31) | collective-permute-done | bytes 491552 | tf_op jit(solution)/shard_map/mixer_grads_two/ppermute | solution.py:822
  236.1 5.6 %place_rows.2 = (bf16[1024,1024]{1,0:T(8,128)(2,1)}, f32[1024,1024]{1,0:T(8,128)}) custom-call(s32[4]{0:T(128)} %pad_add_fusion.at_ref, f32[256,1024]{1,0:T(8,128)} %copy-done.2, f32[256,1024]{1,0:T(8,128)} %first_norm_back.1.g0_ref, f32[256,1024]{1,0:T(8,128)} %collective-permute-done.32.r1_ref, f32[256,1024]{1,0:T(8,128)} %collective-permute-done.33.g1_ref), custom_call_target="tpu_custom_call" | custom-call | flops 3000000000 | bytes 1024 | tf_op jit(solution)/shard_map/place_rows/pallas_call | solution.py:525
  243.4 6.7 %collective-permute-done.34 = f32[3,32,768]{2,1,0:T(8,128)S(1)} collective-permute-done((f32[3,32,768]{2,1,0:T(8,128)S(1)}, f32[3,32,768]{2,1,0:T(8,128)S(1)}, u32[]{:S(2)}, u32[]{:S(2)}) %collective-permute-start.34) | collective-permute-done | bytes 294944 | tf_op jit(solution)/shard_map/mixer_grads_two/ppermute | solution.py:827
  251.0 3.8 %collective-permute-start.36 = (f32[32,1536]{1,0:T(8,128)S(1)}, f32[32,1536]{1,0:T(8,128)S(1)}, u32[]{:S(2)}, u32[]{:S(2)}) collective-permute-start(f32[32,1536]{1,0:T(8,128)S(1)} %get-tuple-element.349), channel_id=1, source_target_pairs={{0,16},{4,20},{8,24},{12,28},{16,0},{20,4},{24,8},{28,12},{32,48},... | collective-permute-start | bytes 589832 | tf_op jit(solution)/shard_map/rows/ppermute | solution.py:834
  256.8 5.6 %place_rows.3 = (bf16[1024,1024]{1,0:T(8,128)(2,1)}, f32[1024,1024]{1,0:T(8,128)}) custom-call(s32[4]{0:T(128)} %pad_add_fusion.at_ref, f32[256,1024]{1,0:T(8,128)} %collective-permute-done.23.r0_ref, f32[256,1024]{1,0:T(8,128)} %collective-permute-done.29.g0_ref, f32[256,1024]{1,0:T(8,128)} %copy-done.13, ...), custom_call_target="tpu_custom_call", output_to_operand_aliasing={{0}: (5, {}), {1}: (6, {})} | custom-call | flops 3000000000 | bytes 1024 | tf_op jit(solution)/shard_map/place_rows/pallas_call | solution.py:525
  266.9 6.9 %collective-permute-done.39.far_ref = f32[32,768]{1,0:T(8,128)S(1)} collective-permute-done((f32[32,768]{1,0:T(8,128)S(1)}, f32[32,768]{1,0:T(8,128)S(1)}, u32[]{:S(2)}, u32[]{:S(2)}) %collective-permute-start.39) | collective-permute-done | bytes 98336 | tf_op jit(solution)/shard_map/small_sums/ppermute | solution.py:66
  (148 shorter events, 65.7 us)
Async XLA Ops:
  7.2 213.3 %reduce-scatter.3.cloned.1.call-start = ((), (), s32[]{:S(2)}) async-start(), calls=%async_computation.2 | async-start | bytes 11141120 | tf_op jit(solution)/shard_map/feed_grads_x/reduce_scatter | solution.py:683
  8.4 13.5 %collective-permute-start.1 = (f32[256,1024]{1,0:T(8,128)S(1)}, f32[256,1024]{1,0:T(8,128)S(1)}, u32[]{:S(2)}, u32[]{:S(2)}) collective-permute-start(f32[256,1024]{1,0:T(8,128)S(1)} %convert_element_type.3), channel_id=1, source_target_pairs={{0,1},{1,0},{2,3},{3,2},{4,5},{5,4},{6,7},{7,6},{8,9},{9,8},{10,11... | collective-permute-start | bytes 3145736 | tf_op jit(solution)/shard_map/out_weights/ppermute | solution.py:62
  8.5 25.8 %collective-permute-start = (f32[256,1024]{1,0:T(8,128)S(1)}, f32[256,1024]{1,0:T(8,128)S(1)}, u32[]{:S(2)}, u32[]{:S(2)}) collective-permute-start(f32[256,1024]{1,0:T(8,128)S(1)} %convert_element_type.3), channel_id=1, source_target_pairs={{0,2},{2,0},{1,3},{3,1},{4,6},{6,4},{5,7},{7,5},{8,10},{10,8},{9,1... | collective-permute-start | bytes 3145736 | tf_op jit(solution)/shard_map/out_weights/ppermute | solution.py:66
  34.3 11.4 %collective-permute-start.3 = (f32[512,256]{1,0:T(8,128)}, f32[512,256]{1,0:T(8,128)}, u32[]{:S(2)}, u32[]{:S(2)}) collective-permute-start(f32[512,256]{1,0:T(8,128)} %get-tuple-element.178.m0_ref.m1_ref), channel_id=1, source_target_pairs={{0,1},{1,0},{2,3},{3,2},{4,5},{5,4},{6,7},{7,6},{8,9},{9,8},{10,11... | collective-permute-start | bytes 1572872 | tf_op jit(solution)/shard_map/heads_one/ppermute | solution.py:62
  34.8 14.2 %collective-permute-start.2 = (f32[512,256]{1,0:T(8,128)}, f32[512,256]{1,0:T(8,128)}, u32[]{:S(2)}, u32[]{:S(2)}) collective-permute-start(f32[512,256]{1,0:T(8,128)} %get-tuple-element.178.m0_ref.m1_ref), channel_id=1, source_target_pairs={{0,2},{2,0},{1,3},{3,1},{4,6},{6,4},{5,7},{7,5},{8,10},{10,8},{9,1... | collective-permute-start | bytes 1572872 | tf_op jit(solution)/shard_map/heads_one/ppermute | solution.py:66
  49.6 16.7 %collective-permute-start.6 = (f32[512,256]{1,0:T(8,128)}, f32[512,256]{1,0:T(8,128)S(1)}, u32[]{:S(2)}, u32[]{:S(2)}) collective-permute-start(f32[512,256]{1,0:T(8,128)} %get-tuple-element.184.m0_ref), channel_id=1, source_target_pairs={{0,2},{2,0},{1,3},{3,1},{4,6},{6,4},{5,7},{7,5},{8,10},{10,8},{9,1... | collective-permute-start | bytes 1572872 | tf_op jit(solution)/shard_map/heads_two/ppermute | solution.py:66
  71.0 16.7 %collective-permute-start.9 = (f32[128,1024]{1,0:T(8,128)S(1)}, f32[128,1024]{1,0:T(8,128)S(1)}, u32[]{:S(2)}, u32[]{:S(2)}) collective-permute-start(f32[128,1024]{1,0:T(8,128)S(1)} %dynamic-slice_add_fusion.7), channel_id=1, source_target_pairs={{0,2},{2,0},{1,3},{3,1},{4,6},{6,4},{5,7},{7,5},{8,10},{10,8},{9,1... | collective-permute-start | bytes 1572872 | tf_op jit(solution)/shard_map/second_norm_z/ppermute | solution.py:66
  92.9 14.3 %collective-permute-start.12 = (f32[128,1024]{1,0:T(8,128)}, f32[128,1024]{1,0:T(8,128)}, u32[]{:S(2)}, u32[]{:S(2)}) collective-permute-start(f32[128,1024]{1,0:T(8,128)} %dynamic-slice_add_fusion.6), channel_id=1, source_target_pairs={{0,2},{2,0},{1,3},{3,1},{4,6},{6,4},{5,7},{7,5},{8,10},{10,8},{9,1... | collective-permute-start | bytes 1572872 | tf_op jit(solution)/shard_map/second_norm_z/ppermute | solution.py:66
  94.4 12.8 %collective-permute-start.13 = (f32[256,1024]{1,0:T(8,128)}, f32[256,1024]{1,0:T(8,128)S(1)}, u32[]{:S(2)}, u32[]{:S(2)}) collective-permute-start(f32[256,1024]{1,0:T(8,128)} %get-tuple-element.236), channel_id=1, source_target_pairs={{0,1},{1,0},{2,3},{3,2},{4,5},{5,4},{6,7},{7,6},{8,9},{9,8},{10,11... | collective-permute-start | bytes 3145736 | tf_op jit(solution)/shard_map/second_norm_z/ppermute | solution.py:62
  94.4 12.8 %collective-permute-start.14 = (f32[256,1024]{1,0:T(8,128)}, f32[256,1024]{1,0:T(8,128)S(1)}, u32[]{:S(2)}, u32[]{:S(2)}) collective-permute-start(f32[256,1024]{1,0:T(8,128)} %get-tuple-element.237), channel_id=1, source_target_pairs={{0,1},{1,0},{2,3},{3,2},{4,5},{5,4},{6,7},{7,6},{8,9},{9,8},{10,11... | collective-permute-start | bytes 3145736 | tf_op jit(solution)/shard_map/second_norm_z/ppermute | solution.py:62
  111.8 150.6 %reduce-scatter.5.cloned.1.call-start = ((), (), s32[]{:S(2)}) async-start(), calls=%async_computation.3 | async-start | bytes 2785280 | tf_op jit(solution)/shard_map/feed_grads_y/reduce_scatter | solution.py:683
  111.9 25.9 %collective-permute-start.15 = (f32[256,1024]{1,0:T(8,128)}, f32[256,1024]{1,0:T(8,128)}, u32[]{:S(2)}, u32[]{:S(2)}) collective-permute-start(f32[256,1024]{1,0:T(8,128)} %get-tuple-element.255.refs_0_.base_ref), channel_id=1, source_target_pairs={{0,2},{2,0},{1,3},{3,1},{4,6},{6,4},{5,7},{7,5},{8,10},{10,8},{9,1... | collective-permute-start | bytes 3145736 | tf_op jit(solution)/shard_map/second_norm_join/ppermute | solution.py:66
  140.8 27.1 %collective-permute-start.18 = (f32[256,1024]{1,0:T(8,128)S(1)}, f32[256,1024]{1,0:T(8,128)S(1)}, u32[]{:S(2)}, u32[]{:S(2)}) collective-permute-start(f32[256,1024]{1,0:T(8,128)S(1)} %pad_maximum_fusion), channel_id=1, source_target_pairs={{0,2},{2,0},{1,3},{3,1},{4,6},{6,4},{5,7},{7,5},{8,10},{10,8},{9,1... | collective-permute-start | bytes 3145736 | tf_op jit(solution)/shard_map/feed_sum/ppermute | solution.py:66
  169.7 23.5 %collective-permute-start.25 = (f32[9,32,768]{2,1,0:T(8,128)}, f32[9,32,768]{2,1,0:T(8,128)}, u32[]{:S(2)}, u32[]{:S(2)}) collective-permute-start(f32[9,32,768]{2,1,0:T(8,128)} %get-tuple-element.302), channel_id=1, source_target_pairs={{0,32},{4,36},{8,40},{12,44},{16,48},{20,52},{24,56},{28,60},{32,6... | collective-permute-start | bytes 2654216 | tf_op jit(solution)/shard_map/mixer_grads_first/ppermute | solution.py:687
  171.4 23.9 %collective-permute-start.27 = (f32[9,32,768]{2,1,0:T(8,128)}, f32[9,32,768]{2,1,0:T(8,128)}, u32[]{:S(2)}, u32[]{:S(2)}) collective-permute-start(f32[9,32,768]{2,1,0:T(8,128)} %get-tuple-element.303), channel_id=1, source_target_pairs={{0,96},{4,100},{8,104},{12,108},{16,112},{20,116},{24,120},{28,124... | collective-permute-start | bytes 2654216 | tf_op jit(solution)/shard_map/mixer_grads_first/ppermute | solution.py:687
  173.0 27.1 %collective-permute-start.24 = (f32[256,1024]{1,0:T(8,128)S(1)}, f32[256,1024]{1,0:T(8,128)}, u32[]{:S(2)}, u32[]{:S(2)}) collective-permute-start(f32[256,1024]{1,0:T(8,128)S(1)} %pad_maximum_fusion.2), channel_id=1, source_target_pairs={{0,2},{2,0},{1,3},{3,1},{4,6},{6,4},{5,7},{7,5},{8,10},{10,8},{9,1... | collective-permute-start | bytes 3145736 | tf_op jit(solution)/shard_map/first_norm_z/ppermute | solution.py:66
  175.9 44.6 %collective-permute-start.23 = (f32[256,1024]{1,0:T(8,128)S(1)}, f32[256,1024]{1,0:T(8,128)}, u32[]{:S(2)}, u32[]{:S(2)}) collective-permute-start(f32[256,1024]{1,0:T(8,128)S(1)} %pad_maximum_fusion.1.r0_ref), channel_id=1, source_target_pairs={{0,2},{2,0},{1,3},{3,1},{4,6},{6,4},{5,7},{7,5},{8,10},{10,8},{9,1... | collective-permute-start | bytes 3145736 | tf_op jit(solution)/shard_map/result_join/ppermute | solution.py:66
  195.0 12.0 %collective-permute-start.26 = (f32[4,32,768]{2,1,0:T(8,128)}, f32[4,32,768]{2,1,0:T(8,128)S(1)}, u32[]{:S(2)}, u32[]{:S(2)}) collective-permute-start(f32[4,32,768]{2,1,0:T(8,128)} %slice_add_fusion.3), channel_id=1, source_target_pairs={{0,32},{4,36},{8,40},{12,44},{16,48},{20,52},{24,56},{28,60},{32,6... | collective-permute-start | bytes 1179656 | tf_op jit(solution)/shard_map/mixer_grads_last/ppermute | solution.py:696
  197.1 13.3 %collective-permute-start.28 = (f32[5,32,768]{2,1,0:T(8,128)}, f32[5,32,768]{2,1,0:T(8,128)}, u32[]{:S(2)}, u32[]{:S(2)}) collective-permute-start(f32[5,32,768]{2,1,0:T(8,128)} %slice_add_fusion), channel_id=1, source_target_pairs={{0,96},{4,100},{8,104},{12,108},{16,112},{20,116},{24,120},{28,124... | collective-permute-start | bytes 1474568 | tf_op jit(solution)/shard_map/mixer_grads_last/ppermute | solution.py:696
  220.5 15.6 %collective-permute-start.32 = (f32[256,1024]{1,0:T(8,128)S(1)}, f32[256,1024]{1,0:T(8,128)}, u32[]{:S(2)}, u32[]{:S(2)}) collective-permute-start(f32[256,1024]{1,0:T(8,128)S(1)} %pad_maximum_fusion.1.r0_ref), channel_id=1, source_target_pairs={{0,1},{1,0},{2,3},{3,2},{4,5},{5,4},{6,7},{7,6},{8,9},{9,8},{10,11... | collective-permute-start | bytes 3145736 | tf_op jit(solution)/shard_map/result_join/ppermute | solution.py:62
  220.6 15.5 %collective-permute-start.33 = (f32[256,1024]{1,0:T(8,128)}, f32[256,1024]{1,0:T(8,128)}, u32[]{:S(2)}, u32[]{:S(2)}) collective-permute-start(f32[256,1024]{1,0:T(8,128)} %first_norm_back.1.g0_ref), channel_id=1, source_target_pairs={{0,1},{1,0},{2,3},{3,2},{4,5},{5,4},{6,7},{7,6},{8,9},{9,8},{10,11... | collective-permute-start | bytes 3145736 | tf_op jit(solution)/shard_map/grad_join/ppermute | solution.py:62
  221.2 14.8 %collective-permute-start.31 = (f32[5,32,768]{2,1,0:T(8,128)S(1)}, f32[5,32,768]{2,1,0:T(8,128)S(1)}, u32[]{:S(2)}, u32[]{:S(2)}) collective-permute-start(f32[5,32,768]{2,1,0:T(8,128)S(1)} %pad_maximum_fusion.4), channel_id=1, source_target_pairs={{0,8},{4,12},{8,0},{12,4},{16,24},{20,28},{24,16},{28,20},{32,40},... | collective-permute-start | bytes 1474568 | tf_op jit(solution)/shard_map/mixer_grads_two/ppermute | solution.py:822
  224.2 25.9 %collective-permute-start.29 = (f32[256,1024]{1,0:T(8,128)}, f32[256,1024]{1,0:T(8,128)}, u32[]{:S(2)}, u32[]{:S(2)}) collective-permute-start(f32[256,1024]{1,0:T(8,128)} %first_norm_back.1.g0_ref), channel_id=1, source_target_pairs={{0,2},{2,0},{1,3},{3,1},{4,6},{6,4},{5,7},{7,5},{8,10},{10,8},{9,1... | collective-permute-start | bytes 3145736 | tf_op jit(solution)/shard_map/grad_join/ppermute | solution.py:66
  243.4 11.4 %collective-permute-start.30 = (f32[256,1024]{1,0:T(8,128)}, f32[256,1024]{1,0:T(8,128)S(1)}, u32[]{:S(2)}, u32[]{:S(2)}) collective-permute-start(f32[256,1024]{1,0:T(8,128)} %collective-permute-done.23.r0_ref), channel_id=1, source_target_pairs={{0,1},{1,0},{2,3},{3,2},{4,5},{5,4},{6,7},{7,6},{8,9},{9,8},{10,11... | collective-permute-start | bytes 3145736 | tf_op jit(solution)/shard_map/result_join/ppermute | solution.py:62
  (41 other events, 304.6 us)
Sparse Core Ops, SparseCore 0:
  111.9 86.6 reduce-scatter.2
  220.6 31.1 reduce-scatter.4

commit v5 on v4

--- a/solution.py
+++ b/solution.py
@@ -808,39 +808,40 @@
     with jax.named_scope("mixer_grads_last"):
         c_last = ring_last(ring_on(c, c_got), YS)
         c = ring_total(c, c_got, c_last)
-    feed1, grad0, c, feed_own, a = phase(feed1, grad0, c, feed_own, a)
-
     with jax.named_scope("grad_join"):
-        grad1 = z_swap(grad0)
         grad2 = core_swap(grad0)
     with jax.named_scope("result_join"):
         feed2 = core_swap(feed_own)
+    feed1, feed2, grad0, grad2, c, feed_own, a = phase(feed1, feed2, grad0, grad2, c, feed_own, a)
+
+    with jax.named_scope("grad_join"):
+        grad1 = z_swap(grad0)
     with jax.named_scope("feed_grads_y"):
         a = scatter_rows(a, GY).reshape(2, 32, -1)
     with jax.named_scope("mixer_grads_two"):
-        x_pair, x_one = ix // 2, ix % 2
-        c_far = lax.ppermute(jnp.concatenate([rows_of(c, 4 * (1 - x_pair), 4), c[8:9]], axis=0), "dp", XS[2])
-    placed = run_place(at, 0, after((feed_own, grad0, feed2, grad2), c))
+
+        def with_small(i):
+            return jnp.concatenate([rows_of(c, 2 * (i % 4), 2), c[8:9]], axis=0)
+
+        c_second = [with_small(ix)] + [send(with_small(ix + k), XS, k) for k in (1, 3, 2)]
+    placed = run_place(at, 0, (feed_own, grad0, feed2, grad2))
     with jax.named_scope("mixer_grads_two"):
-        c = jnp.concatenate([rows_of(c, 4 * x_pair, 4), c[8:9]], axis=0) + c_far
-        c = after(c, placed)
-        c_near = lax.ppermute(jnp.concatenate([rows_of(c, 2 * (1 - x_one), 2), c[4:5]], axis=0), "dp", X_PAIR)
-        c = jnp.concatenate([rows_of(c, 2 * x_one, 2), c[4:5]], axis=0) + c_near
+        c = sum(after(c_second, placed))
     with jax.named_scope("rows"):
-        turned_c = after(c, grad1)
-        c = turned_c
+        c = after(c, (grad1, placed))
         turned = lambda i: jnp.concatenate([pick(c, i, 0), c[2]], axis=1)
         own = turned(zh)
         got = lax.ppermute(turned(1 - zh), "dp", ZH)
         a_own = pick(a, zh, 0)
-        a_got = lax.ppermute(after(pick(a, 1 - zh, 0), c), "dp", ZH)
+        a_out = after(pick(a, 1 - zh, 0), c)
+        a_got = lax.ppermute(a_out, "dp", ZH)
     with jax.named_scope("result_join"):
         feed3 = core_swap(feed1)
     with jax.named_scope("grad_join"):
         grad3 = core_swap(after(grad1, c))
-    result, grad_tokens = run_place(at, 1, (feed1, grad1, feed3, grad3), placed)
+    result, grad_tokens = run_place(at, 1, after((feed1, grad1, feed3, grad3), a_out), placed)
     with jax.named_scope("small_sums"):
-        got = after(got, result)
+        got = after(got, (result, a_got))
         sums = own[:, 768:1536] + got[:, 768:1536]
         sums = sums + core_swap(sums)
         far = z_swap(sums)

time: 286 us -> 281 us (0.983)
  waiting for transfers between devices: 107 us -> 99.4 us
  starting transfers between devices: 34.7 us -> 38.7 us
    ppermute x3 -> x4, waiting for transfers between devices: 19.1 us -> 3.89 us  [the longest x3 3.67 us: send(): return lax.ppermute(v, 'dp', shifts[d])]
    ppermute x1, waiting for transfers between devices: 2.31 us -> 8.59 us  [ring_last(): lax.ppermute(on[1], 'dp', shifts[3])]
    ppermute x3 -> x4, starting transfers between devices: 5.77 us -> 9.77 us  [the longest x3 6.6 us: send(): return lax.ppermute(v, 'dp', shifts[d])]
    reduce_scatter x2, waiting for transfers between devices: 0.02 us -> 3.29 us  [scatter_rows(): lax.psum_scatter(v, 'dp', scatter_dimension=0, tiled=True, axis_index_gro...]
  transfers between devices with their start and end apart: 42 -> 43, of which waited for: 19 -> 22; matrix products, arithmetic and copies ran while one was open for 5% -> 5% of each run, Pallas kernels for 34% -> 35%
where the time goes in v5:
time: 281 us; the launch traced here: 280 us
  Pallas kernels  103 us (37%)
  waiting for transfers between devices  99.4 us (35%)
  starting transfers between devices  38.7 us (14%)
  other arithmetic  17.5 us (6%)
  between operations  14.5 us (5%)
  local copies, waits for them, and re-layouts  6.2 us (2%)
    ppermute x11, waiting for transfers between devices, z_swap(): return lax.ppermute(v, 'mp', ZLO)  54.6 us
    pallas_call x2, Pallas kernels, run_feed(): pl.pallas_call(feed_kernel, grid_spec=pltpu.PrefetchScalarGridSpec(num_sc...  28.3 us
    pallas_call x1, Pallas kernels, run_mixer_backward(): pl.pallas_call(mixer_backward, grid_spec=pltpu.PrefetchScalarGridSpec(num...  16.6 us
    ppermute x11, starting transfers between devices, z_swap(): return lax.ppermute(v, 'mp', ZLO)  16 us
    ppermute x1, waiting for transfers between devices, ring_first(): lax.ppermute(v[1], 'dp', shifts[1])  15.7 us
    pallas_call x1, Pallas kernels, run_mixer_forward(): pl.pallas_call(mixer_forward, grid=(t // CH,), in_specs=[pl.BlockSpec(mem...  11.4 us
    pallas_call x2, Pallas kernels, run_place(): pl.pallas_call(place_kernel, grid_spec=pltpu.PrefetchScalarGridSpec(num_s...  11.2 us
    ppermute x21, waiting for transfers between devices, core_swap(): return lax.ppermute(v, 'mp', CORE)  11.1 us
  transfers between devices with their start and end apart: 43, of which 22 were waited for; matrix products, arithmetic and copies ran while one was open for 5% of the time, Pallas kernels for 35%

profile of v5, /device:TPU:0, one launch (start us, length us, event | category | flops | bytes accessed | tf_op | source)
XLA Modules:
  0.0 279.6 jit_solution(64484642596360249)
XLA Ops:
  10.6 11.4 %mixer_forward.1 = (bf16[1024,1024]{1,0:T(8,128)(2,1)}, bf16[1024,128]{1,0:T(8,128)(2,1)}, bf16[1024,128]{1,0:T(8,128)(2,1)}, bf16[1024,256]{1,0:T(8,128)(2,1)},...) custom-call(s32[1,8]{1,0:T(1,128)} %len_ref.3, ...), custom_call_target="tpu_custom_call" | custom-call | flops 10000000000 | bytes 1024 | tf_op jit(solution)/shard_map/mixer_forward/pallas_call | solution.py:206
  21.9 12.4 %collective-permute-done.w1_ref = f32[256,1024]{1,0:T(8,128)S(1)} collective-permute-done((f32[256,1024]{1,0:T(8,128)S(1)}, f32[256,1024]{1,0:T(8,128)S(1)}, u32[]{:S(2)}, u32[]{:S(2)}) %collective-permute-start) | collective-permute-done | bytes 1048608 | tf_op jit(solution)/shard_map/out_weights/ppermute | solution.py:66
  38.7 7.0 %before_feed.1 = (bf16[1024,1024]{1,0:T(8,128)(2,1)}, f32[1024,704]{1,0:T(8,128)}) custom-call(bf16[256,1024]{1,0:T(8,128)(2,1)} %refs_14_.1, f32[256,1024]{1,0:T(8,128)} %copy-done.17, f32[256,1024]{1,0:T(8,128)} %copy-done.16, f32[256,1024]{1,0:T(8,128)} %copy-done.18, bf16[1024,1024]{1,0:T(8,128)(2,1)} %base1_ref.1, bf16[704,1024]{1,0:T(8,128)(2,1)} %wd_ref.5), custom_call_target="tpu_custom_call" | custom-call | flops 7000000000 | bytes 1024 | tf_op jit(solution)/shard_map/before_feed/pallas_call | solution.py:236
  45.7 3.3 %collective-permute-done.2.m1_ref = f32[512,256]{1,0:T(8,128)} collective-permute-done((f32[512,256]{1,0:T(8,128)}, f32[512,256]{1,0:T(8,128)}, u32[]{:S(2)}, u32[]{:S(2)}) %collective-permute-start.2) | collective-permute-done | bytes 524320 | tf_op jit(solution)/shard_map/heads_one/ppermute | solution.py:66
  52.1 14.1 %feed_both_ways.2 = (f32[512,1024]{1,0:T(8,128)}, bf16[512,1024]{1,0:T(8,128)(2,1)}, bf16[512,704]{1,0:T(8,128)(2,1)}, bf16[512,1408]{1,0:T(8,128)(2,1)}, f32[25...) custom-call(s32[4]{0:T(128)} %pad_add_fusion.at_ref, ...), custom_call_target="tpu_custom_call" | custom-call | flops 14000000000 | bytes 1024 | tf_op jit(solution)/shard_map/feed_both_ways/pallas_call | solution.py:293
  73.5 14.2 %feed_both_ways.3 = (f32[512,1024]{1,0:T(8,128)}, bf16[512,1024]{1,0:T(8,128)(2,1)}, bf16[512,704]{1,0:T(8,128)(2,1)}, bf16[512,1408]{1,0:T(8,128)(2,1)}, f32[25...) custom-call(s32[4]{0:T(128)} %pad_add_fusion.at_ref, ...), custom_call_target="tpu_custom_call" | custom-call | flops 14000000000 | bytes 1024 | tf_op jit(solution)/shard_map/feed_both_ways/pallas_call | solution.py:293
  94.9 10.4 %feed_weight_grads.1 = f32[4,4,2,32,2176]{4,3,2,1,0:T(8,128)} custom-call(bf16[512,1024]{1,0:T(8,128)(2,1)} %get-tuple-element.243.l0_ref, bf16[512,1024]{1,0:T(8,128)(2,1)} %get-tuple-element.244.l1_ref, bf16[512,1408]{1,0:T(8,128)(2,1)} %get-tuple-element.245.r0_ref, bf16[512,1408]{1,0:T(8,128)(2,1)} %get-tuple-element.246.r1_ref, ...), custom_call_target="tpu_custom_call" | custom-call | flops 12000000000 | bytes 1024 | tf_op jit(solution)/shard_map/feed_weight_grads/pallas_call | solution.py:556
  107.2 4.5 %second_norm_back.1 = (f32[256,1024]{1,0:T(8,128)}, f32[8,1024]{1,0:T(8,128)}) custom-call(s32[4]{0:T(128)} %pad_add_fusion.at_ref, f32[256,1024]{1,0:T(8,128)} %get-tuple-element.238.a0_ref, f32[256,1024]{1,0:T(8,128)} %copy-done.1, f32[128,1024]{1,0:T(8,128)} %collective-permute-done.12.c0_ref, f32[512,1024]{1,0:T(8,128)} %get-tuple-element.250.y0_ref, ...), custom_call_target="tpu_custom_call" | custom-call | flops 3000000000 | bytes 1024 | tf_op jit(solution)/shard_map/second_norm_back/pallas_call | solution.py:469
  114.9 22.9 %collective-permute-done.15.refs_1_ = f32[256,1024]{1,0:T(8,128)} collective-permute-done((f32[256,1024]{1,0:T(8,128)}, f32[256,1024]{1,0:T(8,128)}, u32[]{:S(2)}, u32[]{:S(2)}) %collective-permute-start.15) | collective-permute-done | bytes 1048608 | tf_op jit(solution)/shard_map/second_norm_join/ppermute | solution.py:66
  137.8 3.0 %collective-permute-done.17.refs_3_ = f32[256,1024]{1,0:T(8,128)} collective-permute-done((f32[256,1024]{1,0:T(8,128)}, f32[256,1024]{1,0:T(8,128)}, u32[]{:S(2)}, u32[]{:S(2)}) %collective-permute-start.17) | collective-permute-done | bytes 1048608 | tf_op jit(solution)/shard_map/second_norm_join/ppermute | solution.py:62
  142.3 16.6 %mixer_backward.1 = (bf16[1024,512]{1,0:T(8,128)(2,1)}, f32[128,1024]{1,0:T(8,128)}, f32[128,1024]{1,0:T(8,128)}, f32[128,1024]{1,0:T(8,128)}, f32[128,1024]{1,0...) custom-call(s32[4]{0:T(128)} %pad_add_fusion.at_ref, ...), custom_call_target="tpu_custom_call" | custom-call | flops 16000000000 | bytes 1024 | tf_op jit(solution)/shard_map/mixer_backward/pallas_call | solution.py:416
  159.9 7.9 %mixer_weight_grads.1 = (f32[9,32,768]{2,1,0:T(8,128)}, f32[9,32,768]{2,1,0:T(8,128)}, f32[9,32,768]{2,1,0:T(8,128)}, f32[4,32,768]{2,1,0:T(8,128)}, f32[5,32,768]{2,1,0:T(8,128)}) custom-call(s32[4]{0:T(128)} %pad_add_fusion.at_ref, bf16[1024,1024]{1,0:T(8,128)(2,1)} %get-tuple-element.270.refs_6_.l_ref, bf16[1024,512]{1,0:T(8,128)(2,1)} %get-tuple-element.283.r0_ref, ...), custom_call_target="tpu_custom_call" | custom-call | flops 8000000000 | bytes 1024 | tf_op jit(solution)/shard_map/mixer_weight_grads/pallas_call | solution.py:623
  177.9 15.7 %collective-permute-done.27 = f32[9,32,768]{2,1,0:T(8,128)} collective-permute-done((f32[9,32,768]{2,1,0:T(8,128)}, f32[9,32,768]{2,1,0:T(8,128)}, u32[]{:S(2)}, u32[]{:S(2)}) %collective-permute-start.27) | collective-permute-done | bytes 884768 | tf_op jit(solution)/shard_map/mixer_grads_first/ppermute | solution.py:687
  197.9 4.1 %first_norm_back.1.g0_ref = f32[256,1024]{1,0:T(8,128)} custom-call(s32[4]{0:T(128)} %pad_add_fusion.at_ref, f32[512,1024]{1,0:T(8,128)} %get-tuple-element.294.a_ref, f32[128,1024]{1,0:T(8,128)} %collective-permute-done.21.b0_ref, f32[128,1024]{1,0:T(8,128)} %collective-permute-done.22.b1_ref, f32[256,1024]{1,0:T(8,128)} %collective-permute-done.25.c_ref, ...), custom_call_target="tpu_custom_call" | custom-call | flops 3000000000 | bytes 1024 | tf_op jit(solution)/shard_map/first_norm_back/pallas_call | solution.py:495
  208.4 8.6 %collective-permute-done.30 = f32[5,32,768]{2,1,0:T(8,128)S(1)} collective-permute-done((f32[5,32,768]{2,1,0:T(8,128)S(1)}, f32[5,32,768]{2,1,0:T(8,128)S(1)}, u32[]{:S(2)}, u32[]{:S(2)}) %collective-permute-start.30) | collective-permute-done | bytes 491552 | tf_op jit(solution)/shard_map/mixer_grads_last/ppermute | solution.py:696
  220.1 3.4 %collective-permute-start.35 = (f32[3,32,768]{2,1,0:T(8,128)S(1)}, f32[3,32,768]{2,1,0:T(8,128)S(1)}, u32[]{:S(2)}, u32[]{:S(2)}) collective-permute-start(f32[3,32,768]{2,1,0:T(8,128)S(1)} %get-tuple-element.361), channel_id=1, source_target_pairs={{0,8},{4,12},{8,0},{12,4},{16,24},{20,28},{24,16},{28,20},{32,40},... | collective-permute-start | bytes 884744 | tf_op jit(solution)/shard_map/mixer_grads_two/ppermute | solution.py:675
  226.7 5.7 %place_rows.2 = (bf16[1024,1024]{1,0:T(8,128)(2,1)}, f32[1024,1024]{1,0:T(8,128)}) custom-call(s32[4]{0:T(128)} %pad_add_fusion.at_ref, f32[256,1024]{1,0:T(8,128)} %copy-done.2, f32[256,1024]{1,0:T(8,128)} %first_norm_back.1.g0_ref, f32[256,1024]{1,0:T(8,128)} %collective-permute-done.24.r1_ref, f32[256,1024]{1,0:T(8,128)} %collective-permute-done.26.g1_ref), custom_call_target="tpu_custom_call" | custom-call | flops 3000000000 | bytes 1024 | tf_op jit(solution)/shard_map/place_rows/pallas_call | solution.py:525
  232.3 3.5 %collective-permute-done.33 = f32[3,32,768]{2,1,0:T(8,128)S(1)} collective-permute-done((f32[3,32,768]{2,1,0:T(8,128)S(1)}, f32[3,32,768]{2,1,0:T(8,128)S(1)}, u32[]{:S(2)}, u32[]{:S(2)}) %collective-permute-start.33) | collective-permute-done | bytes 294944 | tf_op jit(solution)/shard_map/mixer_grads_two/ppermute | solution.py:675
  236.1 7.5 %collective-permute-done.31.g0_ref = f32[256,1024]{1,0:T(8,128)S(1)} collective-permute-done((f32[256,1024]{1,0:T(8,128)}, f32[256,1024]{1,0:T(8,128)S(1)}, u32[]{:S(2)}, u32[]{:S(2)}) %collective-permute-start.31) | collective-permute-done | bytes 1048608 | tf_op jit(solution)/shard_map/grad_join/ppermute | solution.py:66
  244.3 4.2 %collective-permute-start.37 = (f32[32,1536]{1,0:T(8,128)S(1)}, f32[32,1536]{1,0:T(8,128)S(1)}, u32[]{:S(2)}, u32[]{:S(2)}) collective-permute-start(f32[32,1536]{1,0:T(8,128)S(1)} %get-tuple-element.359), channel_id=1, source_target_pairs={{0,16},{4,20},{8,24},{12,28},{16,0},{20,4},{24,8},{28,12},{32,48},... | collective-permute-start | bytes 589832 | tf_op jit(solution)/shard_map/rows/ppermute | solution.py:834
  248.5 3.3 %reduce-scatter.5.cloned.1.call-done = f32[64,2176]{1,0:T(8,128)} async-done(((f32[256,2176]{1,0:T(8,128)}), f32[64,2176]{1,0:T(8,128)}) %reduce-scatter.5.cloned.1.call-update) | async-done | bytes 557072 | tf_op jit(solution)/shard_map/feed_grads_y/reduce_scatter | solution.py:683
  253.6 3.2 %collective-permute-start.38 = (f32[32,2176]{1,0:T(8,128)S(1)}, f32[32,2176]{1,0:T(8,128)S(1)}, u32[]{:S(2)}, u32[]{:S(2)}) collective-permute-start(f32[32,2176]{1,0:T(8,128)S(1)} %get-tuple-element.326), channel_id=1, source_target_pairs={{0,16},{4,20},{8,24},{12,28},{16,0},{20,4},{24,8},{28,12},{32,48},... | collective-permute-start | bytes 835592 | tf_op jit(solution)/shard_map/rows/ppermute | solution.py:837
  257.8 5.6 %place_rows.3 = (bf16[1024,1024]{1,0:T(8,128)(2,1)}, f32[1024,1024]{1,0:T(8,128)}) custom-call(s32[4]{0:T(128)} %pad_add_fusion.at_ref, f32[256,1024]{1,0:T(8,128)} %collective-permute-done.23.r0_ref, f32[256,1024]{1,0:T(8,128)} %copy-done.14, f32[256,1024]{1,0:T(8,128)} %collective-permute-done.32.r1_ref, ...), custom_call_target="tpu_custom_call", output_to_operand_aliasing={{0}: (5, {}), {1}: (6, {})} | custom-call | flops 3000000000 | bytes 1024 | tf_op jit(solution)/shard_map/place_rows/pallas_call | solution.py:525
  266.7 3.3 %collective-permute-done.40.far_ref = f32[32,768]{1,0:T(8,128)S(1)} collective-permute-done((f32[32,768]{1,0:T(8,128)S(1)}, f32[32,768]{1,0:T(8,128)S(1)}, u32[]{:S(2)}, u32[]{:S(2)}) %collective-permute-start.40) | collective-permute-done | bytes 98336 | tf_op jit(solution)/shard_map/small_sums/ppermute | solution.py:66
  (148 shorter events, 69.6 us)
Async XLA Ops:
  7.2 212.1 %reduce-scatter.3.cloned.1.call-start = ((), (), s32[]{:S(2)}) async-start(), calls=%async_computation.2 | async-start | bytes 11141120 | tf_op jit(solution)/shard_map/feed_grads_x/reduce_scatter | solution.py:683
  8.4 13.5 %collective-permute-start.1 = (f32[256,1024]{1,0:T(8,128)S(1)}, f32[256,1024]{1,0:T(8,128)S(1)}, u32[]{:S(2)}, u32[]{:S(2)}) collective-permute-start(f32[256,1024]{1,0:T(8,128)S(1)} %convert_element_type.3), channel_id=1, source_target_pairs={{0,1},{1,0},{2,3},{3,2},{4,5},{5,4},{6,7},{7,6},{8,9},{9,8},{10,11... | collective-permute-start | bytes 3145736 | tf_op jit(solution)/shard_map/out_weights/ppermute | solution.py:62
  8.5 25.8 %collective-permute-start = (f32[256,1024]{1,0:T(8,128)S(1)}, f32[256,1024]{1,0:T(8,128)S(1)}, u32[]{:S(2)}, u32[]{:S(2)}) collective-permute-start(f32[256,1024]{1,0:T(8,128)S(1)} %convert_element_type.3), channel_id=1, source_target_pairs={{0,2},{2,0},{1,3},{3,1},{4,6},{6,4},{5,7},{7,5},{8,10},{10,8},{9,1... | collective-permute-start | bytes 3145736 | tf_op jit(solution)/shard_map/out_weights/ppermute | solution.py:66
  34.8 14.2 %collective-permute-start.2 = (f32[512,256]{1,0:T(8,128)}, f32[512,256]{1,0:T(8,128)}, u32[]{:S(2)}, u32[]{:S(2)}) collective-permute-start(f32[512,256]{1,0:T(8,128)} %get-tuple-element.183.m0_ref.m1_ref), channel_id=1, source_target_pairs={{0,2},{2,0},{1,3},{3,1},{4,6},{6,4},{5,7},{7,5},{8,10},{10,8},{9,1... | collective-permute-start | bytes 1572872 | tf_op jit(solution)/shard_map/heads_one/ppermute | solution.py:66
  49.6 16.7 %collective-permute-start.6 = (f32[512,256]{1,0:T(8,128)}, f32[512,256]{1,0:T(8,128)S(1)}, u32[]{:S(2)}, u32[]{:S(2)}) collective-permute-start(f32[512,256]{1,0:T(8,128)} %get-tuple-element.189.m0_ref), channel_id=1, source_target_pairs={{0,2},{2,0},{1,3},{3,1},{4,6},{6,4},{5,7},{7,5},{8,10},{10,8},{9,1... | collective-permute-start | bytes 1572872 | tf_op jit(solution)/shard_map/heads_two/ppermute | solution.py:66
  71.0 16.7 %collective-permute-start.9 = (f32[128,1024]{1,0:T(8,128)S(1)}, f32[128,1024]{1,0:T(8,128)S(1)}, u32[]{:S(2)}, u32[]{:S(2)}) collective-permute-start(f32[128,1024]{1,0:T(8,128)S(1)} %dynamic-slice_add_fusion.7), channel_id=1, source_target_pairs={{0,2},{2,0},{1,3},{3,1},{4,6},{6,4},{5,7},{7,5},{8,10},{10,8},{9,1... | collective-permute-start | bytes 1572872 | tf_op jit(solution)/shard_map/second_norm_z/ppermute | solution.py:66
  92.9 14.3 %collective-permute-start.12 = (f32[128,1024]{1,0:T(8,128)}, f32[128,1024]{1,0:T(8,128)}, u32[]{:S(2)}, u32[]{:S(2)}) collective-permute-start(f32[128,1024]{1,0:T(8,128)} %dynamic-slice_add_fusion.6), channel_id=1, source_target_pairs={{0,2},{2,0},{1,3},{3,1},{4,6},{6,4},{5,7},{7,5},{8,10},{10,8},{9,1... | collective-permute-start | bytes 1572872 | tf_op jit(solution)/shard_map/second_norm_z/ppermute | solution.py:66
  94.4 12.8 %collective-permute-start.13 = (f32[256,1024]{1,0:T(8,128)}, f32[256,1024]{1,0:T(8,128)S(1)}, u32[]{:S(2)}, u32[]{:S(2)}) collective-permute-start(f32[256,1024]{1,0:T(8,128)} %get-tuple-element.241), channel_id=1, source_target_pairs={{0,1},{1,0},{2,3},{3,2},{4,5},{5,4},{6,7},{7,6},{8,9},{9,8},{10,11... | collective-permute-start | bytes 3145736 | tf_op jit(solution)/shard_map/second_norm_z/ppermute | solution.py:62
  94.4 12.8 %collective-permute-start.14 = (f32[256,1024]{1,0:T(8,128)}, f32[256,1024]{1,0:T(8,128)S(1)}, u32[]{:S(2)}, u32[]{:S(2)}) collective-permute-start(f32[256,1024]{1,0:T(8,128)} %get-tuple-element.242), channel_id=1, source_target_pairs={{0,1},{1,0},{2,3},{3,2},{4,5},{5,4},{6,7},{7,6},{8,9},{9,8},{10,11... | collective-permute-start | bytes 3145736 | tf_op jit(solution)/shard_map/second_norm_z/ppermute | solution.py:62
  111.8 140.1 %reduce-scatter.5.cloned.1.call-start = ((), (), s32[]{:S(2)}) async-start(), calls=%async_computation.3 | async-start | bytes 2785280 | tf_op jit(solution)/shard_map/feed_grads_y/reduce_scatter | solution.py:683
  111.9 25.9 %collective-permute-start.15 = (f32[256,1024]{1,0:T(8,128)}, f32[256,1024]{1,0:T(8,128)}, u32[]{:S(2)}, u32[]{:S(2)}) collective-permute-start(f32[256,1024]{1,0:T(8,128)} %get-tuple-element.260.refs_0_.base_ref), channel_id=1, source_target_pairs={{0,2},{2,0},{1,3},{3,1},{4,6},{6,4},{5,7},{7,5},{8,10},{10,8},{9,1... | collective-permute-start | bytes 3145736 | tf_op jit(solution)/shard_map/second_norm_join/ppermute | solution.py:66
  140.8 27.1 %collective-permute-start.18 = (f32[256,1024]{1,0:T(8,128)S(1)}, f32[256,1024]{1,0:T(8,128)S(1)}, u32[]{:S(2)}, u32[]{:S(2)}) collective-permute-start(f32[256,1024]{1,0:T(8,128)S(1)} %pad_maximum_fusion), channel_id=1, source_target_pairs={{0,2},{2,0},{1,3},{3,1},{4,6},{6,4},{5,7},{7,5},{8,10},{10,8},{9,1... | collective-permute-start | bytes 3145736 | tf_op jit(solution)/shard_map/feed_sum/ppermute | solution.py:66
  170.1 23.5 %collective-permute-start.27 = (f32[9,32,768]{2,1,0:T(8,128)}, f32[9,32,768]{2,1,0:T(8,128)}, u32[]{:S(2)}, u32[]{:S(2)}) collective-permute-start(f32[9,32,768]{2,1,0:T(8,128)} %get-tuple-element.307), channel_id=1, source_target_pairs={{0,32},{4,36},{8,40},{12,44},{16,48},{20,52},{24,56},{28,60},{32,6... | collective-permute-start | bytes 2654216 | tf_op jit(solution)/shard_map/mixer_grads_first/ppermute | solution.py:687
  171.8 26.2 %collective-permute-start.25 = (f32[256,1024]{1,0:T(8,128)S(1)}, f32[256,1024]{1,0:T(8,128)}, u32[]{:S(2)}, u32[]{:S(2)}) collective-permute-start(f32[256,1024]{1,0:T(8,128)S(1)} %pad_maximum_fusion.2), channel_id=1, source_target_pairs={{0,2},{2,0},{1,3},{3,1},{4,6},{6,4},{5,7},{7,5},{8,10},{10,8},{9,1... | collective-permute-start | bytes 3145736 | tf_op jit(solution)/shard_map/first_norm_z/ppermute | solution.py:66
  172.4 29.6 %collective-permute-start.29 = (f32[9,32,768]{2,1,0:T(8,128)}, f32[9,32,768]{2,1,0:T(8,128)}, u32[]{:S(2)}, u32[]{:S(2)}) collective-permute-start(f32[9,32,768]{2,1,0:T(8,128)} %get-tuple-element.308), channel_id=1, source_target_pairs={{0,96},{4,100},{8,104},{12,108},{16,112},{20,116},{24,120},{28,124... | collective-permute-start | bytes 2654216 | tf_op jit(solution)/shard_map/mixer_grads_first/ppermute | solution.py:687
  176.4 41.8 %collective-permute-start.24 = (f32[256,1024]{1,0:T(8,128)S(1)}, f32[256,1024]{1,0:T(8,128)}, u32[]{:S(2)}, u32[]{:S(2)}) collective-permute-start(f32[256,1024]{1,0:T(8,128)S(1)} %pad_maximum_fusion.1.r0_ref), channel_id=1, source_target_pairs={{0,1},{1,0},{2,3},{3,2},{4,5},{5,4},{6,7},{7,6},{8,9},{9,8},{10,11... | collective-permute-start | bytes 3145736 | tf_op jit(solution)/shard_map/result_join/ppermute | solution.py:62
  176.5 42.7 %collective-permute-start.23 = (f32[256,1024]{1,0:T(8,128)S(1)}, f32[256,1024]{1,0:T(8,128)}, u32[]{:S(2)}, u32[]{:S(2)}) collective-permute-start(f32[256,1024]{1,0:T(8,128)S(1)} %pad_maximum_fusion.1.r0_ref), channel_id=1, source_target_pairs={{0,2},{2,0},{1,3},{3,1},{4,6},{6,4},{5,7},{7,5},{8,10},{10,8},{9,1... | collective-permute-start | bytes 3145736 | tf_op jit(solution)/shard_map/result_join/ppermute | solution.py:66
  202.0 17.2 %collective-permute-start.26 = (f32[256,1024]{1,0:T(8,128)}, f32[256,1024]{1,0:T(8,128)}, u32[]{:S(2)}, u32[]{:S(2)}) collective-permute-start(f32[256,1024]{1,0:T(8,128)} %first_norm_back.1.g0_ref), channel_id=1, source_target_pairs={{0,1},{1,0},{2,3},{3,2},{4,5},{5,4},{6,7},{7,6},{8,9},{9,8},{10,11... | collective-permute-start | bytes 3145736 | tf_op jit(solution)/shard_map/grad_join/ppermute | solution.py:62
  203.3 13.7 %collective-permute-start.30 = (f32[5,32,768]{2,1,0:T(8,128)S(1)}, f32[5,32,768]{2,1,0:T(8,128)S(1)}, u32[]{:S(2)}, u32[]{:S(2)}) collective-permute-start(f32[5,32,768]{2,1,0:T(8,128)S(1)} %slice_add_fusion), channel_id=1, source_target_pairs={{0,96},{4,100},{8,104},{12,108},{16,112},{20,116},{24,120},{28,124... | collective-permute-start | bytes 1474568 | tf_op jit(solution)/shard_map/mixer_grads_last/ppermute | solution.py:696
  219.3 24.3 %collective-permute-start.31 = (f32[256,1024]{1,0:T(8,128)}, f32[256,1024]{1,0:T(8,128)S(1)}, u32[]{:S(2)}, u32[]{:S(2)}) collective-permute-start(f32[256,1024]{1,0:T(8,128)} %first_norm_back.1.g0_ref), channel_id=1, source_target_pairs={{0,2},{2,0},{1,3},{3,1},{4,6},{6,4},{5,7},{7,5},{8,10},{10,8},{9,1... | collective-permute-start | bytes 3145736 | tf_op jit(solution)/shard_map/grad_join/ppermute | solution.py:66
  223.4 12.4 %collective-permute-start.33 = (f32[3,32,768]{2,1,0:T(8,128)S(1)}, f32[3,32,768]{2,1,0:T(8,128)S(1)}, u32[]{:S(2)}, u32[]{:S(2)}) collective-permute-start(f32[3,32,768]{2,1,0:T(8,128)S(1)} %get-tuple-element.362), channel_id=1, source_target_pairs={{0,4},{4,8},{8,12},{12,0},{16,20},{20,24},{24,28},{28,16},{32,36},... | collective-permute-start | bytes 884744 | tf_op jit(solution)/shard_map/mixer_grads_two/ppermute | solution.py:675
  226.7 30.1 %collective-permute-start.32 = (f32[256,1024]{1,0:T(8,128)}, f32[256,1024]{1,0:T(8,128)}, u32[]{:S(2)}, u32[]{:S(2)}) collective-permute-start(f32[256,1024]{1,0:T(8,128)} %collective-permute-done.23.r0_ref), channel_id=1, source_target_pairs={{0,1},{1,0},{2,3},{3,2},{4,5},{5,4},{6,7},{7,6},{8,9},{9,8},{10,11... | collective-permute-start | bytes 3145736 | tf_op jit(solution)/shard_map/result_join/ppermute | solution.py:62
  243.5 13.3 %collective-permute-start.36 = (f32[256,1024]{1,0:T(8,128)S(1)}, f32[256,1024]{1,0:T(8,128)S(1)}, u32[]{:S(2)}, u32[]{:S(2)}) collective-permute-start(f32[256,1024]{1,0:T(8,128)S(1)} %collective-permute-done.31.g0_ref), channel_id=1, source_target_pairs={{0,1},{1,0},{2,3},{3,2},{4,5},{5,4},{6,7},{7,6},{8,9},{9,8},{10,11... | collective-permute-start | bytes 3145736 | tf_op jit(solution)/shard_map/grad_join/ppermute | solution.py:62
  244.3 19.1 %collective-permute-start.37 = (f32[32,1536]{1,0:T(8,128)S(1)}, f32[32,1536]{1,0:T(8,128)S(1)}, u32[]{:S(2)}, u32[]{:S(2)}) collective-permute-start(f32[32,1536]{1,0:T(8,128)S(1)} %get-tuple-element.359), channel_id=1, source_target_pairs={{0,16},{4,20},{8,24},{12,28},{16,0},{20,4},{24,8},{28,12},{32,48},... | collective-permute-start | bytes 589832 | tf_op jit(solution)/shard_map/rows/ppermute | solution.py:834
  (43 other events, 301.9 us)
Sparse Core Ops, SparseCore 0:
  111.9 86.6 reduce-scatter.2
  219.4 32.4 reduce-scatter.4

commit v6 on v5

--- a/solution.py
+++ b/solution.py
@@ -839,9 +839,9 @@
         feed3 = core_swap(feed1)
     with jax.named_scope("grad_join"):
         grad3 = core_swap(after(grad1, c))
-    result, grad_tokens = run_place(at, 1, after((feed1, grad1, feed3, grad3), a_out), placed)
+    result, grad_tokens = run_place(at, 1, (feed1, grad1, feed3, grad3), placed)
     with jax.named_scope("small_sums"):
-        got = after(got, (result, a_got))
+        got = after(got, result)
         sums = own[:, 768:1536] + got[:, 768:1536]
         sums = sums + core_swap(sums)
         far = z_swap(sums)

time: 281 us -> 279 us (level)
    ppermute x11, waiting for transfers between devices: 54.6 us -> 58 us  [z_swap(): return lax.ppermute(v, 'mp', ZLO)]
    reduce_scatter x2, waiting for transfers between devices: 3.29 us -> 0.02 us  [scatter_rows(): lax.psum_scatter(v, 'dp', scatter_dimension=0, tiled=True, axis_index_gro...]
  transfers between devices with their start and end apart: 43 -> 43, of which waited for: 22 -> 21; matrix products, arithmetic and copies ran while one was open for 5% -> 5% of each run, Pallas kernels for 35% -> 35%
where the time goes in v6:
time: 279 us; the launch traced here: 278 us
  Pallas kernels  103 us (37%)
  waiting for transfers between devices  100 us (36%)
  starting transfers between devices  36.1 us (13%)
  other arithmetic  17.4 us (6%)
  between operations  14.5 us (5%)
  local copies, waits for them, and re-layouts  6.3 us (2%)
    ppermute x11, waiting for transfers between devices, z_swap(): return lax.ppermute(v, 'mp', ZLO)  58 us
    pallas_call x2, Pallas kernels, run_feed(): pl.pallas_call(feed_kernel, grid_spec=pltpu.PrefetchScalarGridSpec(num_sc...  28.3 us
    pallas_call x1, Pallas kernels, run_mixer_backward(): pl.pallas_call(mixer_backward, grid_spec=pltpu.PrefetchScalarGridSpec(num...  16.6 us
    ppermute x1, waiting for transfers between devices, ring_first(): lax.ppermute(v[1], 'dp', shifts[1])  15.7 us
    ppermute x11, starting transfers between devices, z_swap(): return lax.ppermute(v, 'mp', ZLO)  14.5 us
    pallas_call x1, Pallas kernels, run_mixer_forward(): pl.pallas_call(mixer_forward, grid=(t // CH,), in_specs=[pl.BlockSpec(mem...  11.4 us
    pallas_call x2, Pallas kernels, run_place(): pl.pallas_call(place_kernel, grid_spec=pltpu.PrefetchScalarGridSpec(num_s...  11.2 us
    ppermute x21, waiting for transfers between devices, core_swap(): return lax.ppermute(v, 'mp', CORE)  11.1 us
  transfers between devices with their start and end apart: 43, of which 21 were waited for; matrix products, arithmetic and copies ran while one was open for 5% of the time, Pallas kernels for 35%

profile of v6, /device:TPU:0, one launch (start us, length us, event | category | flops | bytes accessed | tf_op | source)
XLA Modules:
  0.0 277.7 jit_solution(11316098961430825217)
XLA Ops:
  10.6 11.4 %mixer_forward.1 = (bf16[1024,1024]{1,0:T(8,128)(2,1)}, bf16[1024,128]{1,0:T(8,128)(2,1)}, bf16[1024,128]{1,0:T(8,128)(2,1)}, bf16[1024,256]{1,0:T(8,128)(2,1)},...) custom-call(s32[1,8]{1,0:T(1,128)} %len_ref.3, ...), custom_call_target="tpu_custom_call" | custom-call | flops 10000000000 | bytes 1024 | tf_op jit(solution)/shard_map/mixer_forward/pallas_call | solution.py:206
  21.9 12.4 %collective-permute-done.w1_ref = f32[256,1024]{1,0:T(8,128)S(1)} collective-permute-done((f32[256,1024]{1,0:T(8,128)S(1)}, f32[256,1024]{1,0:T(8,128)S(1)}, u32[]{:S(2)}, u32[]{:S(2)}) %collective-permute-start) | collective-permute-done | bytes 1048608 | tf_op jit(solution)/shard_map/out_weights/ppermute | solution.py:66
  38.7 7.0 %before_feed.1 = (bf16[1024,1024]{1,0:T(8,128)(2,1)}, f32[1024,704]{1,0:T(8,128)}) custom-call(bf16[256,1024]{1,0:T(8,128)(2,1)} %refs_14_.1, f32[256,1024]{1,0:T(8,128)} %copy-done.17, f32[256,1024]{1,0:T(8,128)} %copy-done.16, f32[256,1024]{1,0:T(8,128)} %copy-done.18, bf16[1024,1024]{1,0:T(8,128)(2,1)} %base1_ref.1, bf16[704,1024]{1,0:T(8,128)(2,1)} %wd_ref.5), custom_call_target="tpu_custom_call" | custom-call | flops 7000000000 | bytes 1024 | tf_op jit(solution)/shard_map/before_feed/pallas_call | solution.py:236
  45.7 3.3 %collective-permute-done.2.m1_ref = f32[512,256]{1,0:T(8,128)} collective-permute-done((f32[512,256]{1,0:T(8,128)}, f32[512,256]{1,0:T(8,128)}, u32[]{:S(2)}, u32[]{:S(2)}) %collective-permute-start.2) | collective-permute-done | bytes 524320 | tf_op jit(solution)/shard_map/heads_one/ppermute | solution.py:66
  52.1 14.1 %feed_both_ways.2 = (f32[512,1024]{1,0:T(8,128)}, bf16[512,1024]{1,0:T(8,128)(2,1)}, bf16[512,704]{1,0:T(8,128)(2,1)}, bf16[512,1408]{1,0:T(8,128)(2,1)}, f32[25...) custom-call(s32[4]{0:T(128)} %pad_add_fusion.at_ref, ...), custom_call_target="tpu_custom_call" | custom-call | flops 14000000000 | bytes 1024 | tf_op jit(solution)/shard_map/feed_both_ways/pallas_call | solution.py:293
  66.6 2.7 collective-permute-done.8.b1_ref
  73.5 14.2 %feed_both_ways.3 = (f32[512,1024]{1,0:T(8,128)}, bf16[512,1024]{1,0:T(8,128)(2,1)}, bf16[512,704]{1,0:T(8,128)(2,1)}, bf16[512,1408]{1,0:T(8,128)(2,1)}, f32[25...) custom-call(s32[4]{0:T(128)} %pad_add_fusion.at_ref, ...), custom_call_target="tpu_custom_call" | custom-call | flops 14000000000 | bytes 1024 | tf_op jit(solution)/shard_map/feed_both_ways/pallas_call | solution.py:293
  87.9 2.7 collective-permute-done.11.b0_ref
  94.9 10.4 %feed_weight_grads.1 = f32[4,4,2,32,2176]{4,3,2,1,0:T(8,128)} custom-call(bf16[512,1024]{1,0:T(8,128)(2,1)} %get-tuple-element.239.l0_ref, bf16[512,1024]{1,0:T(8,128)(2,1)} %get-tuple-element.240.l1_ref, bf16[512,1408]{1,0:T(8,128)(2,1)} %get-tuple-element.241.r0_ref, bf16[512,1408]{1,0:T(8,128)(2,1)} %get-tuple-element.242.r1_ref, ...), custom_call_target="tpu_custom_call" | custom-call | flops 12000000000 | bytes 1024 | tf_op jit(solution)/shard_map/feed_weight_grads/pallas_call | solution.py:556
  107.2 4.5 %second_norm_back.1 = (f32[256,1024]{1,0:T(8,128)}, f32[8,1024]{1,0:T(8,128)}) custom-call(s32[4]{0:T(128)} %pad_add_fusion.at_ref, f32[256,1024]{1,0:T(8,128)} %get-tuple-element.234.a0_ref, f32[256,1024]{1,0:T(8,128)} %copy-done.1, f32[128,1024]{1,0:T(8,128)} %collective-permute-done.12.c0_ref, f32[512,1024]{1,0:T(8,128)} %get-tuple-element.246.y0_ref, ...), custom_call_target="tpu_custom_call" | custom-call | flops 3000000000 | bytes 1024 | tf_op jit(solution)/shard_map/second_norm_back/pallas_call | solution.py:469
  114.9 22.9 %collective-permute-done.15.refs_1_ = f32[256,1024]{1,0:T(8,128)} collective-permute-done((f32[256,1024]{1,0:T(8,128)}, f32[256,1024]{1,0:T(8,128)}, u32[]{:S(2)}, u32[]{:S(2)}) %collective-permute-start.15) | collective-permute-done | bytes 1048608 | tf_op jit(solution)/shard_map/second_norm_join/ppermute | solution.py:66
  137.8 3.0 %collective-permute-done.17.refs_3_ = f32[256,1024]{1,0:T(8,128)} collective-permute-done((f32[256,1024]{1,0:T(8,128)}, f32[256,1024]{1,0:T(8,128)}, u32[]{:S(2)}, u32[]{:S(2)}) %collective-permute-start.17) | collective-permute-done | bytes 1048608 | tf_op jit(solution)/shard_map/second_norm_join/ppermute | solution.py:62
  142.3 16.6 %mixer_backward.1 = (bf16[1024,512]{1,0:T(8,128)(2,1)}, f32[128,1024]{1,0:T(8,128)}, f32[128,1024]{1,0:T(8,128)}, f32[128,1024]{1,0:T(8,128)}, f32[128,1024]{1,0...) custom-call(s32[4]{0:T(128)} %pad_add_fusion.at_ref, ...), custom_call_target="tpu_custom_call" | custom-call | flops 16000000000 | bytes 1024 | tf_op jit(solution)/shard_map/mixer_backward/pallas_call | solution.py:416
  159.9 7.9 %mixer_weight_grads.1 = (f32[9,32,768]{2,1,0:T(8,128)}, f32[9,32,768]{2,1,0:T(8,128)}, f32[9,32,768]{2,1,0:T(8,128)}, f32[4,32,768]{2,1,0:T(8,128)}, f32[5,32,768]{2,1,0:T(8,128)}) custom-call(s32[4]{0:T(128)} %pad_add_fusion.at_ref, bf16[1024,1024]{1,0:T(8,128)(2,1)} %get-tuple-element.266.refs_6_.l_ref, bf16[1024,512]{1,0:T(8,128)(2,1)} %get-tuple-element.279.r0_ref, ...), custom_call_target="tpu_custom_call" | custom-call | flops 8000000000 | bytes 1024 | tf_op jit(solution)/shard_map/mixer_weight_grads/pallas_call | solution.py:623
  177.9 15.7 %collective-permute-done.27 = f32[9,32,768]{2,1,0:T(8,128)} collective-permute-done((f32[9,32,768]{2,1,0:T(8,128)}, f32[9,32,768]{2,1,0:T(8,128)}, u32[]{:S(2)}, u32[]{:S(2)}) %collective-permute-start.27) | collective-permute-done | bytes 884768 | tf_op jit(solution)/shard_map/mixer_grads_first/ppermute | solution.py:687
  197.9 4.1 %first_norm_back.1.g0_ref = f32[256,1024]{1,0:T(8,128)} custom-call(s32[4]{0:T(128)} %pad_add_fusion.at_ref, f32[512,1024]{1,0:T(8,128)} %get-tuple-element.290.a_ref, f32[128,1024]{1,0:T(8,128)} %collective-permute-done.21.b0_ref, f32[128,1024]{1,0:T(8,128)} %collective-permute-done.22.b1_ref, f32[256,1024]{1,0:T(8,128)} %collective-permute-done.25.c_ref, ...), custom_call_target="tpu_custom_call" | custom-call | flops 3000000000 | bytes 1024 | tf_op jit(solution)/shard_map/first_norm_back/pallas_call | solution.py:495
  208.4 8.6 %collective-permute-done.30 = f32[5,32,768]{2,1,0:T(8,128)S(1)} collective-permute-done((f32[5,32,768]{2,1,0:T(8,128)S(1)}, f32[5,32,768]{2,1,0:T(8,128)S(1)}, u32[]{:S(2)}, u32[]{:S(2)}) %collective-permute-start.30) | collective-permute-done | bytes 491552 | tf_op jit(solution)/shard_map/mixer_grads_last/ppermute | solution.py:696
  220.1 3.4 %collective-permute-start.35 = (f32[3,32,768]{2,1,0:T(8,128)S(1)}, f32[3,32,768]{2,1,0:T(8,128)S(1)}, u32[]{:S(2)}, u32[]{:S(2)}) collective-permute-start(f32[3,32,768]{2,1,0:T(8,128)S(1)} %get-tuple-element.353), channel_id=1, source_target_pairs={{0,8},{4,12},{8,0},{12,4},{16,24},{20,28},{24,16},{28,20},{32,40},... | collective-permute-start | bytes 884744 | tf_op jit(solution)/shard_map/mixer_grads_two/ppermute | solution.py:675
  226.7 5.7 %place_rows.2 = (bf16[1024,1024]{1,0:T(8,128)(2,1)}, f32[1024,1024]{1,0:T(8,128)}) custom-call(s32[4]{0:T(128)} %pad_add_fusion.at_ref, f32[256,1024]{1,0:T(8,128)} %copy-done.2, f32[256,1024]{1,0:T(8,128)} %first_norm_back.1.g0_ref, f32[256,1024]{1,0:T(8,128)} %collective-permute-done.24.r1_ref, f32[256,1024]{1,0:T(8,128)} %collective-permute-done.26.g1_ref), custom_call_target="tpu_custom_call" | custom-call | flops 3000000000 | bytes 1024 | tf_op jit(solution)/shard_map/place_rows/pallas_call | solution.py:525
  232.3 3.5 %collective-permute-done.33 = f32[3,32,768]{2,1,0:T(8,128)S(1)} collective-permute-done((f32[3,32,768]{2,1,0:T(8,128)S(1)}, f32[3,32,768]{2,1,0:T(8,128)S(1)}, u32[]{:S(2)}, u32[]{:S(2)}) %collective-permute-start.33) | collective-permute-done | bytes 294944 | tf_op jit(solution)/shard_map/mixer_grads_two/ppermute | solution.py:675
  236.1 7.5 %collective-permute-done.31.g0_ref = f32[256,1024]{1,0:T(8,128)S(1)} collective-permute-done((f32[256,1024]{1,0:T(8,128)}, f32[256,1024]{1,0:T(8,128)S(1)}, u32[]{:S(2)}, u32[]{:S(2)}) %collective-permute-start.31) | collective-permute-done | bytes 1048608 | tf_op jit(solution)/shard_map/grad_join/ppermute | solution.py:66
  244.3 4.2 %collective-permute-start.37 = (f32[32,1536]{1,0:T(8,128)S(1)}, f32[32,1536]{1,0:T(8,128)S(1)}, u32[]{:S(2)}, u32[]{:S(2)}) collective-permute-start(f32[32,1536]{1,0:T(8,128)S(1)} %get-tuple-element.351), channel_id=1, source_target_pairs={{0,16},{4,20},{8,24},{12,28},{16,0},{20,4},{24,8},{28,12},{32,48},... | collective-permute-start | bytes 589832 | tf_op jit(solution)/shard_map/rows/ppermute | solution.py:834
  249.6 5.6 %place_rows.3 = (bf16[1024,1024]{1,0:T(8,128)(2,1)}, f32[1024,1024]{1,0:T(8,128)}) custom-call(s32[4]{0:T(128)} %pad_add_fusion.at_ref, f32[256,1024]{1,0:T(8,128)} %collective-permute-done.23.r0_ref, f32[256,1024]{1,0:T(8,128)} %copy-done.14, f32[256,1024]{1,0:T(8,128)} %collective-permute-done.32.r1_ref, ...), custom_call_target="tpu_custom_call", output_to_operand_aliasing={{0}: (5, {}), {1}: (6, {})} | custom-call | flops 3000000000 | bytes 1024 | tf_op jit(solution)/shard_map/place_rows/pallas_call | solution.py:525
  260.7 6.7 %collective-permute-done.40.far_ref = f32[32,768]{1,0:T(8,128)S(1)} collective-permute-done((f32[32,768]{1,0:T(8,128)S(1)}, f32[32,768]{1,0:T(8,128)S(1)}, u32[]{:S(2)}, u32[]{:S(2)}) %collective-permute-start.40) | collective-permute-done | bytes 98336 | tf_op jit(solution)/shard_map/small_sums/ppermute | solution.py:66
  (148 shorter events, 65.4 us)
Async XLA Ops:
  7.2 212.1 %reduce-scatter.3.cloned.1.call-start = ((), (), s32[]{:S(2)}) async-start(), calls=%async_computation.2 | async-start | bytes 11141120 | tf_op jit(solution)/shard_map/feed_grads_x/reduce_scatter | solution.py:683
  8.4 13.5 %collective-permute-start.1 = (f32[256,1024]{1,0:T(8,128)S(1)}, f32[256,1024]{1,0:T(8,128)S(1)}, u32[]{:S(2)}, u32[]{:S(2)}) collective-permute-start(f32[256,1024]{1,0:T(8,128)S(1)} %convert_element_type.3), channel_id=1, source_target_pairs={{0,1},{1,0},{2,3},{3,2},{4,5},{5,4},{6,7},{7,6},{8,9},{9,8},{10,11... | collective-permute-start | bytes 3145736 | tf_op jit(solution)/shard_map/out_weights/ppermute | solution.py:62
  8.5 25.8 %collective-permute-start = (f32[256,1024]{1,0:T(8,128)S(1)}, f32[256,1024]{1,0:T(8,128)S(1)}, u32[]{:S(2)}, u32[]{:S(2)}) collective-permute-start(f32[256,1024]{1,0:T(8,128)S(1)} %convert_element_type.3), channel_id=1, source_target_pairs={{0,2},{2,0},{1,3},{3,1},{4,6},{6,4},{5,7},{7,5},{8,10},{10,8},{9,1... | collective-permute-start | bytes 3145736 | tf_op jit(solution)/shard_map/out_weights/ppermute | solution.py:66
  34.8 14.2 %collective-permute-start.2 = (f32[512,256]{1,0:T(8,128)}, f32[512,256]{1,0:T(8,128)}, u32[]{:S(2)}, u32[]{:S(2)}) collective-permute-start(f32[512,256]{1,0:T(8,128)} %get-tuple-element.179.m0_ref.m1_ref), channel_id=1, source_target_pairs={{0,2},{2,0},{1,3},{3,1},{4,6},{6,4},{5,7},{7,5},{8,10},{10,8},{9,1... | collective-permute-start | bytes 1572872 | tf_op jit(solution)/shard_map/heads_one/ppermute | solution.py:66
  49.6 16.7 %collective-permute-start.6 = (f32[512,256]{1,0:T(8,128)}, f32[512,256]{1,0:T(8,128)S(1)}, u32[]{:S(2)}, u32[]{:S(2)}) collective-permute-start(f32[512,256]{1,0:T(8,128)} %get-tuple-element.185.m0_ref), channel_id=1, source_target_pairs={{0,2},{2,0},{1,3},{3,1},{4,6},{6,4},{5,7},{7,5},{8,10},{10,8},{9,1... | collective-permute-start | bytes 1572872 | tf_op jit(solution)/shard_map/heads_two/ppermute | solution.py:66
  71.0 16.7 %collective-permute-start.9 = (f32[128,1024]{1,0:T(8,128)S(1)}, f32[128,1024]{1,0:T(8,128)S(1)}, u32[]{:S(2)}, u32[]{:S(2)}) collective-permute-start(f32[128,1024]{1,0:T(8,128)S(1)} %dynamic-slice_add_fusion.7), channel_id=1, source_target_pairs={{0,2},{2,0},{1,3},{3,1},{4,6},{6,4},{5,7},{7,5},{8,10},{10,8},{9,1... | collective-permute-start | bytes 1572872 | tf_op jit(solution)/shard_map/second_norm_z/ppermute | solution.py:66
  92.9 14.3 %collective-permute-start.12 = (f32[128,1024]{1,0:T(8,128)}, f32[128,1024]{1,0:T(8,128)}, u32[]{:S(2)}, u32[]{:S(2)}) collective-permute-start(f32[128,1024]{1,0:T(8,128)} %dynamic-slice_add_fusion.6), channel_id=1, source_target_pairs={{0,2},{2,0},{1,3},{3,1},{4,6},{6,4},{5,7},{7,5},{8,10},{10,8},{9,1... | collective-permute-start | bytes 1572872 | tf_op jit(solution)/shard_map/second_norm_z/ppermute | solution.py:66
  94.4 12.8 %collective-permute-start.13 = (f32[256,1024]{1,0:T(8,128)}, f32[256,1024]{1,0:T(8,128)S(1)}, u32[]{:S(2)}, u32[]{:S(2)}) collective-permute-start(f32[256,1024]{1,0:T(8,128)} %get-tuple-element.237), channel_id=1, source_target_pairs={{0,1},{1,0},{2,3},{3,2},{4,5},{5,4},{6,7},{7,6},{8,9},{9,8},{10,11... | collective-permute-start | bytes 3145736 | tf_op jit(solution)/shard_map/second_norm_z/ppermute | solution.py:62
  94.4 12.8 %collective-permute-start.14 = (f32[256,1024]{1,0:T(8,128)}, f32[256,1024]{1,0:T(8,128)S(1)}, u32[]{:S(2)}, u32[]{:S(2)}) collective-permute-start(f32[256,1024]{1,0:T(8,128)} %get-tuple-element.238), channel_id=1, source_target_pairs={{0,1},{1,0},{2,3},{3,2},{4,5},{5,4},{6,7},{7,6},{8,9},{9,8},{10,11... | collective-permute-start | bytes 3145736 | tf_op jit(solution)/shard_map/second_norm_z/ppermute | solution.py:62
  111.8 143.4 %reduce-scatter.5.cloned.1.call-start = ((), (), s32[]{:S(2)}) async-start(), calls=%async_computation.3 | async-start | bytes 2785280 | tf_op jit(solution)/shard_map/feed_grads_y/reduce_scatter | solution.py:683
  111.9 25.9 %collective-permute-start.15 = (f32[256,1024]{1,0:T(8,128)}, f32[256,1024]{1,0:T(8,128)}, u32[]{:S(2)}, u32[]{:S(2)}) collective-permute-start(f32[256,1024]{1,0:T(8,128)} %get-tuple-element.256.refs_0_.base_ref), channel_id=1, source_target_pairs={{0,2},{2,0},{1,3},{3,1},{4,6},{6,4},{5,7},{7,5},{8,10},{10,8},{9,1... | collective-permute-start | bytes 3145736 | tf_op jit(solution)/shard_map/second_norm_join/ppermute | solution.py:66
  140.8 27.1 %collective-permute-start.18 = (f32[256,1024]{1,0:T(8,128)S(1)}, f32[256,1024]{1,0:T(8,128)S(1)}, u32[]{:S(2)}, u32[]{:S(2)}) collective-permute-start(f32[256,1024]{1,0:T(8,128)S(1)} %pad_maximum_fusion), channel_id=1, source_target_pairs={{0,2},{2,0},{1,3},{3,1},{4,6},{6,4},{5,7},{7,5},{8,10},{10,8},{9,1... | collective-permute-start | bytes 3145736 | tf_op jit(solution)/shard_map/feed_sum/ppermute | solution.py:66
  170.1 23.5 %collective-permute-start.27 = (f32[9,32,768]{2,1,0:T(8,128)}, f32[9,32,768]{2,1,0:T(8,128)}, u32[]{:S(2)}, u32[]{:S(2)}) collective-permute-start(f32[9,32,768]{2,1,0:T(8,128)} %get-tuple-element.303), channel_id=1, source_target_pairs={{0,32},{4,36},{8,40},{12,44},{16,48},{20,52},{24,56},{28,60},{32,6... | collective-permute-start | bytes 2654216 | tf_op jit(solution)/shard_map/mixer_grads_first/ppermute | solution.py:687
  171.8 26.2 %collective-permute-start.25 = (f32[256,1024]{1,0:T(8,128)S(1)}, f32[256,1024]{1,0:T(8,128)}, u32[]{:S(2)}, u32[]{:S(2)}) collective-permute-start(f32[256,1024]{1,0:T(8,128)S(1)} %pad_maximum_fusion.2), channel_id=1, source_target_pairs={{0,2},{2,0},{1,3},{3,1},{4,6},{6,4},{5,7},{7,5},{8,10},{10,8},{9,1... | collective-permute-start | bytes 3145736 | tf_op jit(solution)/shard_map/first_norm_z/ppermute | solution.py:66
  172.4 29.6 %collective-permute-start.29 = (f32[9,32,768]{2,1,0:T(8,128)}, f32[9,32,768]{2,1,0:T(8,128)}, u32[]{:S(2)}, u32[]{:S(2)}) collective-permute-start(f32[9,32,768]{2,1,0:T(8,128)} %get-tuple-element.304), channel_id=1, source_target_pairs={{0,96},{4,100},{8,104},{12,108},{16,112},{20,116},{24,120},{28,124... | collective-permute-start | bytes 2654216 | tf_op jit(solution)/shard_map/mixer_grads_first/ppermute | solution.py:687
  176.4 41.8 %collective-permute-start.24 = (f32[256,1024]{1,0:T(8,128)S(1)}, f32[256,1024]{1,0:T(8,128)}, u32[]{:S(2)}, u32[]{:S(2)}) collective-permute-start(f32[256,1024]{1,0:T(8,128)S(1)} %pad_maximum_fusion.1.r0_ref), channel_id=1, source_target_pairs={{0,1},{1,0},{2,3},{3,2},{4,5},{5,4},{6,7},{7,6},{8,9},{9,8},{10,11... | collective-permute-start | bytes 3145736 | tf_op jit(solution)/shard_map/result_join/ppermute | solution.py:62
  176.5 42.7 %collective-permute-start.23 = (f32[256,1024]{1,0:T(8,128)S(1)}, f32[256,1024]{1,0:T(8,128)}, u32[]{:S(2)}, u32[]{:S(2)}) collective-permute-start(f32[256,1024]{1,0:T(8,128)S(1)} %pad_maximum_fusion.1.r0_ref), channel_id=1, source_target_pairs={{0,2},{2,0},{1,3},{3,1},{4,6},{6,4},{5,7},{7,5},{8,10},{10,8},{9,1... | collective-permute-start | bytes 3145736 | tf_op jit(solution)/shard_map/result_join/ppermute | solution.py:66
  202.0 17.2 %collective-permute-start.26 = (f32[256,1024]{1,0:T(8,128)}, f32[256,1024]{1,0:T(8,128)}, u32[]{:S(2)}, u32[]{:S(2)}) collective-permute-start(f32[256,1024]{1,0:T(8,128)} %first_norm_back.1.g0_ref), channel_id=1, source_target_pairs={{0,1},{1,0},{2,3},{3,2},{4,5},{5,4},{6,7},{7,6},{8,9},{9,8},{10,11... | collective-permute-start | bytes 3145736 | tf_op jit(solution)/shard_map/grad_join/ppermute | solution.py:62
  203.3 13.7 %collective-permute-start.30 = (f32[5,32,768]{2,1,0:T(8,128)S(1)}, f32[5,32,768]{2,1,0:T(8,128)S(1)}, u32[]{:S(2)}, u32[]{:S(2)}) collective-permute-start(f32[5,32,768]{2,1,0:T(8,128)S(1)} %slice_add_fusion), channel_id=1, source_target_pairs={{0,96},{4,100},{8,104},{12,108},{16,112},{20,116},{24,120},{28,124... | collective-permute-start | bytes 1474568 | tf_op jit(solution)/shard_map/mixer_grads_last/ppermute | solution.py:696
  219.3 24.3 %collective-permute-start.31 = (f32[256,1024]{1,0:T(8,128)}, f32[256,1024]{1,0:T(8,128)S(1)}, u32[]{:S(2)}, u32[]{:S(2)}) collective-permute-start(f32[256,1024]{1,0:T(8,128)} %first_norm_back.1.g0_ref), channel_id=1, source_target_pairs={{0,2},{2,0},{1,3},{3,1},{4,6},{6,4},{5,7},{7,5},{8,10},{10,8},{9,1... | collective-permute-start | bytes 3145736 | tf_op jit(solution)/shard_map/grad_join/ppermute | solution.py:66
  220.1 12.3 %collective-permute-start.35 = (f32[3,32,768]{2,1,0:T(8,128)S(1)}, f32[3,32,768]{2,1,0:T(8,128)S(1)}, u32[]{:S(2)}, u32[]{:S(2)}) collective-permute-start(f32[3,32,768]{2,1,0:T(8,128)S(1)} %get-tuple-element.353), channel_id=1, source_target_pairs={{0,8},{4,12},{8,0},{12,4},{16,24},{20,28},{24,16},{28,20},{32,40},... | collective-permute-start | bytes 884744 | tf_op jit(solution)/shard_map/mixer_grads_two/ppermute | solution.py:675
  223.4 12.4 %collective-permute-start.33 = (f32[3,32,768]{2,1,0:T(8,128)S(1)}, f32[3,32,768]{2,1,0:T(8,128)S(1)}, u32[]{:S(2)}, u32[]{:S(2)}) collective-permute-start(f32[3,32,768]{2,1,0:T(8,128)S(1)} %get-tuple-element.354), channel_id=1, source_target_pairs={{0,4},{4,8},{8,12},{12,0},{16,20},{20,24},{24,28},{28,16},{32,36},... | collective-permute-start | bytes 884744 | tf_op jit(solution)/shard_map/mixer_grads_two/ppermute | solution.py:675
  224.1 11.9 %collective-permute-start.34 = (f32[3,32,768]{2,1,0:T(8,128)S(1)}, f32[3,32,768]{2,1,0:T(8,128)S(1)}, u32[]{:S(2)}, u32[]{:S(2)}) collective-permute-start(f32[3,32,768]{2,1,0:T(8,128)S(1)} %get-tuple-element.355), channel_id=1, source_target_pairs={{0,12},{4,0},{8,4},{12,8},{16,28},{20,16},{24,20},{28,24},{32,44},... | collective-permute-start | bytes 884744 | tf_op jit(solution)/shard_map/mixer_grads_two/ppermute | solution.py:675
  226.7 21.9 %collective-permute-start.32 = (f32[256,1024]{1,0:T(8,128)}, f32[256,1024]{1,0:T(8,128)}, u32[]{:S(2)}, u32[]{:S(2)}) collective-permute-start(f32[256,1024]{1,0:T(8,128)} %collective-permute-done.23.r0_ref), channel_id=1, source_target_pairs={{0,1},{1,0},{2,3},{3,2},{4,5},{5,4},{6,7},{7,6},{8,9},{9,8},{10,11... | collective-permute-start | bytes 3145736 | tf_op jit(solution)/shard_map/result_join/ppermute | solution.py:62
  (43 other events, 291.3 us)
Sparse Core Ops, SparseCore 0:
  111.9 86.6 reduce-scatter.2
  219.4 32.4 reduce-scatter.4

commit v7 on v6

--- a/solution.py
+++ b/solution.py
@@ -781,7 +781,6 @@
 
     with jax.named_scope("second_norm_join"):
         gm3 = core_swap(gm1)
-    gm3, gm1, feed_z_out = phase(gm3, gm1, feed_z_out)
 
     with jax.named_scope("feed_sum"):
         feed_z = z_swap(feed_z_out)

time: 279 us -> 278 us (level)
  transfers between devices with their start and end apart: 43 -> 43, of which waited for: 21 -> 20; matrix products, arithmetic and copies ran while one was open for 5% -> 5% of each run, Pallas kernels for 35% -> 35%
where the time goes in v7:
time: 278 us; the launch traced here: 276 us
  Pallas kernels  104 us (37%)
  waiting for transfers between devices  97.5 us (35%)
  starting transfers between devices  36.7 us (13%)
  other arithmetic  17.3 us (6%)
  between operations  14.5 us (5%)
  local copies, waits for them, and re-layouts  6.32 us (2%)
    ppermute x11, waiting for transfers between devices, z_swap(): return lax.ppermute(v, 'mp', ZLO)  57.3 us
    pallas_call x2, Pallas kernels, run_feed(): pl.pallas_call(feed_kernel, grid_spec=pltpu.PrefetchScalarGridSpec(num_sc...  28.3 us
    pallas_call x1, Pallas kernels, run_mixer_backward(): pl.pallas_call(mixer_backward, grid_spec=pltpu.PrefetchScalarGridSpec(num...  16.5 us
    ppermute x11, starting transfers between devices, z_swap(): return lax.ppermute(v, 'mp', ZLO)  16.2 us
    ppermute x1, waiting for transfers between devices, ring_first(): lax.ppermute(v[1], 'dp', shifts[1])  15.5 us
    pallas_call x1, Pallas kernels, run_mixer_forward(): pl.pallas_call(mixer_forward, grid=(t // CH,), in_specs=[pl.BlockSpec(mem...  11.4 us
    pallas_call x2, Pallas kernels, run_place(): pl.pallas_call(place_kernel, grid_spec=pltpu.PrefetchScalarGridSpec(num_s...  11.3 us
    pallas_call x1, Pallas kernels, run_feed_grads(): pl.pallas_call(feed_grads_kernel, grid=(4,), in_specs=[cols(0), cols(0),...  10.4 us
  transfers between devices with their start and end apart: 43, of which 20 were waited for; matrix products, arithmetic and copies ran while one was open for 5% of the time, Pallas kernels for 35%

profile of v7, /device:TPU:0, one launch (start us, length us, event | category | flops | bytes accessed | tf_op | source)
XLA Modules:
  0.0 276.1 jit_solution(10360097430271675860)
XLA Ops:
  10.6 11.4 %mixer_forward.1 = (bf16[1024,1024]{1,0:T(8,128)(2,1)}, bf16[1024,128]{1,0:T(8,128)(2,1)}, bf16[1024,128]{1,0:T(8,128)(2,1)}, bf16[1024,256]{1,0:T(8,128)(2,1)},...) custom-call(s32[1,8]{1,0:T(1,128)} %len_ref.3, ...), custom_call_target="tpu_custom_call" | custom-call | flops 10000000000 | bytes 1024 | tf_op jit(solution)/shard_map/mixer_forward/pallas_call | solution.py:206
  21.9 12.4 %collective-permute-done.w1_ref = f32[256,1024]{1,0:T(8,128)S(1)} collective-permute-done((f32[256,1024]{1,0:T(8,128)S(1)}, f32[256,1024]{1,0:T(8,128)S(1)}, u32[]{:S(2)}, u32[]{:S(2)}) %collective-permute-start) | collective-permute-done | bytes 1048608 | tf_op jit(solution)/shard_map/out_weights/ppermute | solution.py:66
  38.7 7.0 %before_feed.1 = (bf16[1024,1024]{1,0:T(8,128)(2,1)}, f32[1024,704]{1,0:T(8,128)}) custom-call(bf16[256,1024]{1,0:T(8,128)(2,1)} %refs_14_.1, f32[256,1024]{1,0:T(8,128)} %copy-done.17, f32[256,1024]{1,0:T(8,128)} %copy-done.16, f32[256,1024]{1,0:T(8,128)} %copy-done.18, bf16[1024,1024]{1,0:T(8,128)(2,1)} %base1_ref.1, bf16[704,1024]{1,0:T(8,128)(2,1)} %wd_ref.5), custom_call_target="tpu_custom_call" | custom-call | flops 7000000000 | bytes 1024 | tf_op jit(solution)/shard_map/before_feed/pallas_call | solution.py:236
  45.7 3.3 %collective-permute-done.2.m1_ref = f32[512,256]{1,0:T(8,128)} collective-permute-done((f32[512,256]{1,0:T(8,128)}, f32[512,256]{1,0:T(8,128)}, u32[]{:S(2)}, u32[]{:S(2)}) %collective-permute-start.2) | collective-permute-done | bytes 524320 | tf_op jit(solution)/shard_map/heads_one/ppermute | solution.py:66
  52.1 14.1 %feed_both_ways.2 = (f32[512,1024]{1,0:T(8,128)}, bf16[512,1024]{1,0:T(8,128)(2,1)}, bf16[512,704]{1,0:T(8,128)(2,1)}, bf16[512,1408]{1,0:T(8,128)(2,1)}, f32[25...) custom-call(s32[4]{0:T(128)} %pad_add_fusion.at_ref, ...), custom_call_target="tpu_custom_call" | custom-call | flops 14000000000 | bytes 1024 | tf_op jit(solution)/shard_map/feed_both_ways/pallas_call | solution.py:293
  66.6 2.7 collective-permute-done.8.b1_ref
  73.5 14.2 %feed_both_ways.3 = (f32[512,1024]{1,0:T(8,128)}, bf16[512,1024]{1,0:T(8,128)(2,1)}, bf16[512,704]{1,0:T(8,128)(2,1)}, bf16[512,1408]{1,0:T(8,128)(2,1)}, f32[25...) custom-call(s32[4]{0:T(128)} %pad_add_fusion.at_ref, ...), custom_call_target="tpu_custom_call" | custom-call | flops 14000000000 | bytes 1024 | tf_op jit(solution)/shard_map/feed_both_ways/pallas_call | solution.py:293
  87.9 2.7 collective-permute-done.11.b0_ref
  94.9 10.4 %feed_weight_grads.1 = f32[4,4,2,32,2176]{4,3,2,1,0:T(8,128)} custom-call(bf16[512,1024]{1,0:T(8,128)(2,1)} %get-tuple-element.236.l0_ref, bf16[512,1024]{1,0:T(8,128)(2,1)} %get-tuple-element.237.l1_ref, bf16[512,1408]{1,0:T(8,128)(2,1)} %get-tuple-element.238.r0_ref, bf16[512,1408]{1,0:T(8,128)(2,1)} %get-tuple-element.239.r1_ref, ...), custom_call_target="tpu_custom_call" | custom-call | flops 12000000000 | bytes 1024 | tf_op jit(solution)/shard_map/feed_weight_grads/pallas_call | solution.py:556
  107.2 4.5 %second_norm_back.1 = (f32[256,1024]{1,0:T(8,128)}, f32[8,1024]{1,0:T(8,128)}) custom-call(s32[4]{0:T(128)} %pad_add_fusion.at_ref, f32[256,1024]{1,0:T(8,128)} %get-tuple-element.231.a0_ref, f32[256,1024]{1,0:T(8,128)} %copy-done.1, f32[128,1024]{1,0:T(8,128)} %collective-permute-done.12.c0_ref, f32[512,1024]{1,0:T(8,128)} %get-tuple-element.243.y0_ref, ...), custom_call_target="tpu_custom_call" | custom-call | flops 3000000000 | bytes 1024 | tf_op jit(solution)/shard_map/second_norm_back/pallas_call | solution.py:469
  114.9 22.9 %collective-permute-done.15.refs_1_ = f32[256,1024]{1,0:T(8,128)} collective-permute-done((f32[256,1024]{1,0:T(8,128)}, f32[256,1024]{1,0:T(8,128)}, u32[]{:S(2)}, u32[]{:S(2)}) %collective-permute-start.15) | collective-permute-done | bytes 1048608 | tf_op jit(solution)/shard_map/second_norm_join/ppermute | solution.py:66
  140.8 16.5 %mixer_backward.1 = (bf16[1024,512]{1,0:T(8,128)(2,1)}, f32[128,1024]{1,0:T(8,128)}, f32[128,1024]{1,0:T(8,128)}, f32[128,1024]{1,0:T(8,128)}, f32[128,1024]{1,0...) custom-call(s32[4]{0:T(128)} %pad_add_fusion.at_ref, ...), custom_call_target="tpu_custom_call" | custom-call | flops 16000000000 | bytes 1024 | tf_op jit(solution)/shard_map/mixer_backward/pallas_call | solution.py:416
  158.5 8.2 %mixer_weight_grads.1 = (f32[9,32,768]{2,1,0:T(8,128)}, f32[9,32,768]{2,1,0:T(8,128)}, f32[9,32,768]{2,1,0:T(8,128)}, f32[4,32,768]{2,1,0:T(8,128)}, f32[5,32,768]{2,1,0:T(8,128)}) custom-call(s32[4]{0:T(128)} %pad_add_fusion.at_ref, bf16[1024,1024]{1,0:T(8,128)(2,1)} %get-tuple-element.260.refs_6_.l_ref, bf16[1024,512]{1,0:T(8,128)(2,1)} %get-tuple-element.273.r0_ref, ...), custom_call_target="tpu_custom_call" | custom-call | flops 8000000000 | bytes 1024 | tf_op jit(solution)/shard_map/mixer_weight_grads/pallas_call | solution.py:623
  176.6 15.5 %collective-permute-done.27 = f32[9,32,768]{2,1,0:T(8,128)} collective-permute-done((f32[9,32,768]{2,1,0:T(8,128)}, f32[9,32,768]{2,1,0:T(8,128)}, u32[]{:S(2)}, u32[]{:S(2)}) %collective-permute-start.27) | collective-permute-done | bytes 884768 | tf_op jit(solution)/shard_map/mixer_grads_first/ppermute | solution.py:687
  194.2 2.5 collective-permute-done.25.c_ref
  196.7 4.2 %first_norm_back.1.g0_ref = f32[256,1024]{1,0:T(8,128)} custom-call(s32[4]{0:T(128)} %pad_add_fusion.at_ref, f32[512,1024]{1,0:T(8,128)} %get-tuple-element.284.a_ref, f32[128,1024]{1,0:T(8,128)} %collective-permute-done.21.b0_ref, f32[128,1024]{1,0:T(8,128)} %collective-permute-done.22.b1_ref, f32[256,1024]{1,0:T(8,128)} %collective-permute-done.25.c_ref, ...), custom_call_target="tpu_custom_call" | custom-call | flops 3000000000 | bytes 1024 | tf_op jit(solution)/shard_map/first_norm_back/pallas_call | solution.py:495
  206.5 9.3 %collective-permute-done.30 = f32[5,32,768]{2,1,0:T(8,128)S(1)} collective-permute-done((f32[5,32,768]{2,1,0:T(8,128)S(1)}, f32[5,32,768]{2,1,0:T(8,128)S(1)}, u32[]{:S(2)}, u32[]{:S(2)}) %collective-permute-start.30) | collective-permute-done | bytes 491552 | tf_op jit(solution)/shard_map/mixer_grads_last/ppermute | solution.py:696
  219.7 2.9 %collective-permute-start.35 = (f32[3,32,768]{2,1,0:T(8,128)S(1)}, f32[3,32,768]{2,1,0:T(8,128)S(1)}, u32[]{:S(2)}, u32[]{:S(2)}) collective-permute-start(f32[3,32,768]{2,1,0:T(8,128)S(1)} %get-tuple-element.347), channel_id=1, source_target_pairs={{0,8},{4,12},{8,0},{12,4},{16,24},{20,28},{24,16},{28,20},{32,40},... | collective-permute-start | bytes 884744 | tf_op jit(solution)/shard_map/mixer_grads_two/ppermute | solution.py:675
  225.8 5.6 %place_rows.2 = (bf16[1024,1024]{1,0:T(8,128)(2,1)}, f32[1024,1024]{1,0:T(8,128)}) custom-call(s32[4]{0:T(128)} %pad_add_fusion.at_ref, f32[256,1024]{1,0:T(8,128)} %copy-done.2, f32[256,1024]{1,0:T(8,128)} %first_norm_back.1.g0_ref, f32[256,1024]{1,0:T(8,128)} %collective-permute-done.24.r1_ref, f32[256,1024]{1,0:T(8,128)} %collective-permute-done.26.g1_ref), custom_call_target="tpu_custom_call" | custom-call | flops 3000000000 | bytes 1024 | tf_op jit(solution)/shard_map/place_rows/pallas_call | solution.py:525
  231.5 3.7 %collective-permute-done.33 = f32[3,32,768]{2,1,0:T(8,128)S(1)} collective-permute-done((f32[3,32,768]{2,1,0:T(8,128)S(1)}, f32[3,32,768]{2,1,0:T(8,128)S(1)}, u32[]{:S(2)}, u32[]{:S(2)}) %collective-permute-start.33) | collective-permute-done | bytes 294944 | tf_op jit(solution)/shard_map/mixer_grads_two/ppermute | solution.py:675
  235.8 6.5 %collective-permute-done.31.g0_ref = f32[256,1024]{1,0:T(8,128)S(1)} collective-permute-done((f32[256,1024]{1,0:T(8,128)}, f32[256,1024]{1,0:T(8,128)S(1)}, u32[]{:S(2)}, u32[]{:S(2)}) %collective-permute-start.31) | collective-permute-done | bytes 1048608 | tf_op jit(solution)/shard_map/grad_join/ppermute | solution.py:66
  243.1 3.5 %collective-permute-start.37 = (f32[32,1536]{1,0:T(8,128)S(1)}, f32[32,1536]{1,0:T(8,128)S(1)}, u32[]{:S(2)}, u32[]{:S(2)}) collective-permute-start(f32[32,1536]{1,0:T(8,128)S(1)} %get-tuple-element.345), channel_id=1, source_target_pairs={{0,16},{4,20},{8,24},{12,28},{16,0},{20,4},{24,8},{28,12},{32,48},... | collective-permute-start | bytes 589832 | tf_op jit(solution)/shard_map/rows/ppermute | solution.py:833
  247.5 5.6 %place_rows.3 = (bf16[1024,1024]{1,0:T(8,128)(2,1)}, f32[1024,1024]{1,0:T(8,128)}) custom-call(s32[4]{0:T(128)} %pad_add_fusion.at_ref, f32[256,1024]{1,0:T(8,128)} %collective-permute-done.23.r0_ref, f32[256,1024]{1,0:T(8,128)} %copy-done.14, f32[256,1024]{1,0:T(8,128)} %collective-permute-done.32.r1_ref, ...), custom_call_target="tpu_custom_call", output_to_operand_aliasing={{0}: (5, {}), {1}: (6, {})} | custom-call | flops 3000000000 | bytes 1024 | tf_op jit(solution)/shard_map/place_rows/pallas_call | solution.py:525
  259.5 7.0 %collective-permute-done.40.far_ref = f32[32,768]{1,0:T(8,128)S(1)} collective-permute-done((f32[32,768]{1,0:T(8,128)S(1)}, f32[32,768]{1,0:T(8,128)S(1)}, u32[]{:S(2)}, u32[]{:S(2)}) %collective-permute-start.40) | collective-permute-done | bytes 98336 | tf_op jit(solution)/shard_map/small_sums/ppermute | solution.py:66
  (148 shorter events, 65.1 us)
Async XLA Ops:
  7.2 210.7 %reduce-scatter.3.cloned.1.call-start = ((), (), s32[]{:S(2)}) async-start(), calls=%async_computation.2 | async-start | bytes 11141120 | tf_op jit(solution)/shard_map/feed_grads_x/reduce_scatter | solution.py:683
  8.4 13.5 %collective-permute-start.1 = (f32[256,1024]{1,0:T(8,128)S(1)}, f32[256,1024]{1,0:T(8,128)S(1)}, u32[]{:S(2)}, u32[]{:S(2)}) collective-permute-start(f32[256,1024]{1,0:T(8,128)S(1)} %convert_element_type.3), channel_id=1, source_target_pairs={{0,1},{1,0},{2,3},{3,2},{4,5},{5,4},{6,7},{7,6},{8,9},{9,8},{10,11... | collective-permute-start | bytes 3145736 | tf_op jit(solution)/shard_map/out_weights/ppermute | solution.py:62
  8.5 25.8 %collective-permute-start = (f32[256,1024]{1,0:T(8,128)S(1)}, f32[256,1024]{1,0:T(8,128)S(1)}, u32[]{:S(2)}, u32[]{:S(2)}) collective-permute-start(f32[256,1024]{1,0:T(8,128)S(1)} %convert_element_type.3), channel_id=1, source_target_pairs={{0,2},{2,0},{1,3},{3,1},{4,6},{6,4},{5,7},{7,5},{8,10},{10,8},{9,1... | collective-permute-start | bytes 3145736 | tf_op jit(solution)/shard_map/out_weights/ppermute | solution.py:66
  34.8 14.2 %collective-permute-start.2 = (f32[512,256]{1,0:T(8,128)}, f32[512,256]{1,0:T(8,128)}, u32[]{:S(2)}, u32[]{:S(2)}) collective-permute-start(f32[512,256]{1,0:T(8,128)} %get-tuple-element.176.m0_ref.m1_ref), channel_id=1, source_target_pairs={{0,2},{2,0},{1,3},{3,1},{4,6},{6,4},{5,7},{7,5},{8,10},{10,8},{9,1... | collective-permute-start | bytes 1572872 | tf_op jit(solution)/shard_map/heads_one/ppermute | solution.py:66
  49.6 16.7 %collective-permute-start.6 = (f32[512,256]{1,0:T(8,128)}, f32[512,256]{1,0:T(8,128)S(1)}, u32[]{:S(2)}, u32[]{:S(2)}) collective-permute-start(f32[512,256]{1,0:T(8,128)} %get-tuple-element.182.m0_ref), channel_id=1, source_target_pairs={{0,2},{2,0},{1,3},{3,1},{4,6},{6,4},{5,7},{7,5},{8,10},{10,8},{9,1... | collective-permute-start | bytes 1572872 | tf_op jit(solution)/shard_map/heads_two/ppermute | solution.py:66
  71.0 16.7 %collective-permute-start.9 = (f32[128,1024]{1,0:T(8,128)S(1)}, f32[128,1024]{1,0:T(8,128)S(1)}, u32[]{:S(2)}, u32[]{:S(2)}) collective-permute-start(f32[128,1024]{1,0:T(8,128)S(1)} %dynamic-slice_add_fusion.7), channel_id=1, source_target_pairs={{0,2},{2,0},{1,3},{3,1},{4,6},{6,4},{5,7},{7,5},{8,10},{10,8},{9,1... | collective-permute-start | bytes 1572872 | tf_op jit(solution)/shard_map/second_norm_z/ppermute | solution.py:66
  92.9 14.3 %collective-permute-start.12 = (f32[128,1024]{1,0:T(8,128)}, f32[128,1024]{1,0:T(8,128)}, u32[]{:S(2)}, u32[]{:S(2)}) collective-permute-start(f32[128,1024]{1,0:T(8,128)} %dynamic-slice_add_fusion.6), channel_id=1, source_target_pairs={{0,2},{2,0},{1,3},{3,1},{4,6},{6,4},{5,7},{7,5},{8,10},{10,8},{9,1... | collective-permute-start | bytes 1572872 | tf_op jit(solution)/shard_map/second_norm_z/ppermute | solution.py:66
  94.4 12.8 %collective-permute-start.13 = (f32[256,1024]{1,0:T(8,128)}, f32[256,1024]{1,0:T(8,128)S(1)}, u32[]{:S(2)}, u32[]{:S(2)}) collective-permute-start(f32[256,1024]{1,0:T(8,128)} %get-tuple-element.234), channel_id=1, source_target_pairs={{0,1},{1,0},{2,3},{3,2},{4,5},{5,4},{6,7},{7,6},{8,9},{9,8},{10,11... | collective-permute-start | bytes 3145736 | tf_op jit(solution)/shard_map/second_norm_z/ppermute | solution.py:62
  94.4 12.8 %collective-permute-start.14 = (f32[256,1024]{1,0:T(8,128)}, f32[256,1024]{1,0:T(8,128)S(1)}, u32[]{:S(2)}, u32[]{:S(2)}) collective-permute-start(f32[256,1024]{1,0:T(8,128)} %get-tuple-element.235), channel_id=1, source_target_pairs={{0,1},{1,0},{2,3},{3,2},{4,5},{5,4},{6,7},{7,6},{8,9},{9,8},{10,11... | collective-permute-start | bytes 3145736 | tf_op jit(solution)/shard_map/second_norm_z/ppermute | solution.py:62
  111.8 141.4 %reduce-scatter.5.cloned.1.call-start = ((), (), s32[]{:S(2)}) async-start(), calls=%async_computation.3 | async-start | bytes 2785280 | tf_op jit(solution)/shard_map/feed_grads_y/reduce_scatter | solution.py:683
  111.9 25.9 %collective-permute-start.15 = (f32[256,1024]{1,0:T(8,128)}, f32[256,1024]{1,0:T(8,128)}, u32[]{:S(2)}, u32[]{:S(2)}) collective-permute-start(f32[256,1024]{1,0:T(8,128)} %get-tuple-element.253.refs_0_.base_ref), channel_id=1, source_target_pairs={{0,2},{2,0},{1,3},{3,1},{4,6},{6,4},{5,7},{7,5},{8,10},{10,8},{9,1... | collective-permute-start | bytes 3145736 | tf_op jit(solution)/shard_map/second_norm_join/ppermute | solution.py:66
  137.8 28.9 %collective-permute-start.17 = (f32[256,1024]{1,0:T(8,128)S(1)}, f32[256,1024]{1,0:T(8,128)S(1)}, u32[]{:S(2)}, u32[]{:S(2)}) collective-permute-start(f32[256,1024]{1,0:T(8,128)S(1)} %pad_maximum_fusion), channel_id=1, source_target_pairs={{0,2},{2,0},{1,3},{3,1},{4,6},{6,4},{5,7},{7,5},{8,10},{10,8},{9,1... | collective-permute-start | bytes 3145736 | tf_op jit(solution)/shard_map/feed_sum/ppermute | solution.py:66
  168.9 23.2 %collective-permute-start.27 = (f32[9,32,768]{2,1,0:T(8,128)}, f32[9,32,768]{2,1,0:T(8,128)}, u32[]{:S(2)}, u32[]{:S(2)}) collective-permute-start(f32[9,32,768]{2,1,0:T(8,128)} %get-tuple-element.297), channel_id=1, source_target_pairs={{0,32},{4,36},{8,40},{12,44},{16,48},{20,52},{24,56},{28,60},{32,6... | collective-permute-start | bytes 2654216 | tf_op jit(solution)/shard_map/mixer_grads_first/ppermute | solution.py:687
  170.5 26.2 %collective-permute-start.25 = (f32[256,1024]{1,0:T(8,128)S(1)}, f32[256,1024]{1,0:T(8,128)}, u32[]{:S(2)}, u32[]{:S(2)}) collective-permute-start(f32[256,1024]{1,0:T(8,128)S(1)} %pad_maximum_fusion.2), channel_id=1, source_target_pairs={{0,2},{2,0},{1,3},{3,1},{4,6},{6,4},{5,7},{7,5},{8,10},{10,8},{9,1... | collective-permute-start | bytes 3145736 | tf_op jit(solution)/shard_map/first_norm_z/ppermute | solution.py:66
  172.0 28.9 %collective-permute-start.29 = (f32[9,32,768]{2,1,0:T(8,128)}, f32[9,32,768]{2,1,0:T(8,128)}, u32[]{:S(2)}, u32[]{:S(2)}) collective-permute-start(f32[9,32,768]{2,1,0:T(8,128)} %get-tuple-element.298), channel_id=1, source_target_pairs={{0,96},{4,100},{8,104},{12,108},{16,112},{20,116},{24,120},{28,124... | collective-permute-start | bytes 2654216 | tf_op jit(solution)/shard_map/mixer_grads_first/ppermute | solution.py:687
  175.9 41.1 %collective-permute-start.24 = (f32[256,1024]{1,0:T(8,128)S(1)}, f32[256,1024]{1,0:T(8,128)}, u32[]{:S(2)}, u32[]{:S(2)}) collective-permute-start(f32[256,1024]{1,0:T(8,128)S(1)} %pad_maximum_fusion.1.r0_ref), channel_id=1, source_target_pairs={{0,1},{1,0},{2,3},{3,2},{4,5},{5,4},{6,7},{7,6},{8,9},{9,8},{10,11... | collective-permute-start | bytes 3145736 | tf_op jit(solution)/shard_map/result_join/ppermute | solution.py:62
  176.0 41.8 %collective-permute-start.23 = (f32[256,1024]{1,0:T(8,128)S(1)}, f32[256,1024]{1,0:T(8,128)}, u32[]{:S(2)}, u32[]{:S(2)}) collective-permute-start(f32[256,1024]{1,0:T(8,128)S(1)} %pad_maximum_fusion.1.r0_ref), channel_id=1, source_target_pairs={{0,2},{2,0},{1,3},{3,1},{4,6},{6,4},{5,7},{7,5},{8,10},{10,8},{9,1... | collective-permute-start | bytes 3145736 | tf_op jit(solution)/shard_map/result_join/ppermute | solution.py:66
  200.8 17.0 %collective-permute-start.26 = (f32[256,1024]{1,0:T(8,128)}, f32[256,1024]{1,0:T(8,128)}, u32[]{:S(2)}, u32[]{:S(2)}) collective-permute-start(f32[256,1024]{1,0:T(8,128)} %first_norm_back.1.g0_ref), channel_id=1, source_target_pairs={{0,1},{1,0},{2,3},{3,2},{4,5},{5,4},{6,7},{7,6},{8,9},{9,8},{10,11... | collective-permute-start | bytes 3145736 | tf_op jit(solution)/shard_map/grad_join/ppermute | solution.py:62
  202.1 13.7 %collective-permute-start.30 = (f32[5,32,768]{2,1,0:T(8,128)S(1)}, f32[5,32,768]{2,1,0:T(8,128)S(1)}, u32[]{:S(2)}, u32[]{:S(2)}) collective-permute-start(f32[5,32,768]{2,1,0:T(8,128)S(1)} %slice_add_fusion), channel_id=1, source_target_pairs={{0,96},{4,100},{8,104},{12,108},{16,112},{20,116},{24,120},{28,124... | collective-permute-start | bytes 1474568 | tf_op jit(solution)/shard_map/mixer_grads_last/ppermute | solution.py:696
  217.9 24.4 %collective-permute-start.31 = (f32[256,1024]{1,0:T(8,128)}, f32[256,1024]{1,0:T(8,128)S(1)}, u32[]{:S(2)}, u32[]{:S(2)}) collective-permute-start(f32[256,1024]{1,0:T(8,128)} %first_norm_back.1.g0_ref), channel_id=1, source_target_pairs={{0,2},{2,0},{1,3},{3,1},{4,6},{6,4},{5,7},{7,5},{8,10},{10,8},{9,1... | collective-permute-start | bytes 3145736 | tf_op jit(solution)/shard_map/grad_join/ppermute | solution.py:66
  219.7 11.8 %collective-permute-start.35 = (f32[3,32,768]{2,1,0:T(8,128)S(1)}, f32[3,32,768]{2,1,0:T(8,128)S(1)}, u32[]{:S(2)}, u32[]{:S(2)}) collective-permute-start(f32[3,32,768]{2,1,0:T(8,128)S(1)} %get-tuple-element.347), channel_id=1, source_target_pairs={{0,8},{4,12},{8,0},{12,4},{16,24},{20,28},{24,16},{28,20},{32,40},... | collective-permute-start | bytes 884744 | tf_op jit(solution)/shard_map/mixer_grads_two/ppermute | solution.py:675
  222.6 12.6 %collective-permute-start.33 = (f32[3,32,768]{2,1,0:T(8,128)S(1)}, f32[3,32,768]{2,1,0:T(8,128)S(1)}, u32[]{:S(2)}, u32[]{:S(2)}) collective-permute-start(f32[3,32,768]{2,1,0:T(8,128)S(1)} %get-tuple-element.348), channel_id=1, source_target_pairs={{0,4},{4,8},{8,12},{12,0},{16,20},{20,24},{24,28},{28,16},{32,36},... | collective-permute-start | bytes 884744 | tf_op jit(solution)/shard_map/mixer_grads_two/ppermute | solution.py:675
  223.4 12.3 %collective-permute-start.34 = (f32[3,32,768]{2,1,0:T(8,128)S(1)}, f32[3,32,768]{2,1,0:T(8,128)S(1)}, u32[]{:S(2)}, u32[]{:S(2)}) collective-permute-start(f32[3,32,768]{2,1,0:T(8,128)S(1)} %get-tuple-element.349), channel_id=1, source_target_pairs={{0,12},{4,0},{8,4},{12,8},{16,28},{20,16},{24,20},{28,24},{32,44},... | collective-permute-start | bytes 884744 | tf_op jit(solution)/shard_map/mixer_grads_two/ppermute | solution.py:675
  225.8 20.7 %collective-permute-start.32 = (f32[256,1024]{1,0:T(8,128)}, f32[256,1024]{1,0:T(8,128)}, u32[]{:S(2)}, u32[]{:S(2)}) collective-permute-start(f32[256,1024]{1,0:T(8,128)} %collective-permute-done.23.r0_ref), channel_id=1, source_target_pairs={{0,1},{1,0},{2,3},{3,2},{4,5},{5,4},{6,7},{7,6},{8,9},{9,8},{10,11... | collective-permute-start | bytes 3145736 | tf_op jit(solution)/shard_map/result_join/ppermute | solution.py:62
  (43 other events, 291.3 us)
Sparse Core Ops, SparseCore 0:
  111.9 86.6 reduce-scatter.2
  218.0 32.6 reduce-scatter.4
